TPU v7x, 512 devices: a whole 4x4x16 slice. The times are simulated.
512 devices in a mesh: pool: 64 (over z, y), tp: 8 (over x, core).
Axes of the slice: x: 4, y: 4, z: 16, core: 2. Of those that a mesh axis runs over, the one named last changes fastest.
Arguments:
- query: bfloat16 [512, 2, 32, 128], P('pool', None, 'tp'), may hold values from -6 to 6
- new_kv: bfloat16 [512, 2, 2, 8, 128], P('pool', None, None, 'tp'), may hold values from -6 to 6
- kv_store: bfloat16 [16384, 2, 8, 16, 128], P('pool', None, 'tp'), may hold values from -6 to 6
- prefix_pages: int32 [256, 8], P('pool'), may hold values from 0 to 16383, as said below
- fork_of: int32 [512], P('pool'), may hold values from 0 to 3, as said below
- own_pages: int32 [512, 24], P('pool'), may hold values from 0 to 16383, as said below
- lengths: int32 [512], P('pool'), may hold values from 129 to 512
- o_weight: bfloat16 [4096, 2560], P('tp'), may hold values from -1.5 to 1.5
Outputs:
- projected: bfloat16 [512, 2, 2560], P('pool', None, 'tp')
Inputs may be any that keep to these rules, and one draw needn't show every extreme that they name: `prefix_pages`: page id g lies in the store of instance g // 256, at place g % 256; a page may be named more than once. `own_pages`: ids as for prefix_pages. The own pages of branches 4 to 7 of an instance lie in that instance's store, at distinct places. Of the 128 ids named by an instance's prefixes and by the own pages of its first 4 branches, at most 4 lie in any one store, and exactly 4 in one store, the same store for every instance. `fork_of`: each of an instance's 4 prefixes is named by at least one of its branches.
All inputs are finite; a program needn't handle non-finite values.
Results may differ from a plain program's by a relative error of at most 0.019.
Values may be sent and summed in bfloat16 or wider, within the bound.
No kernel may reach another device: no remote copies, remote signals or barrier semaphores. Data moves between devices by JAX's collectives and lax.ppermute only.
A program may use at most 64 MiB of HBM per device.

v0:
```python
import math

import jax
import jax.numpy as jnp
from jax import lax
from jax.sharding import PartitionSpec as P


def page_parts(queries, page_set, usable, score_scale):
    key_rows = page_set[:, :, 0]
    value_rows = page_set[:, :, 1]
    scores = (
        jnp.einsum("btkgd,bpkjd->btkgpj", queries, key_rows, preferred_element_type=jnp.float32)
        * score_scale
    )
    allowed = usable[:, None, None, None]
    scores = jnp.where(allowed, scores, -1e30)
    block_top = jnp.max(scores, -1)
    weights = jnp.where(allowed, jnp.exp(scores - block_top[..., None]), 0.0).astype(jnp.bfloat16)
    totals = jnp.sum(weights.astype(jnp.float32), -1)
    weighted = jnp.einsum(
        "btkgpj,bpkjd->btkgpd", weights, value_rows, preferred_element_type=jnp.float32
    )
    return (block_top, totals, weighted)


def fresh_parts(queries, fresh_kv, score_scale):
    step_count = queries.shape[1]
    key_rows = fresh_kv[:, :, 0]
    value_rows = fresh_kv[:, :, 1]
    scores = (
        jnp.einsum("btkgd,bnkd->btkgn", queries, key_rows, preferred_element_type=jnp.float32)
        * score_scale
    )
    steps_row = jnp.arange(step_count, dtype=jnp.int32)
    allowed = (steps_row[None, :] <= steps_row[:, None])[None, :, None, None, :]
    scores = jnp.where(allowed, scores, -1e30)
    block_top = jnp.max(scores, -1)
    weights = jnp.where(allowed, jnp.exp(scores - block_top[..., None]), 0.0).astype(jnp.bfloat16)
    totals = jnp.sum(weights.astype(jnp.float32), -1)
    weighted = jnp.einsum(
        "btkgn,bnkd->btkgd", weights, value_rows, preferred_element_type=jnp.float32
    )
    return (block_top, totals, weighted)


def finish(parts, fresh):
    block_top, totals, weighted = parts
    new_top, new_total, new_weighted = fresh
    row_top = jnp.maximum(jnp.max(block_top, -1), new_top)
    factor = jnp.exp(block_top - row_top[..., None])
    new_factor = jnp.exp(new_top - row_top)
    numerator = jnp.sum(factor[..., None] * weighted, -2) + new_factor[..., None] * new_weighted
    denominator = jnp.sum(factor * totals, -1) + new_factor * new_total
    attended = (numerator / denominator[..., None]).astype(jnp.bfloat16)
    return attended.reshape(attended.shape[0], attended.shape[1], -1)


def slot_of(wanted_ids, store_size, instances):
    holder = wanted_ids // store_size
    offset = wanted_ids % store_size
    member = (holder[:, None] == jnp.arange(instances, dtype=jnp.int32)[None, :]).astype(jnp.int32)
    in_slot = jnp.sum((jnp.cumsum(member, 0) - member) * member, 1)
    return (holder, offset, in_slot)


def pull_pages(wanted_ids, kv_store, instances, capacity):
    holder, offset, in_slot = slot_of(wanted_ids, kv_store.shape[0], instances)
    request = jnp.zeros((instances, capacity), jnp.int32).at[holder, in_slot].set(offset)
    arrived = lax.all_to_all(
        kv_store[lax.all_to_all(request, "pool", split_axis=0, concat_axis=0, tiled=True)],
        "pool",
        split_axis=0,
        concat_axis=0,
        tiled=True,
    )
    return arrived[holder, in_slot]


def shards(query, new_kv, kv_store, prefix_pages, fork_of, own_pages, lengths, o_weight):
    branches, step_count, q_heads, head_size = query.shape
    kv_heads = new_kv.shape[3]
    group_size = q_heads // kv_heads
    store_size = kv_store.shape[0]
    page_len = kv_store.shape[3]
    prefix_count, prefix_len = prefix_pages.shape
    own_len = own_pages.shape[1]
    arrived_count = branches // 2
    score_scale = 1.0 / math.sqrt(head_size)
    instances = lax.axis_size("pool")
    remote_count = prefix_count * prefix_len + arrived_count * own_len
    capacity = 2 * ((remote_count + instances - 1) // instances)
    page_tail = kv_store.shape[1:]
    queries = query.reshape(branches, step_count, kv_heads, group_size, head_size)
    position = jnp.arange((prefix_len + own_len) * page_len, dtype=jnp.int32).reshape(
        prefix_len + own_len, page_len
    )
    usable = position[None] < lengths[:, None, None]
    resident_kv = jnp.take(kv_store, own_pages[arrived_count:].reshape(-1) % store_size, axis=0)
    resident_kv = resident_kv.reshape((branches - arrived_count, own_len) + page_tail)
    fresh = fresh_parts(queries, new_kv, score_scale)
    wanted_ids = jnp.concatenate([prefix_pages.reshape(-1), own_pages[:arrived_count].reshape(-1)])
    split_at = prefix_count * prefix_len
    fetched = pull_pages(wanted_ids, kv_store, instances, capacity)
    prefix_kv = jnp.take(
        fetched[:split_at].reshape((prefix_count, prefix_len) + page_tail), fork_of, axis=0
    )
    moved_kv = fetched[split_at:].reshape((arrived_count, own_len) + page_tail)
    page_set = jnp.concatenate([prefix_kv, jnp.concatenate([moved_kv, resident_kv], 0)], 1)
    parts = page_parts(queries, page_set, usable, score_scale)
    attended = finish(parts, fresh)
    partial_value = jnp.dot(
        attended.reshape(branches * step_count, -1), o_weight, preferred_element_type=jnp.float32
    )
    partial_value = partial_value.reshape(branches, step_count, -1)
    return lax.psum_scatter(
        partial_value.astype(jnp.bfloat16), "tp", scatter_dimension=2, tiled=True
    )


def solution(mesh):
    return jax.shard_map(
        shards,
        mesh=mesh,
        in_specs=(
            P("pool", None, "tp", None),
            P("pool", None, None, "tp", None),
            P("pool", None, "tp", None, None),
            P("pool", None),
            P("pool"),
            P("pool", None),
            P("pool"),
            P("tp", None),
        ),
        out_specs=P("pool", None, "tp"),
        check_vma=False,
    )
```

profile of v0, /device:TPU:1, one launch (start us, length us, event | category | flops | bytes accessed | tf_op | source)
XLA Modules:
  0.0 225.4 jit_solution(6334338269179751578)
XLA Ops:
  6.5 0.9 fusion.22
  9.8 6.5 %scatter_fusion = s32[64,4]{0,1:T(4,128)S(1)} fusion(s32[64,4]{0,1:T(4,128)S(1)} %broadcast.314, s32[128]{0:T(128)S(1)} %fusion.18, s32[128]{0:T(128)S(1)} %get-tuple-element.17), kind=kCustom, calls=%fused_computation.4 | custom fusion | bytes 2560 | tf_op jit(solution)/shard_map/scatter | solution.py:69
  16.4 32.5 %all_to_all.17 = s32[64,1,4]{2,1,0:T(1,128)S(1)} all-to-all(s32[64,1,4]{2,1,0:T(1,128)S(1)} %copy.58), channel_id=1, replica_groups=mesh['pool'=64,'tp'=8] {'pool'}, dimensions={0} | all-to-all | bytes 2048 | tf_op jit(solution)/shard_map/all_to_all | solution.py:71
  49.0 3.7 %gather_fusion = bf16[256,2,16,128]{3,2,1,0:T(8,128)(2,1)} fusion(bf16[256,2,16,128]{3,2,1,0:T(8,128)(2,1)} %bitcast.134, s32[1024]{0:T(1024)S(1)} %pad_clamp_fusion.2), kind=kCustom, calls=%fused_computation | custom fusion | bytes 4195328 | tf_op jit(solution)/shard_map/gather | solution.py:71
  52.8 5.6 %all-to-all-start.1 = ((bf16[64,4,2,1,16,128]{5,4,2,1,3,0:T(8,128)(2,1)}), bf16[64,4,2,1,16,128]{5,4,2,1,3,0:T(8,128)(2,1)}, u32[]{:S(2)}, u32[]{:S(2)}) async-start(bf16[64,4,2,1,16,128]{5,4,2,1,3,0:T(8,128)(2,1)} %bitcast.131), calls=%async_computation.1 | async-start | bytes 4194304 | tf_op jit(solution)/shard_map/all_to_all | solution.py:70
  58.6 2.3 %gather_fusion.3 = bf16[96,2,16,128]{3,2,1,0:T(8,128)(2,1)S(1)} fusion(bf16[256,2,16,128]{3,2,1,0:T(8,128)(2,1)} %bitcast.135, s32[1024]{0:T(1024)S(1)} %pad_clamp_fusion), kind=kCustom, calls=%fused_computation.3 | custom fusion | bytes 1573248 | tf_op jit(solution)/shard_map/jit(_take)/gather | solution.py:99
  60.9 1.0 copy.61
  62.8 1.3 broadcast_select_fusion
  64.1 87.9 %all-to-all-done.1 = bf16[64,4,2,1,16,128]{5,4,2,1,3,0:T(8,128)(2,1)} async-done(((bf16[64,4,2,1,16,128]{5,4,2,1,3,0:T(8,128)(2,1)}), bf16[64,4,2,1,16,128]{5,4,2,1,3,0:T(8,128)(2,1)}, u32[]{:S(2)}, u32[]{:S(2)}) %all-to-all-start.1) | async-done | bytes 2097184 | tf_op jit(solution)/shard_map/all_to_all | solution.py:70
  152.0 3.5 %gather_fusion.1 = bf16[128,2,16,128]{3,2,1,0:T(8,128)(2,1)} fusion(bf16[64,4,2,16,128]{4,3,2,1,0:T(8,128)(2,1)} %bitcast.6, s32[128]{0:T(128)S(1)} %get-tuple-element.15), kind=kCustom, calls=%fused_computation.1 | custom fusion | bytes 2098176 | tf_op jit(solution)/shard_map/gather | solution.py:77
  155.4 1.8 slice.44
  157.2 1.0 copy.60
  158.2 2.4 %gather_fusion.2 = bf16[8,8,2,16,128]{4,3,2,1,0:T(8,128)(2,1)} fusion(bf16[4,8,2,16,128]{4,3,2,1,0:T(8,128)(2,1)} %bitcast.138, s32[1024]{0:T(1024)S(1)} %pad_clamp_fusion.1), kind=kCustom, calls=%fused_computation.2 | custom fusion | bytes 1048608 | tf_op jit(solution)/shard_map/jit(_take)/gather | solution.py:105
  160.6 1.2 bitcast_select_fusion
  161.7 1.4 maximum_maximum_fusion
  163.1 1.3 copy-done.1
  164.5 3.7 %fusion.20 = (f32[8,2,4]{2,1,0:T(2,128)S(1)}, f32[8,2,4,32]{2,1,3,0:T(2,128)S(1)}, f32[8,2,1,4,32,16]{5,3,1,4,0,2:T(4,128)}) fusion(bf16[8,2,4,128]{3,2,1,0:T(4,128)(2,1)S(1)} %copy-done.6, bf16[8,32,2,1,16,128]{5,4,1,0,3,2:T(8,128)(2,1)S(1)} %maximum_maximum_fusion, pred[8,32,16]{2,1,0:T(8,128)(4,1)S(1)} %broadcast_compare_fusion), kind=kOutput, calls=%fused_computation.82 | convolution fusion | flops 8517568 | bytes 1237248 | tf_op jit(solution)/shard_map/btkgd,bpkjd->btkgpj/dot_general | solution.py:13
  168.4 2.6 %convert_reduce_fusion = (f32[8,2,4,32]{2,1,3,0:T(2,128)S(1)}, bf16[8,2,1,4,32,16]{5,3,1,4,0,2:T(4,128)(2,1)S(1)}) fusion(f32[8,2,1,4,32,16]{5,3,1,4,0,2:T(4,128)} %get-tuple-element.23, f32[8,2,4,32]{2,1,3,0:T(2,128)S(1)} %get-tuple-element.6, pred[8,32,16]{2,1,0:T(8,128)(4,1)S(1)} %broadcast_compare_fusion), kind=kLoop, calls=%fused_computation.22 | loop fusion | flops 161792 | bytes 217088 | tf_op jit(solution)/shard_map/reduce_sum | solution.py:20
  171.0 1.2 multiply_reduce_fusion.1
  172.5 1.6 fusion.9
  175.5 2.2 copy.80
  177.7 3.4 %reshape.550 = bf16[2560,16]{1,0:T(8,128)(2,1)} reshape(bf16[2560,2,8]{2,1,0:T(2,128)(2,1)} %bitcast.132) | data formatting | bytes 163840
  181.1 35.7 %reduce-scatter.4.cloned.1.call-done = bf16[320,16]{1,0:T(8,128)(2,1)} async-done(((bf16[2560,16]{1,0:T(8,128)(2,1)}), bf16[320,16]{1,0:T(8,128)(2,1)}) %reduce-scatter.4.cloned.1.call-update) | async-done | bytes 10256
  216.8 1.0 reshape.551
  (63 shorter events, 6.2 us)
Async XLA Ops:
  6.5 168.5 %copy-start = (bf16[512,2560]{1,0:T(8,128)(2,1)S(1)}, bf16[512,2560]{1,0:T(8,128)(2,1)}, u32[]{:S(2)}) copy-start(bf16[512,2560]{1,0:T(8,128)(2,1)} %param.15) | copy-start | bytes 7864324
  52.8 99.2 %all-to-all-start.1 = ((bf16[64,4,2,1,16,128]{5,4,2,1,3,0:T(8,128)(2,1)}), bf16[64,4,2,1,16,128]{5,4,2,1,3,0:T(8,128)(2,1)}, u32[]{:S(2)}, u32[]{:S(2)}) async-start(bf16[64,4,2,1,16,128]{5,4,2,1,3,0:T(8,128)(2,1)} %bitcast.131), calls=%async_computation.1 | async-start | bytes 4194304 | tf_op jit(solution)/shard_map/all_to_all | solution.py:70
  58.3 3.5 %copy-start.3 = (bf16[8,2,2,1,128]{4,2,3,1,0:T(2,128)(2,1)S(1)}, bf16[8,2,2,1,128]{4,2,3,1,0:T(2,128)(2,1)}, u32[]{:S(2)}) copy-start(bf16[8,2,2,1,128]{4,2,3,1,0:T(2,128)(2,1)} %param.9) | copy-start | bytes 24580
  58.4 3.6 %copy-start.6 = (bf16[8,2,4,128]{3,2,1,0:T(4,128)(2,1)S(1)}, bf16[8,2,4,128]{3,2,1,0:T(4,128)(2,1)}, u32[]{:S(2)}) copy-start(bf16[8,2,4,128]{3,2,1,0:T(4,128)(2,1)} %param.8) | copy-start | bytes 49156
  58.4 4.2 %copy-start.7 = (s32[8]{0:T(128)S(1)}, s32[8]{0:T(128)}, u32[]{:S(2)}) copy-start(s32[8]{0:T(128)} %param.12) | copy-start | bytes 100
  58.4 4.3 %copy-start.4 = (s32[8,24]{1,0:T(8,128)S(1)}, s32[8,24]{1,0:T(8,128)}, u32[]{:S(2)}) copy-start(s32[8,24]{1,0:T(8,128)} %param.13) | copy-start | bytes 2308
  58.4 4.3 %copy-start.5 = (s32[8]{0:T(128)S(1)}, s32[8]{0:T(128)}, u32[]{:S(2)}) copy-start(s32[8]{0:T(128)} %param.14) | copy-start | bytes 100
  58.4 158.4 %reduce-scatter.4.cloned.1.call-start = ((), (), s32[]{:S(2)}) async-start(), calls=%async_computation.3 | async-start | bytes 737280
  155.4 1.8 slice-start
  163.1 1.4 copy-start.1
  168.2 2.8 %copy-start.2 = (f32[8,2,4,32]{2,1,3,0:T(2,128)}, f32[8,2,4,32]{2,1,3,0:T(2,128)S(1)}, u32[]{:S(2)}) copy-start(f32[8,2,4,32]{2,1,3,0:T(2,128)S(1)} %get-tuple-element.6) | copy-start | bytes 24580
Sparse Core Ops, SparseCore 0:
  181.2 35.5 reduce-scatter.3
where the time goes:
time: 227 us; the launch traced here: 225 us
  waiting for transfers between devices  124 us (55%)
  local copies, waits for them, and re-layouts  34.3 us (15%)
  blocking collectives  32.5 us (14%)
  between operations  13.7 us (6%)
  other arithmetic  9.41 us (4%)
  matrix products  6.23 us (3%)
  starting transfers between devices  5.6 us (2%)
    all_to_all x1, waiting for transfers between devices, pull_pages(): lax.all_to_all(kv_store[lax.all_to_all(request, 'pool', split_axis=0, con...  87.9 us
    unnamed x2, waiting for transfers between devices  35.7 us
    all_to_all x1, blocking collectives, pull_pages(): lax.all_to_all(request, 'pool', split_axis=0, concat_axis=0, tiled=True)  32.5 us
    unnamed x19, local copies, waits for them, and re-layouts  7.93 us
    scatter x1, local copies, waits for them, and re-layouts, pull_pages(): jnp.zeros((instances, capacity), jnp.int32).at[holder, in_slot].set(offset)  6.45 us
    all_to_all x1, starting transfers between devices, pull_pages(): lax.all_to_all(kv_store[lax.all_to_all(request, 'pool', split_axis=0, con...  5.56 us
  transfers between devices with their start and end apart: 2, of which 2 were waited for; matrix products, arithmetic and copies ran while one was open for 2% of the time, Pallas kernels for 0%

commit v1 on v0

v1 whole, which is shorter than its diff:
```python
import math

import jax
import jax.numpy as jnp
from jax import lax
from jax.experimental import pallas as pl
from jax.experimental.pallas import tpu as pltpu
from jax.sharding import Mesh
from jax.sharding import PartitionSpec as P

F32 = jnp.float32
BF16 = jnp.bfloat16
I32 = jnp.int32

HD = 128
PAGE = 16
NPRE = 8
NOWN = 24
ROOTS = 4
B = 8
MIG = 4
STEPS = 2
GROUP = 4
ROWS = B * STEPS * GROUP
SLOTS = 4
P_DEV = 256
NEG = -(2.0**100)
SCALE = 1.0 / math.sqrt(HD)
ZN, YN, XN, CN = 16, 4, 4, 2
POOL = ZN * YN
TPN = XN * CN
PREFIX_IDS = ROOTS * NPRE
KEYS = SLOTS * PAGE
PAGE_ROWS = ZN * KEYS
CHUNK = 2 * PAGE_ROWS + ZN
RES = ROWS + 16

VMEM = pl.BlockSpec(memory_space=pltpu.VMEM)
SMEM = pl.BlockSpec(memory_space=pltpu.SMEM)
NT = (((1,), (1,)), ((), ()))
NN = (((1,), (0,)), ((), ()))


def iota(shape, dim):
    return lax.broadcasted_iota(I32, shape, dim)


def dot(a, b, dims=NN):
    return lax.dot_general(a, b, dims, preferred_element_type=F32)


def request_kernel(prefix, own, fork, length, req):
    lane = iota((8, HD), 1)
    row = iota((8, HD), 0)
    ids = jnp.zeros((8, HD), I32)
    for r in range(ROOTS):
        for c in range(NPRE):
            ids = jnp.where(lane == r * NPRE + c, prefix[r, c], ids)
    for r in range(MIG):
        for c in range(NOWN):
            ids = jnp.where(lane == PREFIX_IDS + r * NOWN + c, own[r, c], ids)
    forks = jnp.zeros((8, HD), I32)
    lens = jnp.zeros((8, HD), I32)
    for b in range(B):
        forks = jnp.where(row == b, fork[b], forks)
        lens = jnp.where(row == b, length[b], lens)
    is_prefix = lane < PREFIX_IDS
    moved = jnp.maximum(lane - PREFIX_IDS, 0)
    chunk = jnp.where(is_prefix, lane % NPRE, NPRE + moved % NOWN)
    wanted = (is_prefix & (forks == lane // NPRE)) | (~is_prefix & (row == moved // NOWN))
    tokens = jnp.where(wanted, jnp.clip(lens - PAGE * chunk, 0, PAGE), 0)
    place = jnp.where(row == 0, ids % P_DEV, 0)
    table = jnp.concatenate([tokens, place], 0).astype(F32).astype(BF16)
    holder = jnp.broadcast_to((ids // P_DEV)[0:1], (POOL, HD))
    member = holder == iota((POOL, HD), 0)
    earlier = (iota((HD, HD), 0) < iota((HD, HD), 1)).astype(F32).astype(BF16)
    rank = dot(member.astype(F32).astype(BF16), earlier)
    out = jnp.zeros((POOL, HD), F32)
    for s in range(SLOTS):
        chosen = jnp.where(member & (rank == float(s)), 1.0, 0.0).astype(BF16)
        parts = [table if k == s else jnp.zeros((16, HD), BF16) for k in range(HD // 16)]
        out = out + dot(chosen, jnp.concatenate(parts, 0), NT)
    req[...] = out.astype(I32)


def spread_kernel(q, out):
    out[...] = jnp.broadcast_to(q[...][None], (ZN, ROWS, HD))


def gather_kernel(places, req, store, out):
    def instance(i, carry):
        y = i % YN
        z = i // YN
        for s in range(SLOTS):
            at = places[i, 16 * s + 8]
            start = pl.multiple_of(z * KEYS + s * PAGE, PAGE)
            out[y, pl.ds(start, PAGE), :] = store[at, 0]
            out[y, pl.ds(PAGE_ROWS + start, PAGE), :] = store[at, 1]
        return carry

    lax.fori_loop(0, POOL, instance, 0, unroll=8)
    rows = req[...].astype(F32)
    for y in range(YN):
        tile = jnp.zeros((ZN, HD), F32)
        for z in range(ZN):
            i = z * YN + y
            tile = jnp.where(iota((ZN, HD), 0) == z, rows[i : i + 1], tile)
        out[y, pl.ds(2 * PAGE_ROWS, ZN), :] = tile.astype(BF16)


def local_kernel(own, length, q, fresh_k, fresh_v, store, sums, top, total, keys, values):
    branches = B - MIG
    span = NOWN * PAGE
    for b in range(branches):
        for p in range(NOWN):
            at = own[MIG + b, p] % P_DEV
            start = b * span + p * PAGE
            keys[pl.ds(start, PAGE), :] = store[at, 0]
            values[pl.ds(start, PAGE), :] = store[at, 1]
    rows = q[...]
    branch_of = (iota((ROWS, 1), 0) % 16) // STEPS
    step_of = iota((ROWS, 1), 0) % STEPS
    lane16 = iota((ROWS, 16), 1)
    score = dot(rows, fresh_k[...], NT) * SCALE
    ok = (lane16 // STEPS == branch_of) & (lane16 % STEPS <= step_of)
    blocks = [(jnp.where(ok, score, NEG), ok, fresh_v[...])]
    position = iota((ROWS, span), 1) + NPRE * PAGE
    for b in range(branches):
        score = dot(rows, keys[pl.ds(b * span, span), :], NT) * SCALE
        ok = (branch_of == MIG + b) & (position < length[MIG + b])
        blocks.append((jnp.where(ok, score, NEG), ok, values[pl.ds(b * span, span), :]))
    best = jnp.max(blocks[0][0], 1, keepdims=True)
    for score, _, _ in blocks[1:]:
        best = jnp.maximum(best, jnp.max(score, 1, keepdims=True))
    acc = jnp.zeros((ROWS, HD), F32)
    count = jnp.zeros((ROWS, 1), F32)
    for score, ok, value in blocks:
        weight = jnp.where(ok, jnp.exp(score - best), 0.0).astype(BF16)
        count = count + jnp.sum(weight.astype(F32), 1, keepdims=True)
        acc = acc + dot(weight, value)
    sums[...] = acc
    top[...] = jnp.broadcast_to(best, (ROWS, HD))
    total[...] = jnp.broadcast_to(count, (ROWS, HD))


def partial_kernel(pages, queries, out):
    lane = iota((16, HD), 1)
    branch = iota((16, HD), 0) // STEPS
    pick = lane % 16 == branch
    blocks = []
    for y in range(YN):
        tile = pages[y, pl.ds(2 * PAGE_ROWS, ZN), :].astype(F32)
        blocks.append(
            jnp.concatenate(
                [jnp.where(pick, jnp.broadcast_to(tile[z : z + 1], (16, HD)), 0.0).astype(BF16) for z in range(ZN)], 0
            )
        )
    width = YN * KEYS
    shape = (YN * HD, width)
    source, key = iota(shape, 0), iota(shape, 1)
    expand = (source // HD == key // KEYS) & ((source % HD) // 16 == (key % KEYS) // PAGE)
    tokens = dot(jnp.concatenate(blocks, 1), expand.astype(F32).astype(BF16))
    slot_token = (iota((16, width), 1) % PAGE).astype(F32)
    column = iota((ROWS, HD), 1)
    stats = jnp.zeros((ROWS, HD), F32)
    for z in range(ZN):
        ok = slot_token < tokens[z * 16 : (z + 1) * 16]
        ok = jnp.concatenate([jnp.where(ok, 1.0, 0.0)] * GROUP, 0) > 0.5
        keys = jnp.concatenate([pages[y, pl.ds(z * KEYS, KEYS), :] for y in range(YN)], 0)
        values = jnp.concatenate([pages[y, pl.ds(PAGE_ROWS + z * KEYS, KEYS), :] for y in range(YN)], 0)
        score = jnp.where(ok, dot(queries[z], keys, NT) * SCALE, NEG)
        best = jnp.max(score, 1, keepdims=True).astype(BF16).astype(F32)
        weight = jnp.where(ok, jnp.exp(score - best), 0.0).astype(BF16)
        count = jnp.sum(weight.astype(F32), 1, keepdims=True)
        out[z, pl.ds(0, ROWS), :] = dot(weight, values).astype(BF16)
        stats = jnp.where(column == z, best, jnp.where(column == ZN + z, count, stats))
    turned = jnp.transpose(stats)
    tops = turned[0:ZN]
    counts = turned[ZN : 2 * ZN]
    high = counts.astype(BF16).astype(F32)
    low = counts - high
    row = iota((16, ROWS), 0)
    for z in range(ZN):
        tile = jnp.where(row == 1, high[z : z + 1], jnp.where(row == 2, low[z : z + 1], 0.0))
        tile = jnp.where(row == 0, tops[z : z + 1], tile).astype(BF16)
        out[z, pl.ds(ROWS, 16), :] = jnp.concatenate([tile, jnp.zeros((16, HD - ROWS), BF16)], 1)


def finish_kernel(parts, sums, top, total, weight, out):
    row = iota((ZN, HD), 0)
    tops = jnp.full((ZN, HD), NEG, F32)
    counts = jnp.zeros((ZN, HD), F32)
    for z in range(ZN):
        tile = parts[z, pl.ds(ROWS, 16), :].astype(F32)
        tops = jnp.where(row == z, tile[0:1], tops)
        counts = jnp.where(row == z, tile[1:2] + tile[2:3], counts)
    tops = jnp.concatenate([tops, jnp.full((HD - ZN, HD), NEG, F32)], 0)
    counts = jnp.concatenate([counts, jnp.zeros((HD - ZN, HD), F32)], 0)
    tops = jnp.transpose(tops)[0:ROWS]
    counts = jnp.transpose(counts)[0:ROWS]
    own_top = top[...]
    best = jnp.maximum(jnp.max(tops, 1, keepdims=True), own_top)
    factor = jnp.exp(tops - best)
    own_factor = jnp.exp(own_top - best)
    denominator = jnp.sum(factor * counts, 1, keepdims=True) + own_factor * total[...]
    numerator = own_factor * sums[...]
    for z in range(ZN):
        numerator = numerator + factor[:, z : z + 1] * parts[z, pl.ds(0, ROWS), :].astype(F32)
    attended = (numerator / denominator).astype(BF16)
    attended = jnp.concatenate([attended[16 * g : 16 * (g + 1)] for g in range(GROUP)], 1)
    result = dot(attended, weight[...]).astype(BF16).astype(F32)
    width = out.shape[2]
    for k in range(TPN):
        out[k] = result[:, k * width : (k + 1) * width].astype(BF16)


def call(kernel, out_shape, in_specs, name, scratch=(), cost=None):
    return pl.pallas_call(
        kernel,
        out_shape=out_shape,
        in_specs=in_specs,
        out_specs=jax.tree.map(lambda _: VMEM, out_shape),
        scratch_shapes=scratch,
        cost_estimate=cost,
        compiler_params=pltpu.CompilerParams(vmem_limit_bytes=40 * 2**20),
        name=name,
    )


def swap(x, axes):
    return lax.all_to_all(x, axes, split_axis=0, concat_axis=0, tiled=True)


def shards(query, new_kv, kv_store, prefix_pages, fork_of, own_pages, lengths, o_weight):
    shape = jax.ShapeDtypeStruct
    store = kv_store.reshape(P_DEV, 2, PAGE, HD)
    request = call(request_kernel, shape((POOL, HD), I32), [SMEM] * 4, "request")(
        prefix_pages, own_pages, fork_of, lengths
    )
    request = swap(request, ("z", "y"))
    q = query.transpose(2, 0, 1, 3).reshape(ROWS, HD)
    queries = call(spread_kernel, shape((ZN, ROWS, HD), BF16), [VMEM], "spread")(q)
    queries = swap(queries, "z")
    fresh_k = new_kv[:, :, 0, 0].reshape(B * STEPS, HD)
    fresh_v = new_kv[:, :, 1, 0].reshape(B * STEPS, HD)
    local = call(
        local_kernel,
        [shape((ROWS, HD), F32)] * 3,
        [SMEM, SMEM, VMEM, VMEM, VMEM, VMEM],
        "resident",
        [pltpu.VMEM(((B - MIG) * NOWN * PAGE, HD), BF16)] * 2,
        pl.CostEstimate(flops=10**8, bytes_accessed=3 * 2**20, transcendentals=10**5),
    )(own_pages, lengths, q, fresh_k, fresh_v, store)
    pages = call(gather_kernel, shape((YN, CHUNK, HD), BF16), [SMEM, VMEM, VMEM], "gather_pages")(
        request, request, store
    )
    pages = swap(pages, "y")
    parts = call(partial_kernel, shape((ZN, RES, HD), BF16), [VMEM, VMEM], "partials")(pages, queries)
    parts = swap(parts, "z")
    width = o_weight.shape[1] // TPN
    shares = call(finish_kernel, shape((TPN, 16, width), BF16), [VMEM] * 5, "finish")(parts, *local, o_weight)
    shares = swap(shares, ("x", "c"))
    return jnp.sum(shares.astype(F32), 0).astype(BF16).reshape(B, STEPS, width)


def solution(mesh):
    fine = Mesh(mesh.devices.reshape(ZN, YN, XN, CN), ("z", "y", "x", "c"))
    pool, tp = ("z", "y"), ("x", "c")
    return jax.shard_map(
        shards,
        mesh=fine,
        in_specs=(
            P(pool, None, tp, None),
            P(pool, None, None, tp, None),
            P(pool, None, tp, None, None),
            P(pool, None),
            P(pool),
            P(pool, None),
            P(pool),
            P(tp, None),
        ),
        out_specs=P(pool, None, tp),
        check_vma=False,
    )
```

time: 227 us -> 128 us (0.56)
  waiting for transfers between devices: 124 us -> 32.4 us
  starting transfers between devices: 5.6 us -> 36.3 us
  local copies, waits for them, and re-layouts: 34.3 us -> 7.39 us
  between operations: 13.7 us -> 0.12 us
  Pallas kernels: 0 us -> 12.1 us
  other arithmetic: 9.41 us -> 0.02 us
  blocking collectives: 32.5 us -> 39.6 us
  matrix products: 6.23 us -> 0 us
    all_to_all x1 -> x3, waiting for transfers between devices: 87.9 us -> 32.4 us  [swap(): return lax.all_to_all(x, axes, split_axis=0, concat_axis=0, tiled=True)]
    unnamed x2 -> x0, waiting for transfers between devices: 35.7 us -> none
    all_to_all x1 -> x3, starting transfers between devices: 5.56 us -> 36.3 us  [swap(): return lax.all_to_all(x, axes, split_axis=0, concat_axis=0, tiled=True)]
    gather x5 -> x0, local copies, waits for them, and re-layouts: 12.9 us -> none  [the longest x1 3.74 us: pull_pages(): kv_store[lax.all_to_all(request, 'pool', split_axis=0, concat_axis=0, til...]
    pallas_call x0 -> x6, Pallas kernels: none -> 12.1 us  [the longest x1 4.41 us: shards(): call(partial_kernel, shape((ZN, RES, HD), BF16), [VMEM, VMEM], 'partials')]
    all_to_all x1 -> x2, blocking collectives: 32.5 us -> 39.6 us  [swap(): return lax.all_to_all(x, axes, split_axis=0, concat_axis=0, tiled=True)]
    scatter x1 -> x0, local copies, waits for them, and re-layouts: 6.45 us -> none  [pull_pages(): jnp.zeros((instances, capacity), jnp.int32).at[holder, in_slot].set(offset)]
    reduce_sum x5 -> x1, other arithmetic: 4.77 us -> 0.02 us  [shards(): return jnp.sum(shares.astype(F32), 0).astype(BF16).reshape(B, STEPS, width)]
  transfers between devices with their start and end apart: 2 -> 3, of which waited for: 2 -> 3; matrix products, arithmetic and copies ran while one was open for 2% -> 1% of each run, Pallas kernels for 0% -> 4%
where the time goes in v1:
time: 128 us
  blocking collectives  39.6 us (31%)
  starting transfers between devices  36.3 us (28%)
  waiting for transfers between devices  32.4 us (25%)
  Pallas kernels  12.1 us (9%)
  local copies, waits for them, and re-layouts  7.39 us (6%)
    all_to_all x2, blocking collectives, swap(): return lax.all_to_all(x, axes, split_axis=0, concat_axis=0, tiled=True)  39.6 us
    all_to_all x3, starting transfers between devices, swap(): return lax.all_to_all(x, axes, split_axis=0, concat_axis=0, tiled=True)  36.3 us
    all_to_all x3, waiting for transfers between devices, swap(): return lax.all_to_all(x, axes, split_axis=0, concat_axis=0, tiled=True)  32.4 us
    unnamed x22, local copies, waits for them, and re-layouts  6.03 us
    pallas_call x1, Pallas kernels, shards(): call(partial_kernel, shape((ZN, RES, HD), BF16), [VMEM, VMEM], 'partials')  4.41 us
    pallas_call x1, Pallas kernels, shards(): call(gather_kernel, shape((YN, CHUNK, HD), BF16), [SMEM, VMEM, VMEM], 'ga...  2.79 us
  transfers between devices with their start and end apart: 3, of which 3 were waited for; matrix products, arithmetic and copies ran while one was open for 1% of the time, Pallas kernels for 4%

profile of v1, /device:TPU:1, one launch (start us, length us, event | category | flops | bytes accessed | tf_op | source)
XLA Modules:
  0.0 127.9 jit_solution(17144989291751664691)
XLA Ops:
  0.0 0.7 copy-done.3
  0.7 0.7 copy-done.5
  1.3 0.7 copy-done.7
  2.0 0.7 copy-done.8
  2.7 1.6 %request.1 = s32[64,128]{1,0:T(8,128)} custom-call(s32[4,8]{1,0:T(4,128)S(1)} %copy-done.7, s32[8,24]{1,0:T(8,128)S(1)} %copy-done.3, s32[8]{0:T(128)S(1)} %copy-done.8, s32[8]{0:T(128)S(1)} %copy-done.5), custom_call_target="tpu_custom_call" | custom-call | tf_op jit(solution)/shard_map/request/pallas_call | solution.py:237
  4.3 19.3 %all-to-all-start = ((s32[64,1,128]{2,1,0:T(1,128)}), s32[64,1,128]{2,1,0:T(1,128)S(1)}, u32[]{:S(2)}, u32[]{:S(2)}) async-start(s32[64,1,128]{2,1,0:T(1,128)} %bitcast.1), calls=%async_computation | async-start | bytes 65536 | tf_op jit(solution)/shard_map/all_to_all | solution.py:231
  23.6 0.7 copy.12
  24.3 0.8 spread.1
  25.1 12.1 %all-to-all-done = s32[64,1,128]{2,1,0:T(1,128)S(1)} async-done(((s32[64,1,128]{2,1,0:T(1,128)}), s32[64,1,128]{2,1,0:T(1,128)S(1)}, u32[]{:S(2)}, u32[]{:S(2)}) %all-to-all-start) | async-done | bytes 32800 | tf_op jit(solution)/shard_map/all_to_all | solution.py:231
  37.2 3.5 %all-to-all-start.2 = ((bf16[16,64,128]{2,1,0:T(8,128)(2,1)}), bf16[16,64,128]{2,1,0:T(8,128)(2,1)S(1)}, u32[]{:S(2)}, u32[]{:S(2)}) async-start(bf16[16,64,128]{2,1,0:T(8,128)(2,1)} %spread.1), calls=%async_computation.2 | async-start | bytes 524288 | tf_op jit(solution)/shard_map/all_to_all | solution.py:231
  40.7 0.0 copy-start
  40.7 1.6 %copy-done = bf16[256,2,1,16,128]{4,3,2,1,0:T(8,128)(2,1)S(1)} copy-done((bf16[256,2,1,16,128]{4,3,2,1,0:T(8,128)(2,1)S(1)}, bf16[256,2,1,16,128]{4,3,2,1,0:T(8,128)(2,1)}, u32[]{:S(2)}) %copy-start) | copy-done | bytes 2097176
  42.3 2.8 %gather_pages.1 = bf16[4,2064,128]{2,1,0:T(8,128)(2,1)S(1)} custom-call(s32[64,128]{1,0:T(8,128)S(1)} %bitcast.11, s32[64,128]{1,0:T(8,128)S(1)} %bitcast.12, bf16[256,2,16,128]{3,2,1,0:T(8,128)(2,1)S(1)} %bitcast.9), custom_call_target="tpu_custom_call" | custom-call | tf_op jit(solution)/shard_map/gather_pages/pallas_call | solution.py:254
  45.1 8.4 %all-to-all-done.2.queries = bf16[16,64,128]{2,1,0:T(8,128)(2,1)S(1)} async-done(((bf16[16,64,128]{2,1,0:T(8,128)(2,1)}), bf16[16,64,128]{2,1,0:T(8,128)(2,1)S(1)}, u32[]{:S(2)}, u32[]{:S(2)}) %all-to-all-start.2) | async-done | bytes 262176 | tf_op jit(solution)/shard_map/all_to_all | solution.py:231
  53.5 22.2 %all_to_all.31.pages = bf16[4,2064,128]{2,1,0:T(8,128)(2,1)S(1)} all-to-all(bf16[4,2064,128]{2,1,0:T(8,128)(2,1)S(1)} %gather_pages.1), channel_id=1, replica_groups=mesh['z'=16,'y'=4,'x'=4,'c'=2] {'y'}, dimensions={0} | all-to-all | bytes 4227072 | tf_op jit(solution)/shard_map/all_to_all | solution.py:231
  75.8 4.4 %partials.1 = bf16[16,80,128]{2,1,0:T(8,128)(2,1)} custom-call(bf16[4,2064,128]{2,1,0:T(8,128)(2,1)S(1)} %all_to_all.31.pages, bf16[16,64,128]{2,1,0:T(8,128)(2,1)S(1)} %all-to-all-done.2.queries), custom_call_target="tpu_custom_call" | custom-call | tf_op jit(solution)/shard_map/partials/pallas_call | solution.py:258
  80.2 13.5 %all-to-all-start.3 = ((bf16[16,80,128]{2,1,0:T(8,128)(2,1)}), bf16[16,80,128]{2,1,0:T(8,128)(2,1)S(1)}, u32[]{:S(2)}, u32[]{:S(2)}) async-start(bf16[16,80,128]{2,1,0:T(8,128)(2,1)} %partials.1), calls=%async_computation.3 | async-start | bytes 655360 | tf_op jit(solution)/shard_map/all_to_all | solution.py:231
  93.7 0.0 copy-done.9
  93.8 1.5 %resident.1 = (f32[64,128]{1,0:T(8,128)S(1)}, f32[64,128]{1,0:T(8,128)S(1)}, f32[64,128]{1,0:T(8,128)S(1)}) custom-call(s32[8,24]{1,0:T(8,128)S(1)} %copy-done.4, s32[8]{0:T(128)S(1)} %copy-done.6, bf16[64,128]{1,0:T(8,128)(2,1)S(1)} %bitcast.14, bf16[16,128]{1,0:T(8,128)(2,1)S(1)} %bitcast.15, bf16[16,128]{1,0:T(8,128)(2,1)S(1)} %bitcast.16, ...), custom_call_target="tpu_custom_call" | custom-call | flops 100000000 | bytes 3145728 | tf_op jit(solution)/shard_map/resident/pallas_call | solution.py:246
  95.3 11.9 %all-to-all-done.3.parts = bf16[16,80,128]{2,1,0:T(8,128)(2,1)S(1)} async-done(((bf16[16,80,128]{2,1,0:T(8,128)(2,1)}), bf16[16,80,128]{2,1,0:T(8,128)(2,1)S(1)}, u32[]{:S(2)}, u32[]{:S(2)}) %all-to-all-start.3) | async-done | bytes 327712 | tf_op jit(solution)/shard_map/all_to_all | solution.py:231
  107.2 1.7 %copy-done.2 = bf16[512,2560]{1,0:T(8,128)(2,1)S(1)} copy-done((bf16[512,2560]{1,0:T(8,128)(2,1)S(1)}, bf16[512,2560]{1,0:T(8,128)(2,1)}, u32[]{:S(2)}) %copy-start.2) | copy-done | bytes 2621464
  109.0 1.0 finish.1
  109.9 17.3 %all_to_all.32 = bf16[8,16,320]{2,1,0:T(8,128)(2,1)S(1)} all-to-all(bf16[8,16,320]{2,1,0:T(8,128)(2,1)S(1)} %finish.1), channel_id=1, replica_groups=mesh['z'=16,'y'=4,'x'=4,'c'=2] {'x','c'}, dimensions={0} | all-to-all | bytes 163840 | tf_op jit(solution)/shard_map/all_to_all | solution.py:231
  127.3 0.6 reshape.13
  (16 shorter events, 0.1 us)
Async XLA Ops:
  0.0 0.7 copy-start.3
  0.7 0.7 copy-start.5
  1.3 0.7 copy-start.7
  2.0 0.7 copy-start.8
  4.3 32.9 %all-to-all-start = ((s32[64,1,128]{2,1,0:T(1,128)}), s32[64,1,128]{2,1,0:T(1,128)S(1)}, u32[]{:S(2)}, u32[]{:S(2)}) async-start(s32[64,1,128]{2,1,0:T(1,128)} %bitcast.1), calls=%async_computation | async-start | bytes 65536 | tf_op jit(solution)/shard_map/all_to_all | solution.py:231
  37.2 16.3 %all-to-all-start.2 = ((bf16[16,64,128]{2,1,0:T(8,128)(2,1)}), bf16[16,64,128]{2,1,0:T(8,128)(2,1)S(1)}, u32[]{:S(2)}, u32[]{:S(2)}) async-start(bf16[16,64,128]{2,1,0:T(8,128)(2,1)} %spread.1), calls=%async_computation.2 | async-start | bytes 524288 | tf_op jit(solution)/shard_map/all_to_all | solution.py:231
  40.7 1.6 %copy-start = (bf16[256,2,1,16,128]{4,3,2,1,0:T(8,128)(2,1)S(1)}, bf16[256,2,1,16,128]{4,3,2,1,0:T(8,128)(2,1)}, u32[]{:S(2)}) copy-start(bf16[256,2,1,16,128]{4,3,2,1,0:T(8,128)(2,1)} %param.10) | copy-start | bytes 6291460
  75.8 18.0 %copy-start.9 = (bf16[8,2,2,1,128]{4,2,3,1,0:T(2,128)(2,1)S(1)}, bf16[8,2,2,1,128]{4,2,3,1,0:T(2,128)(2,1)}, u32[]{:S(2)}) copy-start(bf16[8,2,2,1,128]{4,2,3,1,0:T(2,128)(2,1)} %param.9) | copy-start | bytes 24580
  75.8 18.0 %copy-start.1 = (bf16[256,2,1,16,128]{4,3,2,1,0:T(8,128)(2,1)S(1)}, bf16[256,2,1,16,128]{4,3,2,1,0:T(8,128)(2,1)}, u32[]{:S(2)}) copy-start(bf16[256,2,1,16,128]{4,3,2,1,0:T(8,128)(2,1)} %param.10) | copy-start | bytes 6291460
  75.8 18.0 %copy-start.4 = (s32[8,24]{1,0:T(8,128)S(1)}, s32[8,24]{1,0:T(8,128)}, u32[]{:S(2)}) copy-start(s32[8,24]{1,0:T(8,128)} %own.3) | copy-start | bytes 2308
  75.8 18.0 %copy-start.6 = (s32[8]{0:T(128)S(1)}, s32[8]{0:T(128)}, u32[]{:S(2)}) copy-start(s32[8]{0:T(128)} %length.3) | copy-start | bytes 100
  80.2 27.0 %all-to-all-start.3 = ((bf16[16,80,128]{2,1,0:T(8,128)(2,1)}), bf16[16,80,128]{2,1,0:T(8,128)(2,1)S(1)}, u32[]{:S(2)}, u32[]{:S(2)}) async-start(bf16[16,80,128]{2,1,0:T(8,128)(2,1)} %partials.1), calls=%async_computation.3 | async-start | bytes 655360 | tf_op jit(solution)/shard_map/all_to_all | solution.py:231
  107.2 1.7 %copy-start.2 = (bf16[512,2560]{1,0:T(8,128)(2,1)S(1)}, bf16[512,2560]{1,0:T(8,128)(2,1)}, u32[]{:S(2)}) copy-start(bf16[512,2560]{1,0:T(8,128)(2,1)} %weight.1) | copy-start | bytes 7864324

commit v2 on v1

--- a/solution.py
+++ b/solution.py
@@ -37,6 +37,7 @@
 
 VMEM = pl.BlockSpec(memory_space=pltpu.VMEM)
 SMEM = pl.BlockSpec(memory_space=pltpu.SMEM)
+HBM = pl.BlockSpec(memory_space=pltpu.HBM)
 NT = (((1,), (1,)), ((), ()))
 NN = (((1,), (0,)), ((), ()))
 
@@ -49,7 +50,13 @@
     return lax.dot_general(a, b, dims, preferred_element_type=F32)
 
 
-def request_kernel(prefix, own, fork, length, req):
+def request_kernel(prefix_hbm, own_hbm, fork_hbm, length_hbm, req, prefix, own, fork, length, sems):
+    pairs = ((prefix_hbm, prefix), (own_hbm, own), (fork_hbm, fork), (length_hbm, length))
+    copies = [pltpu.make_async_copy(a, b, sems.at[n]) for n, (a, b) in enumerate(pairs)]
+    for copy in copies:
+        copy.start()
+    for copy in copies:
+        copy.wait()
     lane = iota((8, HD), 1)
     row = iota((8, HD), 0)
     ids = jnp.zeros((8, HD), I32)
@@ -71,8 +78,9 @@
     tokens = jnp.where(wanted, jnp.clip(lens - PAGE * chunk, 0, PAGE), 0)
     place = jnp.where(row == 0, ids % P_DEV, 0)
     table = jnp.concatenate([tokens, place], 0).astype(F32).astype(BF16)
-    holder = jnp.broadcast_to((ids // P_DEV)[0:1], (POOL, HD))
-    member = holder == iota((POOL, HD), 0)
+    holder = ids // P_DEV
+    holder = (holder % YN) * ZN + holder // YN
+    member = jnp.broadcast_to(holder[0:1], (POOL, HD)) == iota((POOL, HD), 0)
     earlier = (iota((HD, HD), 0) < iota((HD, HD), 1)).astype(F32).astype(BF16)
     rank = dot(member.astype(F32).astype(BF16), earlier)
     out = jnp.zeros((POOL, HD), F32)
@@ -87,25 +95,30 @@
     out[...] = jnp.broadcast_to(q[...][None], (ZN, ROWS, HD))
 
 
-def gather_kernel(places, req, store, out):
-    def instance(i, carry):
-        y = i % YN
-        z = i // YN
-        for s in range(SLOTS):
-            at = places[i, 16 * s + 8]
-            start = pl.multiple_of(z * KEYS + s * PAGE, PAGE)
-            out[y, pl.ds(start, PAGE), :] = store[at, 0]
-            out[y, pl.ds(PAGE_ROWS + start, PAGE), :] = store[at, 1]
-        return carry
-
-    lax.fori_loop(0, POOL, instance, 0, unroll=8)
-    rows = req[...].astype(F32)
-    for y in range(YN):
-        tile = jnp.zeros((ZN, HD), F32)
+def prefetch_kernel(source, out, sem):
+    copy = pltpu.make_async_copy(source, out, sem)
+    copy.start()
+    copy.wait()
+
+
+def gather_kernel(column, places, req, store, *refs):
+    outs, stages, sems = refs[:YN], refs[YN : 2 * YN], refs[2 * YN]
+    copies = []
+    for k, stage in enumerate(stages):
+        base = ((column[0] + k) % YN) * ZN
         for z in range(ZN):
-            i = z * YN + y
-            tile = jnp.where(iota((ZN, HD), 0) == z, rows[i : i + 1], tile)
-        out[y, pl.ds(2 * PAGE_ROWS, ZN), :] = tile.astype(BF16)
+            for s in range(SLOTS):
+                at = places[base + z, 16 * s + 8]
+                start = z * KEYS + s * PAGE
+                stage[pl.ds(start, PAGE), :] = store[at, 0]
+                stage[pl.ds(PAGE_ROWS + start, PAGE), :] = store[at, 1]
+        rows = req[pl.ds(pl.multiple_of(base, ZN), ZN), :]
+        stage[pl.ds(2 * PAGE_ROWS, ZN), :] = rows.astype(F32).astype(BF16)
+        copy = pltpu.make_async_copy(stage, outs[k], sems.at[k])
+        copy.start()
+        copies.append(copy)
+    for copy in copies:
+        copy.wait()
 
 
 def local_kernel(own, length, q, fresh_k, fresh_v, store, sums, top, total, keys, values):
@@ -143,13 +156,17 @@
     total[...] = jnp.broadcast_to(count, (ROWS, HD))
 
 
-def partial_kernel(pages, queries, out):
+def partial_kernel(own, p1, p2, p3, queries, out, p0, sem):
+    copy = pltpu.make_async_copy(own, p0, sem)
+    copy.start()
+    pages = (p0, p1, p2, p3)
+    copy.wait()
     lane = iota((16, HD), 1)
     branch = iota((16, HD), 0) // STEPS
     pick = lane % 16 == branch
     blocks = []
     for y in range(YN):
-        tile = pages[y, pl.ds(2 * PAGE_ROWS, ZN), :].astype(F32)
+        tile = pages[y][pl.ds(2 * PAGE_ROWS, ZN), :].astype(F32)
         blocks.append(
             jnp.concatenate(
                 [jnp.where(pick, jnp.broadcast_to(tile[z : z + 1], (16, HD)), 0.0).astype(BF16) for z in range(ZN)], 0
@@ -166,8 +183,8 @@
     for z in range(ZN):
         ok = slot_token < tokens[z * 16 : (z + 1) * 16]
         ok = jnp.concatenate([jnp.where(ok, 1.0, 0.0)] * GROUP, 0) > 0.5
-        keys = jnp.concatenate([pages[y, pl.ds(z * KEYS, KEYS), :] for y in range(YN)], 0)
-        values = jnp.concatenate([pages[y, pl.ds(PAGE_ROWS + z * KEYS, KEYS), :] for y in range(YN)], 0)
+        keys = jnp.concatenate([pages[y][pl.ds(z * KEYS, KEYS), :] for y in range(YN)], 0)
+        values = jnp.concatenate([pages[y][pl.ds(PAGE_ROWS + z * KEYS, KEYS), :] for y in range(YN)], 0)
         score = jnp.where(ok, dot(queries[z], keys, NT) * SCALE, NEG)
         best = jnp.max(score, 1, keepdims=True).astype(BF16).astype(F32)
         weight = jnp.where(ok, jnp.exp(score - best), 0.0).astype(BF16)
@@ -186,7 +203,9 @@
         out[z, pl.ds(ROWS, 16), :] = jnp.concatenate([tile, jnp.zeros((16, HD - ROWS), BF16)], 1)
 
 
-def finish_kernel(parts, sums, top, total, weight, out):
+def finish_kernel(parts, sums, top, total, weight_hbm, out, weight, sem):
+    copy = pltpu.make_async_copy(weight_hbm, weight, sem)
+    copy.start()
     row = iota((ZN, HD), 0)
     tops = jnp.full((ZN, HD), NEG, F32)
     counts = jnp.zeros((ZN, HD), F32)
@@ -208,23 +227,47 @@
         numerator = numerator + factor[:, z : z + 1] * parts[z, pl.ds(0, ROWS), :].astype(F32)
     attended = (numerator / denominator).astype(BF16)
     attended = jnp.concatenate([attended[16 * g : 16 * (g + 1)] for g in range(GROUP)], 1)
+    copy.wait()
     result = dot(attended, weight[...]).astype(BF16).astype(F32)
     width = out.shape[2]
     for k in range(TPN):
         out[k] = result[:, k * width : (k + 1) * width].astype(BF16)
 
 
-def call(kernel, out_shape, in_specs, name, scratch=(), cost=None):
+def total_kernel(shares, out):
+    total = shares[0].astype(F32)
+    for k in range(1, TPN):
+        total = total + shares[k].astype(F32)
+    total = total.astype(BF16).astype(F32)
+    for b in range(B):
+        out[b] = total[STEPS * b : STEPS * (b + 1)].astype(BF16)
+
+
+def call(kernel, out_shape, in_specs, name, scratch=(), cost=None, mib=12, out_specs=None):
     return pl.pallas_call(
         kernel,
         out_shape=out_shape,
         in_specs=in_specs,
-        out_specs=jax.tree.map(lambda _: VMEM, out_shape),
+        out_specs=jax.tree.map(lambda _: VMEM, out_shape) if out_specs is None else out_specs,
         scratch_shapes=scratch,
         cost_estimate=cost,
-        compiler_params=pltpu.CompilerParams(vmem_limit_bytes=40 * 2**20),
+        compiler_params=pltpu.CompilerParams(vmem_limit_bytes=mib * 2**20),
         name=name,
     )
+
+
+def hbm(x):
+    return pltpu.with_memory_space_constraint(x, pltpu.HBM)
+
+
+def vmem(x):
+    return pltpu.with_memory_space_constraint(x, pltpu.VMEM)
+
+
+def prefetch(x, name):
+    return call(
+        prefetch_kernel, pltpu.VMEM(x.shape, x.dtype), [HBM], name, [pltpu.SemaphoreType.DMA(())], out_specs=VMEM
+    )(hbm(x))
 
 
 def swap(x, axes):
@@ -234,12 +277,36 @@
 def shards(query, new_kv, kv_store, prefix_pages, fork_of, own_pages, lengths, o_weight):
     shape = jax.ShapeDtypeStruct
     store = kv_store.reshape(P_DEV, 2, PAGE, HD)
-    request = call(request_kernel, shape((POOL, HD), I32), [SMEM] * 4, "request")(
-        prefix_pages, own_pages, fork_of, lengths
-    )
-    request = swap(request, ("z", "y"))
+    request = call(
+        request_kernel,
+        shape((POOL, HD), I32),
+        [HBM] * 4,
+        "request",
+        [
+            pltpu.SMEM(prefix_pages.shape, I32),
+            pltpu.SMEM(own_pages.shape, I32),
+            pltpu.SMEM(fork_of.shape, I32),
+            pltpu.SMEM(lengths.shape, I32),
+            pltpu.SemaphoreType.DMA((4,)),
+        ],
+    )(hbm(prefix_pages), hbm(own_pages), hbm(fork_of), hbm(lengths))
+    request = swap(request, ("y", "z"))
+    column = lax.axis_index("y").astype(I32).reshape(1)
+    store = prefetch(store, "store_ahead")
+    pages = call(
+        gather_kernel,
+        [pltpu.HBM((CHUNK, HD), BF16)] * YN,
+        [SMEM, SMEM, VMEM, VMEM],
+        "gather_pages",
+        [pltpu.VMEM((CHUNK, HD), BF16)] * YN + [pltpu.SemaphoreType.DMA((YN,))],
+        out_specs=[HBM] * YN,
+    )(column, request, request, vmem(store))
+    arrived = [pages[0]]
+    for k in (2, 1, 3):
+        arrived.append(lax.ppermute(pages[k], "y", [(y, (y + k) % YN) for y in range(YN)]))
     q = query.transpose(2, 0, 1, 3).reshape(ROWS, HD)
     queries = call(spread_kernel, shape((ZN, ROWS, HD), BF16), [VMEM], "spread")(q)
+    queries, _ = lax.optimization_barrier((queries, pages[0]))
     queries = swap(queries, "z")
     fresh_k = new_kv[:, :, 0, 0].reshape(B * STEPS, HD)
     fresh_v = new_kv[:, :, 1, 0].reshape(B * STEPS, HD)
@@ -251,16 +318,18 @@
         [pltpu.VMEM(((B - MIG) * NOWN * PAGE, HD), BF16)] * 2,
         pl.CostEstimate(flops=10**8, bytes_accessed=3 * 2**20, transcendentals=10**5),
     )(own_pages, lengths, q, fresh_k, fresh_v, store)
-    pages = call(gather_kernel, shape((YN, CHUNK, HD), BF16), [SMEM, VMEM, VMEM], "gather_pages")(
-        request, request, store
-    )
-    pages = swap(pages, "y")
-    parts = call(partial_kernel, shape((ZN, RES, HD), BF16), [VMEM, VMEM], "partials")(pages, queries)
+    parts = call(partial_kernel, shape((ZN, RES, HD), BF16), [HBM] + [VMEM] * 4, "partials", [
+        pltpu.VMEM((CHUNK, HD), BF16), pltpu.SemaphoreType.DMA(())
+    ])(hbm(arrived[0]), *[vmem(x) for x in arrived[1:]], queries)
     parts = swap(parts, "z")
     width = o_weight.shape[1] // TPN
-    shares = call(finish_kernel, shape((TPN, 16, width), BF16), [VMEM] * 5, "finish")(parts, *local, o_weight)
+    shares = call(finish_kernel, shape((TPN, 16, width), BF16), [VMEM] * 4 + [HBM], "finish", [
+        pltpu.VMEM(o_weight.shape, BF16), pltpu.SemaphoreType.DMA(())
+    ])(
+        parts, *local, hbm(o_weight)
+    )
     shares = swap(shares, ("x", "c"))
-    return jnp.sum(shares.astype(F32), 0).astype(BF16).reshape(B, STEPS, width)
+    return call(total_kernel, shape((B, STEPS, width), BF16), [VMEM], "total")(shares)
 
 
 def solution(mesh):

time: 128 us -> 123 us (0.961)
  blocking collectives: 39.6 us -> 15.9 us
  waiting for transfers between devices: 32.4 us -> 42.9 us
  starting transfers between devices: 36.3 us -> 43.9 us
  local copies, waits for them, and re-layouts: 7.39 us -> 2.63 us
  Pallas kernels: 12.1 us -> 16.6 us
    all_to_all x2 -> x1, blocking collectives: 39.6 us -> 15.9 us  [swap(): return lax.all_to_all(x, axes, split_axis=0, concat_axis=0, tiled=True)]
    ppermute x0 -> x3, waiting for transfers between devices: none -> 19.3 us  [shards(): lax.ppermute(pages[k], 'y', [(y, (y + k) % YN) for y in range(YN)])]
    ppermute x0 -> x3, starting transfers between devices: none -> 9.59 us  [shards(): lax.ppermute(pages[k], 'y', [(y, (y + k) % YN) for y in range(YN)])]
    all_to_all x3, waiting for transfers between devices: 32.4 us -> 23.7 us  [swap(): return lax.all_to_all(x, axes, split_axis=0, concat_axis=0, tiled=True)]
    pallas_call x4 -> x6, Pallas kernels: 9.79 us -> 14.3 us  [the longest x1 5.47 us: shards(): call(partial_kernel, shape((ZN, RES, HD), BF16), [HBM] + [VMEM] * 4, 'par...]
    unnamed x22 -> x12, local copies, waits for them, and re-layouts: 6.03 us -> 1.88 us
    all_to_all x3, starting transfers between devices: 36.3 us -> 34.4 us  [swap(): return lax.all_to_all(x, axes, split_axis=0, concat_axis=0, tiled=True)]
  transfers between devices with their start and end apart: 3 -> 6, of which waited for: 3 -> 4; matrix products, arithmetic and copies ran while one was open for 1% -> 1% of each run, Pallas kernels for 4% -> 3%
where the time goes in v2:
time: 123 us; the launch traced here: 122 us
  starting transfers between devices  43.9 us (36%)
  waiting for transfers between devices  42.9 us (35%)
  Pallas kernels  16.6 us (13%)
  blocking collectives  15.9 us (13%)
  local copies, waits for them, and re-layouts  2.63 us (2%)
    all_to_all x3, starting transfers between devices, swap(): return lax.all_to_all(x, axes, split_axis=0, concat_axis=0, tiled=True)  34.4 us
    all_to_all x3, waiting for transfers between devices, swap(): return lax.all_to_all(x, axes, split_axis=0, concat_axis=0, tiled=True)  23.7 us
    ppermute x3, waiting for transfers between devices, shards(): lax.ppermute(pages[k], 'y', [(y, (y + k) % YN) for y in range(YN)])  19.3 us
    all_to_all x1, blocking collectives, swap(): return lax.all_to_all(x, axes, split_axis=0, concat_axis=0, tiled=True)  15.9 us
    ppermute x3, starting transfers between devices, shards(): lax.ppermute(pages[k], 'y', [(y, (y + k) % YN) for y in range(YN)])  9.59 us
    pallas_call x1, Pallas kernels, shards(): call(partial_kernel, shape((ZN, RES, HD), BF16), [HBM] + [VMEM] * 4, 'par...  5.47 us
    pallas_call x1, Pallas kernels, shards(): call(gather_kernel, [pltpu.HBM((CHUNK, HD), BF16)] * YN, [SMEM, SMEM, VME...  2.54 us
  transfers between devices with their start and end apart: 6, of which 4 were waited for; matrix products, arithmetic and copies ran while one was open for 1% of the time, Pallas kernels for 3%

profile of v2, /device:TPU:1, one launch (start us, length us, event | category | flops | bytes accessed | tf_op | source)
XLA Modules:
  0.0 122.1 jit_solution(10828699393962966427)
XLA Ops:
  0.0 1.8 %request.1 = s32[64,128]{1,0:T(8,128)} custom-call(s32[4,8]{1,0:T(4,128)} %prefix_hbm.1, s32[8,24]{1,0:T(8,128)} %own.1, s32[8]{0:T(128)} %fork_hbm.1, s32[8]{0:T(128)} %length.1), custom_call_target="tpu_custom_call" | custom-call | tf_op jit(solution)/shard_map/request/pallas_call | solution.py:280
  1.8 19.3 %all-to-all-start = ((s32[64,1,128]{2,1,0:T(1,128)}), s32[64,1,128]{2,1,0:T(1,128)S(1)}, u32[]{:S(2)}, u32[]{:S(2)}) async-start(s32[64,1,128]{2,1,0:T(1,128)} %bitcast.2), calls=%async_computation | async-start | bytes 65536 | tf_op jit(solution)/shard_map/all_to_all | solution.py:274
  21.1 0.7 copy.12
  21.8 0.7 spread.1
  22.6 1.6 %store_ahead.1.store = bf16[256,2,16,128]{3,2,1,0:T(8,128)(2,1)S(1)} custom-call(bf16[256,2,16,128]{3,2,1,0:T(8,128)(2,1)} %bitcast.16), custom_call_target="tpu_custom_call" | custom-call | tf_op jit(solution)/shard_map/store_ahead/pallas_call | solution.py:268
  24.2 10.2 %all-to-all-done = s32[64,1,128]{2,1,0:T(1,128)S(1)} async-done(((s32[64,1,128]{2,1,0:T(1,128)}), s32[64,1,128]{2,1,0:T(1,128)S(1)}, u32[]{:S(2)}, u32[]{:S(2)}) %all-to-all-start) | async-done | bytes 32800 | tf_op jit(solution)/shard_map/all_to_all | solution.py:274
  34.4 2.5 %gather_pages.1 = (bf16[2064,128]{1,0:T(8,128)(2,1)}, bf16[2064,128]{1,0:T(8,128)(2,1)}, bf16[2064,128]{1,0:T(8,128)(2,1)}, bf16[2064,128]{1,0:T(8,128)(2,1)}) custom-call(s32[1]{0:T(128)} %bitcast.column, s32[64,128]{1,0:T(8,128)S(1)} %bitcast.10, s32[64,128]{1,0:T(8,128)S(1)} %bitcast.11, bf16[256,2,16,128]{3,2,1,0:T(8,128)(2,1)S(1)} %store_ahead.1.store), custom_call_target="tpu_custom_call" | custom-call | tf_op jit(solution)/shard_map/gather_pages/pallas_call | solution.py:296
  36.9 0.0 copy-start.4
  36.9 0.0 copy-start.2
  36.9 3.7 %all-to-all-start.1 = ((bf16[16,64,128]{2,1,0:T(8,128)(2,1)}), bf16[16,64,128]{2,1,0:T(8,128)(2,1)S(1)}, u32[]{:S(2)}, u32[]{:S(2)}) async-start(bf16[16,64,128]{2,1,0:T(8,128)(2,1)} %spread.1), calls=%async_computation.1 | async-start | bytes 524288 | tf_op jit(solution)/shard_map/all_to_all | solution.py:274
  40.6 3.1 %collective-permute-start = (bf16[2064,128]{1,0:T(8,128)(2,1)}, bf16[2064,128]{1,0:T(8,128)(2,1)S(1)}, u32[]{:S(2)}, u32[]{:S(2)}) collective-permute-start(bf16[2064,128]{1,0:T(8,128)(2,1)} %get-tuple-element.14), channel_id=1, source_target_pairs={{0,16},{8,24},{16,0},{24,8},{1,17},{9,25},{17,1},{25,9},{2,18},{10... | collective-permute-start | bytes 1585160 | tf_op jit(solution)/shard_map/ppermute | solution.py:306
  43.7 1.9 %collective-permute-start.1 = (bf16[2064,128]{1,0:T(8,128)(2,1)}, bf16[2064,128]{1,0:T(8,128)(2,1)S(1)}, u32[]{:S(2)}, u32[]{:S(2)}) collective-permute-start(bf16[2064,128]{1,0:T(8,128)(2,1)} %get-tuple-element.15), channel_id=1, source_target_pairs={{0,8},{8,16},{16,24},{24,0},{1,9},{9,17},{17,25},{25,1},{2,10},{10... | collective-permute-start | bytes 1585160 | tf_op jit(solution)/shard_map/ppermute | solution.py:306
  45.7 4.5 %collective-permute-start.2 = (bf16[2064,128]{1,0:T(8,128)(2,1)}, bf16[2064,128]{1,0:T(8,128)(2,1)S(1)}, u32[]{:S(2)}, u32[]{:S(2)}) collective-permute-start(bf16[2064,128]{1,0:T(8,128)(2,1)} %get-tuple-element.16), channel_id=1, source_target_pairs={{0,24},{8,0},{16,8},{24,16},{1,25},{9,1},{17,9},{25,17},{2,26},{10... | collective-permute-start | bytes 1585160 | tf_op jit(solution)/shard_map/ppermute | solution.py:306
  50.2 5.4 %collective-permute-done.p1 = bf16[2064,128]{1,0:T(8,128)(2,1)S(1)} collective-permute-done((bf16[2064,128]{1,0:T(8,128)(2,1)}, bf16[2064,128]{1,0:T(8,128)(2,1)S(1)}, u32[]{:S(2)}, u32[]{:S(2)}) %collective-permute-start) | collective-permute-done | bytes 528416 | tf_op jit(solution)/shard_map/ppermute | solution.py:306
  55.6 13.9 %collective-permute-done.1.p2 = bf16[2064,128]{1,0:T(8,128)(2,1)S(1)} collective-permute-done((bf16[2064,128]{1,0:T(8,128)(2,1)}, bf16[2064,128]{1,0:T(8,128)(2,1)S(1)}, u32[]{:S(2)}, u32[]{:S(2)}) %collective-permute-start.1) | collective-permute-done | bytes 528416 | tf_op jit(solution)/shard_map/ppermute | solution.py:306
  69.5 0.8 copy-done
  70.3 1.0 copy-done.1
  71.3 5.5 %partials.1 = bf16[16,80,128]{2,1,0:T(8,128)(2,1)} custom-call(bf16[2064,128]{1,0:T(8,128)(2,1)} %get-tuple-element.13.own, bf16[2064,128]{1,0:T(8,128)(2,1)S(1)} %collective-permute-done.p1, bf16[2064,128]{1,0:T(8,128)(2,1)S(1)} %collective-permute-done.1.p2, bf16[2064,128]{1,0:T(8,128)(2,1)S(1)} %copy-done.1, bf16[16,64,128]{2,1,0:T(8,128)(2,1)S(1)} %all-to-all-done.1.queries), custom_call_target="tpu_custom_call" | custom-call | tf_op jit(solution)/shard_map/partials/pallas_call | solution.py:321
  76.8 11.4 %all-to-all-start.2 = ((bf16[16,80,128]{2,1,0:T(8,128)(2,1)}), bf16[16,80,128]{2,1,0:T(8,128)(2,1)S(1)}, u32[]{:S(2)}, u32[]{:S(2)}) async-start(bf16[16,80,128]{2,1,0:T(8,128)(2,1)} %partials.1), calls=%async_computation.2 | async-start | bytes 655360 | tf_op jit(solution)/shard_map/all_to_all | solution.py:274
  88.3 1.5 %resident.1 = (f32[64,128]{1,0:T(8,128)S(1)}, f32[64,128]{1,0:T(8,128)S(1)}, f32[64,128]{1,0:T(8,128)S(1)}) custom-call(s32[8,24]{1,0:T(8,128)S(1)} %copy-done.2, s32[8]{0:T(128)S(1)} %copy-done.3, bf16[64,128]{1,0:T(8,128)(2,1)S(1)} %bitcast.13, bf16[16,128]{1,0:T(8,128)(2,1)S(1)} %bitcast.15, bf16[16,128]{1,0:T(8,128)(2,1)S(1)} %bitcast.14, ...), custom_call_target="tpu_custom_call" | custom-call | flops 100000000 | bytes 3145728 | tf_op jit(solution)/shard_map/resident/pallas_call | solution.py:313
  89.8 13.5 %all-to-all-done.2.parts = bf16[16,80,128]{2,1,0:T(8,128)(2,1)S(1)} async-done(((bf16[16,80,128]{2,1,0:T(8,128)(2,1)}), bf16[16,80,128]{2,1,0:T(8,128)(2,1)S(1)}, u32[]{:S(2)}, u32[]{:S(2)}) %all-to-all-start.2) | async-done | bytes 327712 | tf_op jit(solution)/shard_map/all_to_all | solution.py:274
  103.3 2.3 %finish.1 = bf16[8,16,320]{2,1,0:T(8,128)(2,1)S(1)} custom-call(bf16[16,80,128]{2,1,0:T(8,128)(2,1)S(1)} %all-to-all-done.2.parts, f32[64,128]{1,0:T(8,128)S(1)} %get-tuple-element.18.sums, f32[64,128]{1,0:T(8,128)S(1)} %get-tuple-element.19.top, f32[64,128]{1,0:T(8,128)S(1)} %get-tuple-element.20.total, bf16[512,2560]{1,0:T(8,128)(2,1)} %weight_hbm.1), custom_call_target="tpu_custom_call" | custom-call | tf_op jit(solution)/shard_map/finish/pallas_call | solution.py:326
  105.6 15.9 %all_to_all.26.shares = bf16[8,16,320]{2,1,0:T(8,128)(2,1)S(1)} all-to-all(bf16[8,16,320]{2,1,0:T(8,128)(2,1)S(1)} %finish.1), channel_id=1, replica_groups=mesh['z'=16,'y'=4,'x'=4,'c'=2] {'x','c'}, dimensions={0} | all-to-all | bytes 163840 | tf_op jit(solution)/shard_map/all_to_all | solution.py:274
  121.5 0.6 total.1
  (11 shorter events, 0.0 us)
Async XLA Ops:
  1.8 32.6 %all-to-all-start = ((s32[64,1,128]{2,1,0:T(1,128)}), s32[64,1,128]{2,1,0:T(1,128)S(1)}, u32[]{:S(2)}, u32[]{:S(2)}) async-start(s32[64,1,128]{2,1,0:T(1,128)} %bitcast.2), calls=%async_computation | async-start | bytes 65536 | tf_op jit(solution)/shard_map/all_to_all | solution.py:274
  36.9 51.3 %copy-start.4 = (bf16[8,2,2,1,128]{4,2,3,1,0:T(2,128)(2,1)S(1)}, bf16[8,2,2,1,128]{4,2,3,1,0:T(2,128)(2,1)}, u32[]{:S(2)}) copy-start(bf16[8,2,2,1,128]{4,2,3,1,0:T(2,128)(2,1)} %param.9) | copy-start | bytes 24580
  36.9 51.4 %copy-start.2 = (s32[8,24]{1,0:T(8,128)S(1)}, s32[8,24]{1,0:T(8,128)}, u32[]{:S(2)}) copy-start(s32[8,24]{1,0:T(8,128)} %own.1) | copy-start | bytes 2308
  36.9 51.4 %copy-start.3 = (s32[8]{0:T(128)S(1)}, s32[8]{0:T(128)}, u32[]{:S(2)}) copy-start(s32[8]{0:T(128)} %length.1) | copy-start | bytes 100
  36.9 33.4 %all-to-all-start.1 = ((bf16[16,64,128]{2,1,0:T(8,128)(2,1)}), bf16[16,64,128]{2,1,0:T(8,128)(2,1)S(1)}, u32[]{:S(2)}, u32[]{:S(2)}) async-start(bf16[16,64,128]{2,1,0:T(8,128)(2,1)} %spread.1), calls=%async_computation.1 | async-start | bytes 524288 | tf_op jit(solution)/shard_map/all_to_all | solution.py:274
  40.6 15.0 %collective-permute-start = (bf16[2064,128]{1,0:T(8,128)(2,1)}, bf16[2064,128]{1,0:T(8,128)(2,1)S(1)}, u32[]{:S(2)}, u32[]{:S(2)}) collective-permute-start(bf16[2064,128]{1,0:T(8,128)(2,1)} %get-tuple-element.14), channel_id=1, source_target_pairs={{0,16},{8,24},{16,0},{24,8},{1,17},{9,25},{17,1},{25,9},{2,18},{10... | collective-permute-start | bytes 1585160 | tf_op jit(solution)/shard_map/ppermute | solution.py:306
  43.7 25.8 %collective-permute-start.1 = (bf16[2064,128]{1,0:T(8,128)(2,1)}, bf16[2064,128]{1,0:T(8,128)(2,1)S(1)}, u32[]{:S(2)}, u32[]{:S(2)}) collective-permute-start(bf16[2064,128]{1,0:T(8,128)(2,1)} %get-tuple-element.15), channel_id=1, source_target_pairs={{0,8},{8,16},{16,24},{24,0},{1,9},{9,17},{17,25},{25,1},{2,10},{10... | collective-permute-start | bytes 1585160 | tf_op jit(solution)/shard_map/ppermute | solution.py:306
  45.7 23.8 %collective-permute-start.2 = (bf16[2064,128]{1,0:T(8,128)(2,1)}, bf16[2064,128]{1,0:T(8,128)(2,1)S(1)}, u32[]{:S(2)}, u32[]{:S(2)}) collective-permute-start(bf16[2064,128]{1,0:T(8,128)(2,1)} %get-tuple-element.16), channel_id=1, source_target_pairs={{0,24},{8,0},{16,8},{24,16},{1,25},{9,1},{17,9},{25,17},{2,26},{10... | collective-permute-start | bytes 1585160 | tf_op jit(solution)/shard_map/ppermute | solution.py:306
  69.5 0.8 copy-start
  70.3 1.0 copy-start.1
  76.8 26.5 %all-to-all-start.2 = ((bf16[16,80,128]{2,1,0:T(8,128)(2,1)}), bf16[16,80,128]{2,1,0:T(8,128)(2,1)S(1)}, u32[]{:S(2)}, u32[]{:S(2)}) async-start(bf16[16,80,128]{2,1,0:T(8,128)(2,1)} %partials.1), calls=%async_computation.2 | async-start | bytes 655360 | tf_op jit(solution)/shard_map/all_to_all | solution.py:274

commit v3 on v2

--- a/solution.py
+++ b/solution.py
@@ -33,11 +33,12 @@
 KEYS = SLOTS * PAGE
 PAGE_ROWS = ZN * KEYS
 CHUNK = 2 * PAGE_ROWS + ZN
-RES = ROWS + 16
+RES = ROWS + 8
 
 VMEM = pl.BlockSpec(memory_space=pltpu.VMEM)
 SMEM = pl.BlockSpec(memory_space=pltpu.SMEM)
 HBM = pl.BlockSpec(memory_space=pltpu.HBM)
+ANY = pl.BlockSpec(memory_space=pl.ANY)
 NT = (((1,), (1,)), ((), ()))
 NN = (((1,), (0,)), ((), ()))
 
@@ -91,10 +92,6 @@
     req[...] = out.astype(I32)
 
 
-def spread_kernel(q, out):
-    out[...] = jnp.broadcast_to(q[...][None], (ZN, ROWS, HD))
-
-
 def prefetch_kernel(source, out, sem):
     copy = pltpu.make_async_copy(source, out, sem)
     copy.start()
@@ -156,51 +153,71 @@
     total[...] = jnp.broadcast_to(count, (ROWS, HD))
 
 
-def partial_kernel(own, p1, p2, p3, queries, out, p0, sem):
-    copy = pltpu.make_async_copy(own, p0, sem)
-    copy.start()
-    pages = (p0, p1, p2, p3)
-    copy.wait()
-    lane = iota((16, HD), 1)
-    branch = iota((16, HD), 0) // STEPS
-    pick = lane % 16 == branch
+def mask_kernel(c0, c1, c2, c3, out, tiles, sems):
+    chunks = (c0, c1, c2, c3)
+    copies = [
+        pltpu.make_async_copy(c.at[pl.ds(2 * PAGE_ROWS, ZN), :], tiles.at[k], sems.at[k]) for k, c in enumerate(chunks)
+    ]
+    for copy in copies:
+        copy.start()
+    for copy in copies:
+        copy.wait()
+    pick = iota((16, HD), 1) % 16 == iota((16, HD), 0) // STEPS
     blocks = []
-    for y in range(YN):
-        tile = pages[y][pl.ds(2 * PAGE_ROWS, ZN), :].astype(F32)
-        blocks.append(
-            jnp.concatenate(
-                [jnp.where(pick, jnp.broadcast_to(tile[z : z + 1], (16, HD)), 0.0).astype(BF16) for z in range(ZN)], 0
-            )
-        )
+    for k in range(YN):
+        tile = tiles[k].astype(F32)
+        rows = [jnp.where(pick, jnp.broadcast_to(tile[z : z + 1], (16, HD)), 0.0).astype(BF16) for z in range(ZN)]
+        blocks.append(jnp.concatenate(rows, 0))
     width = YN * KEYS
     shape = (YN * HD, width)
     source, key = iota(shape, 0), iota(shape, 1)
     expand = (source // HD == key // KEYS) & ((source % HD) // 16 == (key % KEYS) // PAGE)
     tokens = dot(jnp.concatenate(blocks, 1), expand.astype(F32).astype(BF16))
-    slot_token = (iota((16, width), 1) % PAGE).astype(F32)
+    number = (iota((ZN * 16, width), 1) % PAGE).astype(F32)
+    out[...] = jnp.where(number < tokens, 0.0, NEG)
+
+
+def partial_kernel(mask, c0, c1, c2, c3, queries, out, pages, sems):
+    half = PAGE_ROWS // 2
+    copies = []
+    for part in range(2):
+        for k, chunk in enumerate((c0, c1, c2, c3)):
+            for kv in range(2):
+                rows = pl.ds(kv * PAGE_ROWS + part * half, half)
+                copy = pltpu.make_async_copy(chunk.at[rows, :], pages.at[k, rows, :], sems.at[part, k, kv])
+                copy.start()
+                copies.append(copy)
     column = iota((ROWS, HD), 1)
     stats = jnp.zeros((ROWS, HD), F32)
+    sums = []
     for z in range(ZN):
-        ok = slot_token < tokens[z * 16 : (z + 1) * 16]
-        ok = jnp.concatenate([jnp.where(ok, 1.0, 0.0)] * GROUP, 0) > 0.5
-        keys = jnp.concatenate([pages[y][pl.ds(z * KEYS, KEYS), :] for y in range(YN)], 0)
-        values = jnp.concatenate([pages[y][pl.ds(PAGE_ROWS + z * KEYS, KEYS), :] for y in range(YN)], 0)
-        score = jnp.where(ok, dot(queries[z], keys, NT) * SCALE, NEG)
+        if z % (ZN // 2) == 0:
+            first = (z // (ZN // 2)) * 2 * YN
+            for copy in copies[first : first + 2 * YN]:
+                copy.wait()
+        bias = jnp.concatenate([mask[pl.ds(z * 16, 16), :]] * GROUP, 0)
+        keys = jnp.concatenate([pages[k, pl.ds(z * KEYS, KEYS), :] for k in range(YN)], 0)
+        values = jnp.concatenate([pages[k, pl.ds(PAGE_ROWS + z * KEYS, KEYS), :] for k in range(YN)], 0)
+        score = jnp.where(bias < 0.0, NEG, dot(queries[z], keys, NT) * SCALE)
         best = jnp.max(score, 1, keepdims=True).astype(BF16).astype(F32)
-        weight = jnp.where(ok, jnp.exp(score - best), 0.0).astype(BF16)
+        weight = jnp.where(bias < 0.0, 0.0, jnp.exp(score - best)).astype(BF16)
         count = jnp.sum(weight.astype(F32), 1, keepdims=True)
-        out[z, pl.ds(0, ROWS), :] = dot(weight, values).astype(BF16)
+        sums.append(dot(weight, values))
         stats = jnp.where(column == z, best, jnp.where(column == ZN + z, count, stats))
     turned = jnp.transpose(stats)
+    turned = jnp.concatenate([turned, jnp.zeros((HD, HD - ROWS), F32)], 1)
     tops = turned[0:ZN]
     counts = turned[ZN : 2 * ZN]
     high = counts.astype(BF16).astype(F32)
     low = counts - high
-    row = iota((16, ROWS), 0)
+    row = iota((8, HD), 0)
+    tiles = []
     for z in range(ZN):
         tile = jnp.where(row == 1, high[z : z + 1], jnp.where(row == 2, low[z : z + 1], 0.0))
-        tile = jnp.where(row == 0, tops[z : z + 1], tile).astype(BF16)
-        out[z, pl.ds(ROWS, 16), :] = jnp.concatenate([tile, jnp.zeros((16, HD - ROWS), BF16)], 1)
+        tiles.append(jnp.where(row == 0, tops[z : z + 1], tile))
+    for z in range(0, ZN, 2):
+        pair = jnp.concatenate([sums[z], tiles[z], sums[z + 1], tiles[z + 1]], 0)
+        out[pl.ds(z * RES, 2 * RES), :] = pair.astype(BF16)
 
 
 def finish_kernel(parts, sums, top, total, weight_hbm, out, weight, sem):
@@ -209,8 +226,12 @@
     row = iota((ZN, HD), 0)
     tops = jnp.full((ZN, HD), NEG, F32)
     counts = jnp.zeros((ZN, HD), F32)
+    received = []
+    for z in range(0, ZN, 2):
+        pair = parts[pl.ds(z * RES, 2 * RES), :].astype(F32)
+        received += [pair[0:RES], pair[RES : 2 * RES]]
     for z in range(ZN):
-        tile = parts[z, pl.ds(ROWS, 16), :].astype(F32)
+        tile = received[z][ROWS:RES]
         tops = jnp.where(row == z, tile[0:1], tops)
         counts = jnp.where(row == z, tile[1:2] + tile[2:3], counts)
     tops = jnp.concatenate([tops, jnp.full((HD - ZN, HD), NEG, F32)], 0)
@@ -224,7 +245,7 @@
     denominator = jnp.sum(factor * counts, 1, keepdims=True) + own_factor * total[...]
     numerator = own_factor * sums[...]
     for z in range(ZN):
-        numerator = numerator + factor[:, z : z + 1] * parts[z, pl.ds(0, ROWS), :].astype(F32)
+        numerator = numerator + factor[:, z : z + 1] * received[z][0:ROWS]
     attended = (numerator / denominator).astype(BF16)
     attended = jnp.concatenate([attended[16 * g : 16 * (g + 1)] for g in range(GROUP)], 1)
     copy.wait()
@@ -305,9 +326,7 @@
     for k in (2, 1, 3):
         arrived.append(lax.ppermute(pages[k], "y", [(y, (y + k) % YN) for y in range(YN)]))
     q = query.transpose(2, 0, 1, 3).reshape(ROWS, HD)
-    queries = call(spread_kernel, shape((ZN, ROWS, HD), BF16), [VMEM], "spread")(q)
-    queries, _ = lax.optimization_barrier((queries, pages[0]))
-    queries = swap(queries, "z")
+    queries = lax.all_gather(q, "z")
     fresh_k = new_kv[:, :, 0, 0].reshape(B * STEPS, HD)
     fresh_v = new_kv[:, :, 1, 0].reshape(B * STEPS, HD)
     local = call(
@@ -318,10 +337,21 @@
         [pltpu.VMEM(((B - MIG) * NOWN * PAGE, HD), BF16)] * 2,
         pl.CostEstimate(flops=10**8, bytes_accessed=3 * 2**20, transcendentals=10**5),
     )(own_pages, lengths, q, fresh_k, fresh_v, store)
-    parts = call(partial_kernel, shape((ZN, RES, HD), BF16), [HBM] + [VMEM] * 4, "partials", [
-        pltpu.VMEM((CHUNK, HD), BF16), pltpu.SemaphoreType.DMA(())
-    ])(hbm(arrived[0]), *[vmem(x) for x in arrived[1:]], queries)
-    parts = swap(parts, "z")
+    mask = call(
+        mask_kernel,
+        shape((ZN * 16, YN * KEYS), F32),
+        [ANY] * YN,
+        "token_masks",
+        [pltpu.VMEM((YN, ZN, HD), BF16), pltpu.SemaphoreType.DMA((YN,))],
+    )(*arrived)
+    parts = call(
+        partial_kernel,
+        shape((ZN * RES, HD), BF16),
+        [VMEM] + [ANY] * YN + [VMEM],
+        "partials",
+        [pltpu.VMEM((YN, CHUNK, HD), BF16), pltpu.SemaphoreType.DMA((2, YN, 2))],
+    )(mask, *arrived, queries)
+    parts = swap(parts.reshape(ZN, RES, HD), "z").reshape(ZN * RES, HD)
     width = o_weight.shape[1] // TPN
     shares = call(finish_kernel, shape((TPN, 16, width), BF16), [VMEM] * 4 + [HBM], "finish", [
         pltpu.VMEM(o_weight.shape, BF16), pltpu.SemaphoreType.DMA(())

time: 123 us -> 118 us (0.959)
  blocking collectives: 15.9 us -> 41.1 us
  waiting for transfers between devices: 42.9 us -> 23.2 us
  starting transfers between devices: 43.9 us -> 33.6 us
  Pallas kernels: 16.6 us -> 18.4 us
  local copies, waits for them, and re-layouts: 2.63 us -> 1.1 us
    all_gather x0 -> x1, blocking collectives: none -> 22.5 us  [shards(): queries = lax.all_gather(q, 'z')]
    ppermute x3, waiting for transfers between devices: 19.3 us -> 0.01 us  [shards(): lax.ppermute(pages[k], 'y', [(y, (y + k) % YN) for y in range(YN)])]
    all_to_all x3 -> x2, starting transfers between devices: 34.4 us -> 24 us  [swap(): return lax.all_to_all(x, axes, split_axis=0, concat_axis=0, tiled=True)]
    all_to_all x1, blocking collectives: 15.9 us -> 18.6 us  [swap(): return lax.all_to_all(x, axes, split_axis=0, concat_axis=0, tiled=True)]
    pallas_call x2, Pallas kernels: 6.22 us -> 8.07 us  [the longest x1 7.73 us: shards(): call(partial_kernel, shape((ZN * RES, HD), BF16), [VMEM] + [ANY] * YN + [...]
    all_to_all x3 -> x2, waiting for transfers between devices: 23.7 us -> 23.2 us  [swap(): return lax.all_to_all(x, axes, split_axis=0, concat_axis=0, tiled=True)]
  transfers between devices with their start and end apart: 6 -> 5, of which waited for: 4 -> 2; matrix products, arithmetic and copies ran while one was open for 1% -> 0% of each run, Pallas kernels for 3% -> 3%
where the time goes in v3:
time: 118 us
  blocking collectives  41.1 us (35%)
  starting transfers between devices  33.6 us (28%)
  waiting for transfers between devices  23.2 us (20%)
  Pallas kernels  18.4 us (16%)
    all_to_all x2, starting transfers between devices, swap(): return lax.all_to_all(x, axes, split_axis=0, concat_axis=0, tiled=True)  24 us
    all_to_all x2, waiting for transfers between devices, swap(): return lax.all_to_all(x, axes, split_axis=0, concat_axis=0, tiled=True)  23.2 us
    all_gather x1, blocking collectives, shards(): queries = lax.all_gather(q, 'z')  22.5 us
    all_to_all x1, blocking collectives, swap(): return lax.all_to_all(x, axes, split_axis=0, concat_axis=0, tiled=True)  18.6 us
    ppermute x3, starting transfers between devices, shards(): lax.ppermute(pages[k], 'y', [(y, (y + k) % YN) for y in range(YN)])  9.53 us
    pallas_call x1, Pallas kernels, shards(): call(partial_kernel, shape((ZN * RES, HD), BF16), [VMEM] + [ANY] * YN + [...  7.73 us
    pallas_call x1, Pallas kernels, shards(): call(gather_kernel, [pltpu.HBM((CHUNK, HD), BF16)] * YN, [SMEM, SMEM, VME...  2.54 us
  transfers between devices with their start and end apart: 5, of which 2 were waited for; matrix products, arithmetic and copies ran while one was open for 0% of the time, Pallas kernels for 3%

profile of v3, /device:TPU:1, one launch (start us, length us, event | category | flops | bytes accessed | tf_op | source)
XLA Modules:
  0.0 117.6 jit_solution(17426283320699074806)
XLA Ops:
  0.0 1.8 %request.1 = s32[64,128]{1,0:T(8,128)} custom-call(s32[4,8]{1,0:T(4,128)} %prefix_hbm.1, s32[8,24]{1,0:T(8,128)} %own.1, s32[8]{0:T(128)} %fork_hbm.1, s32[8]{0:T(128)} %length.1), custom_call_target="tpu_custom_call" | custom-call | tf_op jit(solution)/shard_map/request/pallas_call | solution.py:301
  1.8 19.3 %all-to-all-start = ((s32[64,1,128]{2,1,0:T(1,128)}), s32[64,1,128]{2,1,0:T(1,128)S(1)}, u32[]{:S(2)}, u32[]{:S(2)}) async-start(s32[64,1,128]{2,1,0:T(1,128)} %bitcast.2), calls=%async_computation | async-start | bytes 65536 | tf_op jit(solution)/shard_map/all_to_all | solution.py:295
  21.1 1.6 %store_ahead.1.store = bf16[256,2,16,128]{3,2,1,0:T(8,128)(2,1)S(1)} custom-call(bf16[256,2,16,128]{3,2,1,0:T(8,128)(2,1)} %bitcast.20), custom_call_target="tpu_custom_call" | custom-call | tf_op jit(solution)/shard_map/store_ahead/pallas_call | solution.py:289
  22.7 0.0 copy-start.4
  22.7 11.7 %all-to-all-done = s32[64,1,128]{2,1,0:T(1,128)S(1)} async-done(((s32[64,1,128]{2,1,0:T(1,128)}), s32[64,1,128]{2,1,0:T(1,128)S(1)}, u32[]{:S(2)}, u32[]{:S(2)}) %all-to-all-start) | async-done | bytes 32800 | tf_op jit(solution)/shard_map/all_to_all | solution.py:295
  34.4 2.5 %gather_pages.1 = (bf16[2064,128]{1,0:T(8,128)(2,1)}, bf16[2064,128]{1,0:T(8,128)(2,1)}, bf16[2064,128]{1,0:T(8,128)(2,1)}, bf16[2064,128]{1,0:T(8,128)(2,1)}) custom-call(s32[1]{0:T(128)} %bitcast.column, s32[64,128]{1,0:T(8,128)S(1)} %bitcast.14, s32[64,128]{1,0:T(8,128)S(1)} %bitcast.15, bf16[256,2,16,128]{3,2,1,0:T(8,128)(2,1)S(1)} %store_ahead.1.store), custom_call_target="tpu_custom_call" | custom-call | tf_op jit(solution)/shard_map/gather_pages/pallas_call | solution.py:317
  36.9 3.0 %collective-permute-start = (bf16[2064,128]{1,0:T(8,128)(2,1)}, bf16[2064,128]{1,0:T(8,128)(2,1)S(1)}, u32[]{:S(2)}, u32[]{:S(2)}) collective-permute-start(bf16[2064,128]{1,0:T(8,128)(2,1)} %get-tuple-element.13), channel_id=1, source_target_pairs={{0,16},{8,24},{16,0},{24,8},{1,17},{9,25},{17,1},{25,9},{2,18},{10... | collective-permute-start | bytes 1585160 | tf_op jit(solution)/shard_map/ppermute | solution.py:327
  40.0 2.1 %collective-permute-start.1 = (bf16[2064,128]{1,0:T(8,128)(2,1)}, bf16[2064,128]{1,0:T(8,128)(2,1)S(1)}, u32[]{:S(2)}, u32[]{:S(2)}) collective-permute-start(bf16[2064,128]{1,0:T(8,128)(2,1)} %get-tuple-element.14), channel_id=1, source_target_pairs={{0,8},{8,16},{16,24},{24,0},{1,9},{9,17},{17,25},{25,1},{2,10},{10... | collective-permute-start | bytes 1585160 | tf_op jit(solution)/shard_map/ppermute | solution.py:327
  42.1 4.3 %collective-permute-start.2 = (bf16[2064,128]{1,0:T(8,128)(2,1)}, bf16[2064,128]{1,0:T(8,128)(2,1)S(1)}, u32[]{:S(2)}, u32[]{:S(2)}) collective-permute-start(bf16[2064,128]{1,0:T(8,128)(2,1)} %get-tuple-element.15), channel_id=1, source_target_pairs={{0,24},{8,0},{16,8},{24,16},{1,25},{9,1},{17,9},{25,17},{2,26},{10... | collective-permute-start | bytes 1585160 | tf_op jit(solution)/shard_map/ppermute | solution.py:327
  46.5 22.5 %all_gather.3.queries = bf16[16,64,128]{2,1,0:T(8,128)(2,1)S(1)} all-gather(bf16[1,64,128]{2,1,0:T(8,128)(2,1)S(1)} %bitcast.16), channel_id=1, replica_groups=mesh['z'=16,'y'=4,'x'=4,'c'=2] {'z'}, dimensions={0}, use_global_device_ids=true | all-gather | bytes 278528 | tf_op jit(solution)/shard_map/all_gather | solution.py:329
  69.0 0.0 collective-permute-done.c1
  69.0 0.0 collective-permute-done.1.c2
  69.1 1.0 copy-done
  70.1 0.3 token_masks.1.mask
  70.4 0.0 copy-start.3
  70.4 0.0 copy-start.1
  70.5 0.0 copy-start.2
  70.5 7.7 %partials.1 = bf16[1152,128]{1,0:T(8,128)(2,1)} custom-call(f32[256,256]{1,0:T(8,128)S(1)} %token_masks.1.mask, bf16[2064,128]{1,0:T(8,128)(2,1)S(1)} %copy-done, bf16[2064,128]{1,0:T(8,128)(2,1)S(1)} %collective-permute-done.c1, bf16[2064,128]{1,0:T(8,128)(2,1)S(1)} %collective-permute-done.1.c2, bf16[2064,128]{1,0:T(8,128)(2,1)S(1)} %collective-permute-done.2.c3, ...), custom_call_target="tpu_custom_call" | custom-call | tf_op jit(solution)/shard_map/partials/pallas_call | solution.py:347
  78.2 4.7 %all-to-all-start.1 = ((bf16[16,72,128]{2,1,0:T(8,128)(2,1)}), bf16[16,72,128]{2,1,0:T(8,128)(2,1)S(1)}, u32[]{:S(2)}, u32[]{:S(2)}) async-start(bf16[16,72,128]{2,1,0:T(8,128)(2,1)} %bitcast.7), calls=%async_computation.1 | async-start | bytes 589824 | tf_op jit(solution)/shard_map/all_to_all | solution.py:295
  83.0 1.5 %resident.1 = (f32[64,128]{1,0:T(8,128)S(1)}, f32[64,128]{1,0:T(8,128)S(1)}, f32[64,128]{1,0:T(8,128)S(1)}) custom-call(s32[8,24]{1,0:T(8,128)S(1)} %copy-done.1, s32[8]{0:T(128)S(1)} %copy-done.2, bf16[64,128]{1,0:T(8,128)(2,1)S(1)} %bitcast.17, bf16[16,128]{1,0:T(8,128)(2,1)S(1)} %bitcast.19, bf16[16,128]{1,0:T(8,128)(2,1)S(1)} %bitcast.18, ...), custom_call_target="tpu_custom_call" | custom-call | flops 100000000 | bytes 3145728 | tf_op jit(solution)/shard_map/resident/pallas_call | solution.py:332
  84.6 11.6 %all-to-all-done.1 = bf16[16,72,128]{2,1,0:T(8,128)(2,1)S(1)} async-done(((bf16[16,72,128]{2,1,0:T(8,128)(2,1)}), bf16[16,72,128]{2,1,0:T(8,128)(2,1)S(1)}, u32[]{:S(2)}, u32[]{:S(2)}) %all-to-all-start.1) | async-done | bytes 294944 | tf_op jit(solution)/shard_map/all_to_all | solution.py:295
  96.1 2.3 %finish.1 = bf16[8,16,320]{2,1,0:T(8,128)(2,1)S(1)} custom-call(bf16[1152,128]{1,0:T(8,128)(2,1)S(1)} %bitcast.13, f32[64,128]{1,0:T(8,128)S(1)} %get-tuple-element.16.sums, f32[64,128]{1,0:T(8,128)S(1)} %get-tuple-element.17.top, f32[64,128]{1,0:T(8,128)S(1)} %get-tuple-element.18.total, bf16[512,2560]{1,0:T(8,128)(2,1)} %weight_hbm.1), custom_call_target="tpu_custom_call" | custom-call | tf_op jit(solution)/shard_map/finish/pallas_call | solution.py:356
  98.4 18.6 %all_to_all.21.shares = bf16[8,16,320]{2,1,0:T(8,128)(2,1)S(1)} all-to-all(bf16[8,16,320]{2,1,0:T(8,128)(2,1)S(1)} %finish.1), channel_id=1, replica_groups=mesh['z'=16,'y'=4,'x'=4,'c'=2] {'x','c'}, dimensions={0} | all-to-all | bytes 163840 | tf_op jit(solution)/shard_map/all_to_all | solution.py:295
  117.0 0.6 total.1
  (10 shorter events, 0.1 us)
Async XLA Ops:
  1.8 32.6 %all-to-all-start = ((s32[64,1,128]{2,1,0:T(1,128)}), s32[64,1,128]{2,1,0:T(1,128)S(1)}, u32[]{:S(2)}, u32[]{:S(2)}) async-start(s32[64,1,128]{2,1,0:T(1,128)} %bitcast.2), calls=%async_computation | async-start | bytes 65536 | tf_op jit(solution)/shard_map/all_to_all | solution.py:295
  22.7 23.8 %copy-start.4 = (bf16[8,2,4,128]{3,2,1,0:T(4,128)(2,1)S(1)}, bf16[8,2,4,128]{3,2,1,0:T(4,128)(2,1)}, u32[]{:S(2)}) copy-start(bf16[8,2,4,128]{3,2,1,0:T(4,128)(2,1)} %param.8) | copy-start | bytes 49156
  36.9 32.1 %collective-permute-start = (bf16[2064,128]{1,0:T(8,128)(2,1)}, bf16[2064,128]{1,0:T(8,128)(2,1)S(1)}, u32[]{:S(2)}, u32[]{:S(2)}) collective-permute-start(bf16[2064,128]{1,0:T(8,128)(2,1)} %get-tuple-element.13), channel_id=1, source_target_pairs={{0,16},{8,24},{16,0},{24,8},{1,17},{9,25},{17,1},{25,9},{2,18},{10... | collective-permute-start | bytes 1585160 | tf_op jit(solution)/shard_map/ppermute | solution.py:327
  40.0 29.1 %collective-permute-start.1 = (bf16[2064,128]{1,0:T(8,128)(2,1)}, bf16[2064,128]{1,0:T(8,128)(2,1)S(1)}, u32[]{:S(2)}, u32[]{:S(2)}) collective-permute-start(bf16[2064,128]{1,0:T(8,128)(2,1)} %get-tuple-element.14), channel_id=1, source_target_pairs={{0,8},{8,16},{16,24},{24,0},{1,9},{9,17},{17,25},{25,1},{2,10},{10... | collective-permute-start | bytes 1585160 | tf_op jit(solution)/shard_map/ppermute | solution.py:327
  42.1 26.9 %collective-permute-start.2 = (bf16[2064,128]{1,0:T(8,128)(2,1)}, bf16[2064,128]{1,0:T(8,128)(2,1)S(1)}, u32[]{:S(2)}, u32[]{:S(2)}) collective-permute-start(bf16[2064,128]{1,0:T(8,128)(2,1)} %get-tuple-element.15), channel_id=1, source_target_pairs={{0,24},{8,0},{16,8},{24,16},{1,25},{9,1},{17,9},{25,17},{2,26},{10... | collective-permute-start | bytes 1585160 | tf_op jit(solution)/shard_map/ppermute | solution.py:327
  69.0 1.0 copy-start
  70.4 12.5 %copy-start.3 = (bf16[8,2,2,1,128]{4,2,3,1,0:T(2,128)(2,1)S(1)}, bf16[8,2,2,1,128]{4,2,3,1,0:T(2,128)(2,1)}, u32[]{:S(2)}) copy-start(bf16[8,2,2,1,128]{4,2,3,1,0:T(2,128)(2,1)} %param.9) | copy-start | bytes 24580
  70.4 12.6 %copy-start.1 = (s32[8,24]{1,0:T(8,128)S(1)}, s32[8,24]{1,0:T(8,128)}, u32[]{:S(2)}) copy-start(s32[8,24]{1,0:T(8,128)} %own.1) | copy-start | bytes 2308
  70.5 12.6 %copy-start.2 = (s32[8]{0:T(128)S(1)}, s32[8]{0:T(128)}, u32[]{:S(2)}) copy-start(s32[8]{0:T(128)} %length.1) | copy-start | bytes 100
  78.2 17.9 %all-to-all-start.1 = ((bf16[16,72,128]{2,1,0:T(8,128)(2,1)}), bf16[16,72,128]{2,1,0:T(8,128)(2,1)S(1)}, u32[]{:S(2)}, u32[]{:S(2)}) async-start(bf16[16,72,128]{2,1,0:T(8,128)(2,1)} %bitcast.7), calls=%async_computation.1 | async-start | bytes 589824 | tf_op jit(solution)/shard_map/all_to_all | solution.py:295

commit v4 on v3

--- a/solution.py
+++ b/solution.py
@@ -27,6 +27,8 @@
 NEG = -(2.0**100)
 SCALE = 1.0 / math.sqrt(HD)
 ZN, YN, XN, CN = 16, 4, 4, 2
+ZL = 4
+Z = ("zh", "zl")
 POOL = ZN * YN
 TPN = XN * CN
 PREFIX_IDS = ROOTS * NPRE
@@ -98,20 +100,17 @@
     copy.wait()
 
 
-def gather_kernel(column, places, req, store, *refs):
-    outs, stages, sems = refs[:YN], refs[YN : 2 * YN], refs[2 * YN]
+def gather_kernel(places, req, store, out, stage, sems):
     copies = []
-    for k, stage in enumerate(stages):
-        base = ((column[0] + k) % YN) * ZN
+    for y in range(YN):
         for z in range(ZN):
             for s in range(SLOTS):
-                at = places[base + z, 16 * s + 8]
+                at = places[y * ZN + z, 16 * s + 8]
                 start = z * KEYS + s * PAGE
-                stage[pl.ds(start, PAGE), :] = store[at, 0]
-                stage[pl.ds(PAGE_ROWS + start, PAGE), :] = store[at, 1]
-        rows = req[pl.ds(pl.multiple_of(base, ZN), ZN), :]
-        stage[pl.ds(2 * PAGE_ROWS, ZN), :] = rows.astype(F32).astype(BF16)
-        copy = pltpu.make_async_copy(stage, outs[k], sems.at[k])
+                stage[y, pl.ds(start, PAGE), :] = store[at, 0]
+                stage[y, pl.ds(PAGE_ROWS + start, PAGE), :] = store[at, 1]
+        stage[y, pl.ds(2 * PAGE_ROWS, ZN), :] = req[pl.ds(y * ZN, ZN), :].astype(F32).astype(BF16)
+        copy = pltpu.make_async_copy(stage.at[y], out.at[y], sems.at[y])
         copy.start()
         copies.append(copy)
     for copy in copies:
@@ -153,19 +152,11 @@
     total[...] = jnp.broadcast_to(count, (ROWS, HD))
 
 
-def mask_kernel(c0, c1, c2, c3, out, tiles, sems):
-    chunks = (c0, c1, c2, c3)
-    copies = [
-        pltpu.make_async_copy(c.at[pl.ds(2 * PAGE_ROWS, ZN), :], tiles.at[k], sems.at[k]) for k, c in enumerate(chunks)
-    ]
-    for copy in copies:
-        copy.start()
-    for copy in copies:
-        copy.wait()
+def partial_kernel(pages, queries, out):
     pick = iota((16, HD), 1) % 16 == iota((16, HD), 0) // STEPS
     blocks = []
     for k in range(YN):
-        tile = tiles[k].astype(F32)
+        tile = pages[k, pl.ds(2 * PAGE_ROWS, ZN), :].astype(F32)
         rows = [jnp.where(pick, jnp.broadcast_to(tile[z : z + 1], (16, HD)), 0.0).astype(BF16) for z in range(ZN)]
         blocks.append(jnp.concatenate(rows, 0))
     width = YN * KEYS
@@ -174,28 +165,12 @@
     expand = (source // HD == key // KEYS) & ((source % HD) // 16 == (key % KEYS) // PAGE)
     tokens = dot(jnp.concatenate(blocks, 1), expand.astype(F32).astype(BF16))
     number = (iota((ZN * 16, width), 1) % PAGE).astype(F32)
-    out[...] = jnp.where(number < tokens, 0.0, NEG)
-
-
-def partial_kernel(mask, c0, c1, c2, c3, queries, out, pages, sems):
-    half = PAGE_ROWS // 2
-    copies = []
-    for part in range(2):
-        for k, chunk in enumerate((c0, c1, c2, c3)):
-            for kv in range(2):
-                rows = pl.ds(kv * PAGE_ROWS + part * half, half)
-                copy = pltpu.make_async_copy(chunk.at[rows, :], pages.at[k, rows, :], sems.at[part, k, kv])
-                copy.start()
-                copies.append(copy)
+    mask = jnp.where(number < tokens, 0.0, NEG)
     column = iota((ROWS, HD), 1)
     stats = jnp.zeros((ROWS, HD), F32)
     sums = []
     for z in range(ZN):
-        if z % (ZN // 2) == 0:
-            first = (z // (ZN // 2)) * 2 * YN
-            for copy in copies[first : first + 2 * YN]:
-                copy.wait()
-        bias = jnp.concatenate([mask[pl.ds(z * 16, 16), :]] * GROUP, 0)
+        bias = jnp.concatenate([mask[z * 16 : (z + 1) * 16]] * GROUP, 0)
         keys = jnp.concatenate([pages[k, pl.ds(z * KEYS, KEYS), :] for k in range(YN)], 0)
         values = jnp.concatenate([pages[k, pl.ds(PAGE_ROWS + z * KEYS, KEYS), :] for k in range(YN)], 0)
         score = jnp.where(bias < 0.0, NEG, dot(queries[z], keys, NT) * SCALE)
@@ -311,22 +286,22 @@
             pltpu.SemaphoreType.DMA((4,)),
         ],
     )(hbm(prefix_pages), hbm(own_pages), hbm(fork_of), hbm(lengths))
-    request = swap(request, ("y", "z"))
-    column = lax.axis_index("y").astype(I32).reshape(1)
+    request = swap(request, ("y", *Z))
+    q = query.transpose(2, 0, 1, 3).reshape(ROWS, HD)
+    near = lax.all_gather(q, "zl")
+    request, near = lax.optimization_barrier((request, near))
     store = prefetch(store, "store_ahead")
     pages = call(
         gather_kernel,
-        [pltpu.HBM((CHUNK, HD), BF16)] * YN,
-        [SMEM, SMEM, VMEM, VMEM],
+        pltpu.HBM((YN, CHUNK, HD), BF16),
+        [SMEM, VMEM, VMEM],
         "gather_pages",
-        [pltpu.VMEM((CHUNK, HD), BF16)] * YN + [pltpu.SemaphoreType.DMA((YN,))],
-        out_specs=[HBM] * YN,
-    )(column, request, request, vmem(store))
-    arrived = [pages[0]]
-    for k in (2, 1, 3):
-        arrived.append(lax.ppermute(pages[k], "y", [(y, (y + k) % YN) for y in range(YN)]))
-    q = query.transpose(2, 0, 1, 3).reshape(ROWS, HD)
-    queries = lax.all_gather(q, "z")
+        [pltpu.VMEM((YN, CHUNK, HD), BF16), pltpu.SemaphoreType.DMA((YN,))],
+        out_specs=HBM,
+    )(request, request, vmem(store))
+    near, pages = lax.optimization_barrier((near, pages))
+    pages = swap(pages, "y")
+    queries = lax.all_gather(near, "zh").reshape(ZN, ROWS, HD)
     fresh_k = new_kv[:, :, 0, 0].reshape(B * STEPS, HD)
     fresh_v = new_kv[:, :, 1, 0].reshape(B * STEPS, HD)
     local = call(
@@ -337,21 +312,8 @@
         [pltpu.VMEM(((B - MIG) * NOWN * PAGE, HD), BF16)] * 2,
         pl.CostEstimate(flops=10**8, bytes_accessed=3 * 2**20, transcendentals=10**5),
     )(own_pages, lengths, q, fresh_k, fresh_v, store)
-    mask = call(
-        mask_kernel,
-        shape((ZN * 16, YN * KEYS), F32),
-        [ANY] * YN,
-        "token_masks",
-        [pltpu.VMEM((YN, ZN, HD), BF16), pltpu.SemaphoreType.DMA((YN,))],
-    )(*arrived)
-    parts = call(
-        partial_kernel,
-        shape((ZN * RES, HD), BF16),
-        [VMEM] + [ANY] * YN + [VMEM],
-        "partials",
-        [pltpu.VMEM((YN, CHUNK, HD), BF16), pltpu.SemaphoreType.DMA((2, YN, 2))],
-    )(mask, *arrived, queries)
-    parts = swap(parts.reshape(ZN, RES, HD), "z").reshape(ZN * RES, HD)
+    parts = call(partial_kernel, shape((ZN * RES, HD), BF16), [VMEM] * 2, "partials")(pages, queries)
+    parts = swap(parts.reshape(ZN, RES, HD), Z).reshape(ZN * RES, HD)
     width = o_weight.shape[1] // TPN
     shares = call(finish_kernel, shape((TPN, 16, width), BF16), [VMEM] * 4 + [HBM], "finish", [
         pltpu.VMEM(o_weight.shape, BF16), pltpu.SemaphoreType.DMA(())
@@ -363,8 +325,8 @@
 
 
 def solution(mesh):
-    fine = Mesh(mesh.devices.reshape(ZN, YN, XN, CN), ("z", "y", "x", "c"))
-    pool, tp = ("z", "y"), ("x", "c")
+    fine = Mesh(mesh.devices.reshape(ZN // ZL, ZL, YN, XN, CN), ("zh", "zl", "y", "x", "c"))
+    pool, tp = ("zh", "zl", "y"), ("x", "c")
     return jax.shard_map(
         shards,
         mesh=fine,

time: 118 us -> 115 us (0.975)
  blocking collectives: 41.1 us -> 49.5 us
  waiting for transfers between devices: 23.2 us -> 14.9 us
  Pallas kernels: 18.4 us -> 16.3 us
    ppermute x3 -> x0, starting transfers between devices: 9.53 us -> none  [shards(): lax.ppermute(pages[k], 'y', [(y, (y + k) % YN) for y in range(YN)])]
    all_gather x1 -> x2, blocking collectives: 22.5 us -> 31.6 us  [the longest x1 20.3 us: shards(): queries = lax.all_gather(near, 'zh').reshape(ZN, ROWS, HD)]
    all_to_all x2 -> x3, starting transfers between devices: 24 us -> 32.5 us  [swap(): return lax.all_to_all(x, axes, split_axis=0, concat_axis=0, tiled=True)]
    all_to_all x2 -> x3, waiting for transfers between devices: 23.2 us -> 14.9 us  [swap(): return lax.all_to_all(x, axes, split_axis=0, concat_axis=0, tiled=True)]
    pallas_call x3 -> x2, Pallas kernels: 10.6 us -> 8.47 us  [the longest x1 5.98 us: shards(): call(partial_kernel, shape((ZN * RES, HD), BF16), [VMEM] * 2, 'partials')]
  transfers between devices with their start and end apart: 5 -> 3, of which waited for: 2 -> 2; matrix products, arithmetic and copies ran while one was open for 0% -> 1% of each run, Pallas kernels for 3% -> 3%
where the time goes in v4:
time: 115 us; the launch traced here: 114 us
  blocking collectives  49.5 us (43%)
  starting transfers between devices  32.5 us (28%)
  Pallas kernels  16.3 us (14%)
  waiting for transfers between devices  14.9 us (13%)
    all_to_all x3, starting transfers between devices, swap(): return lax.all_to_all(x, axes, split_axis=0, concat_axis=0, tiled=True)  32.5 us
    all_gather x1, blocking collectives, shards(): queries = lax.all_gather(near, 'zh').reshape(ZN, ROWS, HD)  20.3 us
    all_to_all x1, blocking collectives, swap(): return lax.all_to_all(x, axes, split_axis=0, concat_axis=0, tiled=True)  18 us
    all_to_all x3, waiting for transfers between devices, swap(): return lax.all_to_all(x, axes, split_axis=0, concat_axis=0, tiled=True)  14.9 us
    all_gather x1, blocking collectives, shards(): near = lax.all_gather(q, 'zl')  11.3 us
    pallas_call x1, Pallas kernels, shards(): call(partial_kernel, shape((ZN * RES, HD), BF16), [VMEM] * 2, 'partials')  5.98 us
    pallas_call x1, Pallas kernels, shards(): call(gather_kernel, pltpu.HBM((YN, CHUNK, HD), BF16), [SMEM, VMEM, VMEM],...  2.48 us
  transfers between devices with their start and end apart: 3, of which 2 were waited for; matrix products, arithmetic and copies ran while one was open for 1% of the time, Pallas kernels for 3%

profile of v4, /device:TPU:1, one launch (start us, length us, event | category | flops | bytes accessed | tf_op | source)
XLA Modules:
  0.0 114.1 jit_solution(13102433848935638602)
XLA Ops:
  0.0 1.8 %request.1 = s32[64,128]{1,0:T(8,128)} custom-call(s32[4,8]{1,0:T(4,128)} %prefix_hbm.1, s32[8,24]{1,0:T(8,128)} %own.1, s32[8]{0:T(128)} %fork_hbm.1, s32[8]{0:T(128)} %length.1), custom_call_target="tpu_custom_call" | custom-call | tf_op jit(solution)/shard_map/request/pallas_call | solution.py:276
  1.8 19.3 %all-to-all-start = ((s32[64,1,128]{2,1,0:T(1,128)}), s32[64,1,128]{2,1,0:T(1,128)S(1)}, u32[]{:S(2)}, u32[]{:S(2)}) async-start(s32[64,1,128]{2,1,0:T(1,128)} %bitcast.1), calls=%async_computation | async-start | bytes 65536 | tf_op jit(solution)/shard_map/all_to_all | solution.py:270
  21.1 0.7 copy.14
  21.8 1.6 %store_ahead.1.store = bf16[256,2,16,128]{3,2,1,0:T(8,128)(2,1)S(1)} custom-call(bf16[256,2,16,128]{3,2,1,0:T(8,128)(2,1)} %bitcast.19), custom_call_target="tpu_custom_call" | custom-call | tf_op jit(solution)/shard_map/store_ahead/pallas_call | solution.py:264
  23.4 11.3 %all_gather.9 = bf16[4,64,128]{2,1,0:T(8,128)(2,1)S(1)} all-gather(bf16[1,64,128]{2,1,0:T(8,128)(2,1)S(1)} %bitcast.15), channel_id=1, replica_groups=mesh['zh'=4,'zl'=4,'y'=4,'x'=4,'c'=2] {'zl'}, dimensions={0}, use_global_device_ids=true | all-gather | bytes 81920 | tf_op jit(solution)/shard_map/all_gather | solution.py:291
  34.8 0.0 all-to-all-done
  34.8 2.5 %gather_pages.1 = bf16[4,2064,128]{2,1,0:T(8,128)(2,1)} custom-call(s32[64,128]{1,0:T(8,128)S(1)} %bitcast.13, s32[64,128]{1,0:T(8,128)S(1)} %bitcast.14, bf16[256,2,16,128]{3,2,1,0:T(8,128)(2,1)S(1)} %store_ahead.1.store), custom_call_target="tpu_custom_call" | custom-call | tf_op jit(solution)/shard_map/gather_pages/pallas_call | solution.py:294
  37.2 4.5 %all-to-all-start.1 = ((bf16[4,2064,128]{2,1,0:T(8,128)(2,1)}), bf16[4,2064,128]{2,1,0:T(8,128)(2,1)}, u32[]{:S(2)}, u32[]{:S(2)}) async-start(bf16[4,2064,128]{2,1,0:T(8,128)(2,1)} %gather_pages.1), calls=%async_computation.1 | async-start | bytes 4227072 | tf_op jit(solution)/shard_map/all_to_all | solution.py:270
  41.7 0.0 copy-start.2
  41.7 0.0 copy-start
  41.7 0.0 copy-start.1
  41.7 20.3 %all-gather.queries = bf16[16,64,128]{2,1,0:T(8,128)(2,1)S(1)} all-gather(bf16[4,64,128]{2,1,0:T(8,128)(2,1)S(1)} %all_gather.9), channel_id=2, replica_groups=mesh['zh'=4,'zl'=4,'y'=4,'x'=4,'c'=2] {'zh'}, dimensions={0}, use_global_device_ids=true | all-gather | bytes 327680 | tf_op jit(solution)/shard_map/all_gather | solution.py:304
  62.0 3.4 %all-to-all-done.1.pages = bf16[4,2064,128]{2,1,0:T(8,128)(2,1)} async-done(((bf16[4,2064,128]{2,1,0:T(8,128)(2,1)}), bf16[4,2064,128]{2,1,0:T(8,128)(2,1)}, u32[]{:S(2)}, u32[]{:S(2)}) %all-to-all-start.1) | async-done | bytes 2113568 | tf_op jit(solution)/shard_map/all_to_all | solution.py:270
  65.4 6.0 %partials.1 = bf16[1152,128]{1,0:T(8,128)(2,1)} custom-call(bf16[4,2064,128]{2,1,0:T(8,128)(2,1)} %all-to-all-done.1.pages, bf16[16,64,128]{2,1,0:T(8,128)(2,1)S(1)} %all-gather.queries), custom_call_target="tpu_custom_call" | custom-call | tf_op jit(solution)/shard_map/partials/pallas_call | solution.py:315
  71.4 8.8 %all-to-all-start.2 = ((bf16[16,72,128]{2,1,0:T(8,128)(2,1)}), bf16[16,72,128]{2,1,0:T(8,128)(2,1)S(1)}, u32[]{:S(2)}, u32[]{:S(2)}) async-start(bf16[16,72,128]{2,1,0:T(8,128)(2,1)} %bitcast.6), calls=%async_computation.2 | async-start | bytes 589824 | tf_op jit(solution)/shard_map/all_to_all | solution.py:270
  80.2 0.0 copy-done.2
  80.2 0.0 copy-done
  80.2 0.0 copy-done.1
  80.2 1.5 %resident.1 = (f32[64,128]{1,0:T(8,128)S(1)}, f32[64,128]{1,0:T(8,128)S(1)}, f32[64,128]{1,0:T(8,128)S(1)}) custom-call(s32[8,24]{1,0:T(8,128)S(1)} %copy-done, s32[8]{0:T(128)S(1)} %copy-done.1, bf16[64,128]{1,0:T(8,128)(2,1)S(1)} %bitcast.16, bf16[16,128]{1,0:T(8,128)(2,1)S(1)} %bitcast.18, bf16[16,128]{1,0:T(8,128)(2,1)S(1)} %bitcast.17, ...), custom_call_target="tpu_custom_call" | custom-call | flops 100000000 | bytes 3145728 | tf_op jit(solution)/shard_map/resident/pallas_call | solution.py:307
  81.8 11.5 %all-to-all-done.2 = bf16[16,72,128]{2,1,0:T(8,128)(2,1)S(1)} async-done(((bf16[16,72,128]{2,1,0:T(8,128)(2,1)}), bf16[16,72,128]{2,1,0:T(8,128)(2,1)S(1)}, u32[]{:S(2)}, u32[]{:S(2)}) %all-to-all-start.2) | async-done | bytes 294944 | tf_op jit(solution)/shard_map/all_to_all | solution.py:270
  93.3 2.3 %finish.1 = bf16[8,16,320]{2,1,0:T(8,128)(2,1)S(1)} custom-call(bf16[1152,128]{1,0:T(8,128)(2,1)S(1)} %bitcast.12, f32[64,128]{1,0:T(8,128)S(1)} %get-tuple-element.16.sums, f32[64,128]{1,0:T(8,128)S(1)} %get-tuple-element.17.top, f32[64,128]{1,0:T(8,128)S(1)} %get-tuple-element.18.total, bf16[512,2560]{1,0:T(8,128)(2,1)} %weight_hbm.1), custom_call_target="tpu_custom_call" | custom-call | tf_op jit(solution)/shard_map/finish/pallas_call | solution.py:318
  95.5 18.0 %all_to_all.27.shares = bf16[8,16,320]{2,1,0:T(8,128)(2,1)S(1)} all-to-all(bf16[8,16,320]{2,1,0:T(8,128)(2,1)S(1)} %finish.1), channel_id=1, replica_groups=mesh['zh'=4,'zl'=4,'y'=4,'x'=4,'c'=2] {'x','c'}, dimensions={0} | all-to-all | bytes 163840 | tf_op jit(solution)/shard_map/all_to_all | solution.py:270
  113.5 0.6 total.1
  (3 shorter events, 0.0 us)
Async XLA Ops:
  1.8 33.0 %all-to-all-start = ((s32[64,1,128]{2,1,0:T(1,128)}), s32[64,1,128]{2,1,0:T(1,128)S(1)}, u32[]{:S(2)}, u32[]{:S(2)}) async-start(s32[64,1,128]{2,1,0:T(1,128)} %bitcast.1), calls=%async_computation | async-start | bytes 65536 | tf_op jit(solution)/shard_map/all_to_all | solution.py:270
  37.2 28.2 %all-to-all-start.1 = ((bf16[4,2064,128]{2,1,0:T(8,128)(2,1)}), bf16[4,2064,128]{2,1,0:T(8,128)(2,1)}, u32[]{:S(2)}, u32[]{:S(2)}) async-start(bf16[4,2064,128]{2,1,0:T(8,128)(2,1)} %gather_pages.1), calls=%async_computation.1 | async-start | bytes 4227072 | tf_op jit(solution)/shard_map/all_to_all | solution.py:270
  41.7 38.5 %copy-start.2 = (bf16[8,2,2,1,128]{4,2,3,1,0:T(2,128)(2,1)S(1)}, bf16[8,2,2,1,128]{4,2,3,1,0:T(2,128)(2,1)}, u32[]{:S(2)}) copy-start(bf16[8,2,2,1,128]{4,2,3,1,0:T(2,128)(2,1)} %param.9) | copy-start | bytes 24580
  41.7 38.5 %copy-start = (s32[8,24]{1,0:T(8,128)S(1)}, s32[8,24]{1,0:T(8,128)}, u32[]{:S(2)}) copy-start(s32[8,24]{1,0:T(8,128)} %own.1) | copy-start | bytes 2308
  41.7 38.5 %copy-start.1 = (s32[8]{0:T(128)S(1)}, s32[8]{0:T(128)}, u32[]{:S(2)}) copy-start(s32[8]{0:T(128)} %length.1) | copy-start | bytes 100
  71.4 21.9 %all-to-all-start.2 = ((bf16[16,72,128]{2,1,0:T(8,128)(2,1)}), bf16[16,72,128]{2,1,0:T(8,128)(2,1)S(1)}, u32[]{:S(2)}, u32[]{:S(2)}) async-start(bf16[16,72,128]{2,1,0:T(8,128)(2,1)} %bitcast.6), calls=%async_computation.2 | async-start | bytes 589824 | tf_op jit(solution)/shard_map/all_to_all | solution.py:270

commit v5 on v4

--- a/solution.py
+++ b/solution.py
@@ -28,6 +28,8 @@
 SCALE = 1.0 / math.sqrt(HD)
 ZN, YN, XN, CN = 16, 4, 4, 2
 ZL = 4
+PARTS = 2
+AHEAD = 2
 Z = ("zh", "zl")
 POOL = ZN * YN
 TPN = XN * CN
@@ -94,10 +96,21 @@
     req[...] = out.astype(I32)
 
 
-def prefetch_kernel(source, out, sem):
-    copy = pltpu.make_async_copy(source, out, sem)
-    copy.start()
-    copy.wait()
+def order_kernel(place, own, far, left, right, out):
+    for k, ref in ((0, own), (2, far), (1, left), (3, right)):
+        out[(place[0] + ZL - k) % ZL] = ref[...]
+
+
+def prefetch_kernel(source, out, sems):
+    part = out.shape[0] // sems.shape[0]
+    copies = [
+        pltpu.make_async_copy(source.at[pl.ds(n * part, part)], out.at[pl.ds(n * part, part)], sems.at[n])
+        for n in range(sems.shape[0])
+    ]
+    for copy in copies:
+        copy.start()
+    for copy in copies:
+        copy.wait()
 
 
 def gather_kernel(places, req, store, out, stage, sems):
@@ -152,52 +165,77 @@
     total[...] = jnp.broadcast_to(count, (ROWS, HD))
 
 
-def partial_kernel(pages, queries, out):
+def partial_kernel(source, queries, out, pages, meta, meta_sem, sems):
+    size = PAGE_ROWS // PARTS
+    per = ZN // PARTS
+    meta_copy = pltpu.make_async_copy(source.at[:, pl.ds(2 * PAGE_ROWS, ZN), :], meta, meta_sem)
+    meta_copy.start()
+    copies = []
+    for part in range(PARTS):
+        group = []
+        for kv in range(2):
+            rows = pl.ds(kv * PAGE_ROWS + part * size, size)
+            copy = pltpu.make_async_copy(source.at[:, rows, :], pages.at[:, rows, :], sems.at[part, kv])
+            copy.start()
+            group.append(copy)
+        copies.append(group)
+    meta_copy.wait()
     pick = iota((16, HD), 1) % 16 == iota((16, HD), 0) // STEPS
     blocks = []
     for k in range(YN):
-        tile = pages[k, pl.ds(2 * PAGE_ROWS, ZN), :].astype(F32)
+        tile = meta[k].astype(F32)
         rows = [jnp.where(pick, jnp.broadcast_to(tile[z : z + 1], (16, HD)), 0.0).astype(BF16) for z in range(ZN)]
         blocks.append(jnp.concatenate(rows, 0))
     width = YN * KEYS
     shape = (YN * HD, width)
-    source, key = iota(shape, 0), iota(shape, 1)
-    expand = (source // HD == key // KEYS) & ((source % HD) // 16 == (key % KEYS) // PAGE)
+    origin, key = iota(shape, 0), iota(shape, 1)
+    expand = (origin // HD == key // KEYS) & ((origin % HD) // 16 == (key % KEYS) // PAGE)
     tokens = dot(jnp.concatenate(blocks, 1), expand.astype(F32).astype(BF16))
     number = (iota((ZN * 16, width), 1) % PAGE).astype(F32)
     mask = jnp.where(number < tokens, 0.0, NEG)
     column = iota((ROWS, HD), 1)
-    stats = jnp.zeros((ROWS, HD), F32)
-    sums = []
-    for z in range(ZN):
-        bias = jnp.concatenate([mask[z * 16 : (z + 1) * 16]] * GROUP, 0)
-        keys = jnp.concatenate([pages[k, pl.ds(z * KEYS, KEYS), :] for k in range(YN)], 0)
-        values = jnp.concatenate([pages[k, pl.ds(PAGE_ROWS + z * KEYS, KEYS), :] for k in range(YN)], 0)
-        score = jnp.where(bias < 0.0, NEG, dot(queries[z], keys, NT) * SCALE)
-        best = jnp.max(score, 1, keepdims=True).astype(BF16).astype(F32)
-        weight = jnp.where(bias < 0.0, 0.0, jnp.exp(score - best)).astype(BF16)
-        count = jnp.sum(weight.astype(F32), 1, keepdims=True)
-        sums.append(dot(weight, values))
-        stats = jnp.where(column == z, best, jnp.where(column == ZN + z, count, stats))
-    turned = jnp.transpose(stats)
-    turned = jnp.concatenate([turned, jnp.zeros((HD, HD - ROWS), F32)], 1)
-    tops = turned[0:ZN]
-    counts = turned[ZN : 2 * ZN]
-    high = counts.astype(BF16).astype(F32)
-    low = counts - high
     row = iota((8, HD), 0)
-    tiles = []
-    for z in range(ZN):
-        tile = jnp.where(row == 1, high[z : z + 1], jnp.where(row == 2, low[z : z + 1], 0.0))
-        tiles.append(jnp.where(row == 0, tops[z : z + 1], tile))
-    for z in range(0, ZN, 2):
-        pair = jnp.concatenate([sums[z], tiles[z], sums[z + 1], tiles[z + 1]], 0)
-        out[pl.ds(z * RES, 2 * RES), :] = pair.astype(BF16)
-
-
-def finish_kernel(parts, sums, top, total, weight_hbm, out, weight, sem):
-    copy = pltpu.make_async_copy(weight_hbm, weight, sem)
-    copy.start()
+    for part in range(PARTS):
+        members = range(part * per, (part + 1) * per)
+        for copy in copies[part]:
+            copy.wait()
+        scores = []
+        for z in members:
+            keys = jnp.concatenate([pages[k, pl.ds(z * KEYS, KEYS), :] for k in range(YN)], 0)
+            scores.append(dot(queries[z], keys, NT))
+        stats = jnp.zeros((ROWS, HD), F32)
+        weights = []
+        for n, z in enumerate(members):
+            bias = jnp.concatenate([mask[z * 16 : (z + 1) * 16]] * GROUP, 0)
+            score = jnp.where(bias < 0.0, NEG, scores[n] * SCALE)
+            best = jnp.max(score, 1, keepdims=True).astype(BF16).astype(F32)
+            weight = jnp.where(bias < 0.0, 0.0, jnp.exp(score - best)).astype(BF16)
+            count = jnp.sum(weight.astype(F32), 1, keepdims=True)
+            weights.append(weight)
+            stats = jnp.where(column == n, best, jnp.where(column == 8 + n, count, stats))
+        turned = jnp.transpose(stats)[0:16]
+        turned = jnp.concatenate([turned, jnp.zeros((16, HD - ROWS), F32)], 1)
+        tops, counts = turned[0:8], turned[8:16]
+        high = counts.astype(BF16).astype(F32)
+        low = counts - high
+        rows = []
+        for n, z in enumerate(members):
+            values = jnp.concatenate([pages[k, pl.ds(PAGE_ROWS + z * KEYS, KEYS), :] for k in range(YN)], 0)
+            tile = jnp.where(row == 1, high[n : n + 1], jnp.where(row == 2, low[n : n + 1], 0.0))
+            rows += [dot(weights[n], values), jnp.where(row == 0, tops[n : n + 1], tile)]
+        out[pl.ds(part * per * RES, per * RES), :] = jnp.concatenate(rows, 0).astype(BF16)
+
+
+def finish_kernel(parts, sums, top, total, early, weight_hbm, out, late, sems):
+    ahead = early.shape[0] // HD
+    copies = [
+        pltpu.make_async_copy(
+            weight_hbm.at[pl.ds((ahead + n) * HD, HD), :], late.at[pl.ds(n * HD, HD), :], sems.at[n]
+        )
+        for n in range(GROUP - ahead)
+    ]
+    for copy in copies:
+        copy.start()
     row = iota((ZN, HD), 0)
     tops = jnp.full((ZN, HD), NEG, F32)
     counts = jnp.zeros((ZN, HD), F32)
@@ -222,9 +260,15 @@
     for z in range(ZN):
         numerator = numerator + factor[:, z : z + 1] * received[z][0:ROWS]
     attended = (numerator / denominator).astype(BF16)
-    attended = jnp.concatenate([attended[16 * g : 16 * (g + 1)] for g in range(GROUP)], 1)
-    copy.wait()
-    result = dot(attended, weight[...]).astype(BF16).astype(F32)
+    result = jnp.zeros((16, late.shape[1]), F32)
+    for g in range(GROUP):
+        if g < ahead:
+            rows = early[pl.ds(g * HD, HD), :]
+        else:
+            copies[g - ahead].wait()
+            rows = late[pl.ds((g - ahead) * HD, HD), :]
+        result = result + dot(attended[16 * g : 16 * (g + 1)], rows)
+    result = result.astype(BF16).astype(F32)
     width = out.shape[2]
     for k in range(TPN):
         out[k] = result[:, k * width : (k + 1) * width].astype(BF16)
@@ -260,10 +304,23 @@
     return pltpu.with_memory_space_constraint(x, pltpu.VMEM)
 
 
-def prefetch(x, name):
+def prefetch(x, name, rows=None):
     return call(
-        prefetch_kernel, pltpu.VMEM(x.shape, x.dtype), [HBM], name, [pltpu.SemaphoreType.DMA(())], out_specs=VMEM
+        prefetch_kernel,
+        pltpu.VMEM((rows or x.shape[0], *x.shape[1:]), x.dtype),
+        [HBM],
+        name,
+        [pltpu.SemaphoreType.DMA((8,))],
+        out_specs=VMEM,
     )(hbm(x))
+
+
+PARTIAL_SCRATCH = [
+    pltpu.VMEM((YN, CHUNK, HD), BF16),
+    pltpu.VMEM((YN, ZN, HD), BF16),
+    pltpu.SemaphoreType.DMA(()),
+    pltpu.SemaphoreType.DMA((PARTS, 2)),
+]
 
 
 def swap(x, axes):
@@ -288,7 +345,9 @@
     )(hbm(prefix_pages), hbm(own_pages), hbm(fork_of), hbm(lengths))
     request = swap(request, ("y", *Z))
     q = query.transpose(2, 0, 1, 3).reshape(ROWS, HD)
-    near = lax.all_gather(q, "zl")
+    shifted = [lax.ppermute(q, "zl", [(z, (z + k) % ZL) for z in range(ZL)]) for k in (2, 1, 3)]
+    place = lax.axis_index("zl").astype(I32).reshape(1)
+    near = call(order_kernel, shape((ZL, ROWS, HD), BF16), [SMEM] + [VMEM] * ZL, "order")(place, q, *shifted)
     request, near = lax.optimization_barrier((request, near))
     store = prefetch(store, "store_ahead")
     pages = call(
@@ -312,14 +371,18 @@
         [pltpu.VMEM(((B - MIG) * NOWN * PAGE, HD), BF16)] * 2,
         pl.CostEstimate(flops=10**8, bytes_accessed=3 * 2**20, transcendentals=10**5),
     )(own_pages, lengths, q, fresh_k, fresh_v, store)
-    parts = call(partial_kernel, shape((ZN * RES, HD), BF16), [VMEM] * 2, "partials")(pages, queries)
+    parts = call(partial_kernel, shape((ZN * RES, HD), BF16), [HBM, VMEM], "partials", PARTIAL_SCRATCH)(pages, queries)
     parts = swap(parts.reshape(ZN, RES, HD), Z).reshape(ZN * RES, HD)
     width = o_weight.shape[1] // TPN
-    shares = call(finish_kernel, shape((TPN, 16, width), BF16), [VMEM] * 4 + [HBM], "finish", [
-        pltpu.VMEM(o_weight.shape, BF16), pltpu.SemaphoreType.DMA(())
-    ])(
-        parts, *local, hbm(o_weight)
-    )
+    early = prefetch(o_weight, "weight_ahead", AHEAD * HD)
+    rest = (GROUP - AHEAD) * HD
+    shares = call(
+        finish_kernel,
+        shape((TPN, 16, width), BF16),
+        [VMEM] * 5 + [HBM],
+        "finish",
+        [pltpu.VMEM((rest, o_weight.shape[1]), BF16), pltpu.SemaphoreType.DMA((GROUP - AHEAD,))],
+    )(parts, *local, vmem(early), hbm(o_weight))
     shares = swap(shares, ("x", "c"))
     return call(total_kernel, shape((B, STEPS, width), BF16), [VMEM], "total")(shares)
 

time: 115 us -> 112 us (0.974)
  blocking collectives: 49.5 us -> 36.4 us
  starting transfers between devices: 32.5 us -> 41.9 us
  waiting for transfers between devices: 14.9 us -> 16.6 us
    all_gather x1 -> x0, blocking collectives: 11.3 us -> none  [shards(): near = lax.all_gather(q, 'zl')]
    ppermute x0 -> x3, starting transfers between devices: none -> 9.1 us  [shards(): lax.ppermute(q, 'zl', [(z, (z + k) % ZL) for z in range(ZL)])]
    ppermute x0 -> x3, waiting for transfers between devices: none -> 1.62 us  [shards(): lax.ppermute(q, 'zl', [(z, (z + k) % ZL) for z in range(ZL)])]
    pallas_call x3 -> x5, Pallas kernels: 9.86 us -> 9.13 us  [the longest x1 3.56 us: shards(): call(partial_kernel, shape((ZN * RES, HD), BF16), [HBM, VMEM], 'partials'...]
  transfers between devices with their start and end apart: 3 -> 6, of which waited for: 2 -> 4; matrix products, arithmetic and copies ran while one was open for 1% -> 1% of each run, Pallas kernels for 3% -> 4%
where the time goes in v5:
time: 112 us; the launch traced here: 111 us
  starting transfers between devices  41.9 us (37%)
  blocking collectives  36.4 us (32%)
  waiting for transfers between devices  16.6 us (15%)
  Pallas kernels  15.5 us (14%)
    all_to_all x3, starting transfers between devices, swap(): return lax.all_to_all(x, axes, split_axis=0, concat_axis=0, tiled=True)  32.8 us
    all_gather x1, blocking collectives, shards(): queries = lax.all_gather(near, 'zh').reshape(ZN, ROWS, HD)  19.4 us
    all_to_all x1, blocking collectives, swap(): return lax.all_to_all(x, axes, split_axis=0, concat_axis=0, tiled=True)  17 us
    all_to_all x3, waiting for transfers between devices, swap(): return lax.all_to_all(x, axes, split_axis=0, concat_axis=0, tiled=True)  15 us
    ppermute x3, starting transfers between devices, shards(): lax.ppermute(q, 'zl', [(z, (z + k) % ZL) for z in range(ZL)])  9.1 us
    pallas_call x1, Pallas kernels, shards(): call(partial_kernel, shape((ZN * RES, HD), BF16), [HBM, VMEM], 'partials'...  3.56 us
    pallas_call x2, Pallas kernels, prefetch(): call(prefetch_kernel, pltpu.VMEM((rows or x.shape[0], *x.shape[1:]), x.dt...  3.03 us
    pallas_call x1, Pallas kernels, shards(): call(finish_kernel, shape((TPN, 16, width), BF16), [VMEM] * 5 + [HBM], 'f...  2.53 us
  transfers between devices with their start and end apart: 6, of which 4 were waited for; matrix products, arithmetic and copies ran while one was open for 1% of the time, Pallas kernels for 4%

profile of v5, /device:TPU:1, one launch (start us, length us, event | category | flops | bytes accessed | tf_op | source)
XLA Modules:
  0.0 111.4 jit_solution(14860821673243717684)
XLA Ops:
  0.0 1.8 %request.1 = s32[64,128]{1,0:T(8,128)} custom-call(s32[4,8]{1,0:T(4,128)} %prefix_hbm.1, s32[8,24]{1,0:T(8,128)} %own.1, s32[8]{0:T(128)} %fork_hbm.1, s32[8]{0:T(128)} %length.1), custom_call_target="tpu_custom_call" | custom-call | tf_op jit(solution)/shard_map/request/pallas_call | solution.py:333
  1.8 19.3 %all-to-all-start = ((s32[64,1,128]{2,1,0:T(1,128)}), s32[64,1,128]{2,1,0:T(1,128)S(1)}, u32[]{:S(2)}, u32[]{:S(2)}) async-start(s32[64,1,128]{2,1,0:T(1,128)} %bitcast.1), calls=%async_computation | async-start | bytes 65536 | tf_op jit(solution)/shard_map/all_to_all | solution.py:327
  21.1 0.7 copy.12
  21.8 4.7 %collective-permute-start.2 = (bf16[64,128]{1,0:T(8,128)(2,1)S(1)}, bf16[64,128]{1,0:T(8,128)(2,1)S(1)}, u32[]{:S(2)}, u32[]{:S(2)}) collective-permute-start(bf16[64,128]{1,0:T(8,128)(2,1)S(1)} %bitcast.14), channel_id=1, source_target_pairs={{0,96},{32,0},{64,32},{96,64},{1,97},{33,1},{65,33},{97,65},{2,98}... | collective-permute-start | bytes 49160 | tf_op jit(solution)/shard_map/ppermute | solution.py:348
  26.6 1.9 %collective-permute-start.1 = (bf16[64,128]{1,0:T(8,128)(2,1)S(1)}, bf16[64,128]{1,0:T(8,128)(2,1)S(1)}, u32[]{:S(2)}, u32[]{:S(2)}) collective-permute-start(bf16[64,128]{1,0:T(8,128)(2,1)S(1)} %bitcast.15), channel_id=1, source_target_pairs={{0,32},{32,64},{64,96},{96,0},{1,33},{33,65},{65,97},{97,1},{2,34}... | collective-permute-start | bytes 49160 | tf_op jit(solution)/shard_map/ppermute | solution.py:348
  28.5 2.5 %collective-permute-start = (bf16[64,128]{1,0:T(8,128)(2,1)S(1)}, bf16[64,128]{1,0:T(8,128)(2,1)S(1)}, u32[]{:S(2)}, u32[]{:S(2)}) collective-permute-start(bf16[64,128]{1,0:T(8,128)(2,1)S(1)} %bitcast.16), channel_id=1, source_target_pairs={{0,64},{32,96},{64,0},{96,32},{1,65},{33,97},{65,1},{97,33},{2,66}... | collective-permute-start | bytes 49160 | tf_op jit(solution)/shard_map/ppermute | solution.py:348
  31.0 1.6 %store_ahead.1.store = bf16[256,2,16,128]{3,2,1,0:T(8,128)(2,1)S(1)} custom-call(bf16[256,2,16,128]{3,2,1,0:T(8,128)(2,1)} %bitcast.21), custom_call_target="tpu_custom_call" | custom-call | tf_op jit(solution)/shard_map/store_ahead/pallas_call | solution.py:308
  32.5 0.6 collective-permute-done.1.left
  33.1 1.0 collective-permute-done.far
  34.2 0.0 all-to-all-done
  34.2 2.5 %gather_pages.1 = bf16[4,2064,128]{2,1,0:T(8,128)(2,1)} custom-call(s32[64,128]{1,0:T(8,128)S(1)} %bitcast.12, s32[64,128]{1,0:T(8,128)S(1)} %bitcast.13, bf16[256,2,16,128]{3,2,1,0:T(8,128)(2,1)S(1)} %store_ahead.1.store), custom_call_target="tpu_custom_call" | custom-call | tf_op jit(solution)/shard_map/gather_pages/pallas_call | solution.py:353
  36.7 4.5 %all-to-all-start.1 = ((bf16[4,2064,128]{2,1,0:T(8,128)(2,1)}), bf16[4,2064,128]{2,1,0:T(8,128)(2,1)}, u32[]{:S(2)}, u32[]{:S(2)}) async-start(bf16[4,2064,128]{2,1,0:T(8,128)(2,1)} %gather_pages.1), calls=%async_computation.1 | async-start | bytes 4227072 | tf_op jit(solution)/shard_map/all_to_all | solution.py:327
  41.2 0.0 copy-start.2
  41.2 19.4 %all-gather.queries = bf16[16,64,128]{2,1,0:T(8,128)(2,1)S(1)} all-gather(bf16[4,64,128]{2,1,0:T(8,128)(2,1)S(1)} %order.1), channel_id=2, replica_groups=mesh['zh'=4,'zl'=4,'y'=4,'x'=4,'c'=2] {'zh'}, dimensions={0}, use_global_device_ids=true | all-gather | bytes 327680 | tf_op jit(solution)/shard_map/all_gather | solution.py:363
  60.5 4.9 %all-to-all-done.1.source = bf16[4,2064,128]{2,1,0:T(8,128)(2,1)} async-done(((bf16[4,2064,128]{2,1,0:T(8,128)(2,1)}), bf16[4,2064,128]{2,1,0:T(8,128)(2,1)}, u32[]{:S(2)}, u32[]{:S(2)}) %all-to-all-start.1) | async-done | bytes 2113568 | tf_op jit(solution)/shard_map/all_to_all | solution.py:327
  65.4 3.6 %partials.1 = bf16[1152,128]{1,0:T(8,128)(2,1)} custom-call(bf16[4,2064,128]{2,1,0:T(8,128)(2,1)} %all-to-all-done.1.source, bf16[16,64,128]{2,1,0:T(8,128)(2,1)S(1)} %all-gather.queries), custom_call_target="tpu_custom_call" | custom-call | tf_op jit(solution)/shard_map/partials/pallas_call | solution.py:374
  69.0 9.1 %all-to-all-start.2 = ((bf16[16,72,128]{2,1,0:T(8,128)(2,1)}), bf16[16,72,128]{2,1,0:T(8,128)(2,1)}, u32[]{:S(2)}, u32[]{:S(2)}) async-start(bf16[16,72,128]{2,1,0:T(8,128)(2,1)} %bitcast.7), calls=%async_computation.2 | async-start | bytes 589824 | tf_op jit(solution)/shard_map/all_to_all | solution.py:327
  78.1 0.0 copy-start.1
  78.1 1.5 %weight_ahead.1.early = bf16[256,2560]{1,0:T(8,128)(2,1)S(1)} custom-call(bf16[512,2560]{1,0:T(8,128)(2,1)} %weight_hbm.1), custom_call_target="tpu_custom_call" | custom-call | tf_op jit(solution)/shard_map/weight_ahead/pallas_call | solution.py:308
  79.6 1.5 %resident.1 = (f32[64,128]{1,0:T(8,128)S(1)}, f32[64,128]{1,0:T(8,128)S(1)}, f32[64,128]{1,0:T(8,128)S(1)}) custom-call(s32[8,24]{1,0:T(8,128)S(1)} %copy-done, s32[8]{0:T(128)S(1)} %copy-done.1, bf16[64,128]{1,0:T(8,128)(2,1)S(1)} %bitcast.18, bf16[16,128]{1,0:T(8,128)(2,1)S(1)} %bitcast.20, bf16[16,128]{1,0:T(8,128)(2,1)S(1)} %bitcast.19, ...), custom_call_target="tpu_custom_call" | custom-call | flops 100000000 | bytes 3145728 | tf_op jit(solution)/shard_map/resident/pallas_call | solution.py:366
  81.2 10.1 %all-to-all-done.2 = bf16[16,72,128]{2,1,0:T(8,128)(2,1)} async-done(((bf16[16,72,128]{2,1,0:T(8,128)(2,1)}), bf16[16,72,128]{2,1,0:T(8,128)(2,1)}, u32[]{:S(2)}, u32[]{:S(2)}) %all-to-all-start.2) | async-done | bytes 294944 | tf_op jit(solution)/shard_map/all_to_all | solution.py:327
  91.2 2.5 %finish.1 = bf16[8,16,320]{2,1,0:T(8,128)(2,1)S(1)} custom-call(bf16[1152,128]{1,0:T(8,128)(2,1)} %bitcast.8.parts, f32[64,128]{1,0:T(8,128)S(1)} %get-tuple-element.16.sums, f32[64,128]{1,0:T(8,128)S(1)} %get-tuple-element.17.top, f32[64,128]{1,0:T(8,128)S(1)} %get-tuple-element.18.total, bf16[256,2560]{1,0:T(8,128)(2,1)S(1)} %weight_ahead.1.early, ...), custom_call_target="tpu_custom_call" | custom-call | tf_op jit(solution)/shard_map/finish/pallas_call | solution.py:379
  93.8 17.0 %all_to_all.27.shares = bf16[8,16,320]{2,1,0:T(8,128)(2,1)S(1)} all-to-all(bf16[8,16,320]{2,1,0:T(8,128)(2,1)S(1)} %finish.1), channel_id=1, replica_groups=mesh['zh'=4,'zl'=4,'y'=4,'x'=4,'c'=2] {'x','c'}, dimensions={0} | all-to-all | bytes 163840 | tf_op jit(solution)/shard_map/all_to_all | solution.py:327
  110.8 0.6 total.1
  (9 shorter events, 0.0 us)
Async XLA Ops:
  1.8 32.4 %all-to-all-start = ((s32[64,1,128]{2,1,0:T(1,128)}), s32[64,1,128]{2,1,0:T(1,128)S(1)}, u32[]{:S(2)}, u32[]{:S(2)}) async-start(s32[64,1,128]{2,1,0:T(1,128)} %bitcast.1), calls=%async_computation | async-start | bytes 65536 | tf_op jit(solution)/shard_map/all_to_all | solution.py:327
  21.8 10.7 %collective-permute-start.2 = (bf16[64,128]{1,0:T(8,128)(2,1)S(1)}, bf16[64,128]{1,0:T(8,128)(2,1)S(1)}, u32[]{:S(2)}, u32[]{:S(2)}) collective-permute-start(bf16[64,128]{1,0:T(8,128)(2,1)S(1)} %bitcast.14), channel_id=1, source_target_pairs={{0,96},{32,0},{64,32},{96,64},{1,97},{33,1},{65,33},{97,65},{2,98}... | collective-permute-start | bytes 49160 | tf_op jit(solution)/shard_map/ppermute | solution.py:348
  26.6 6.6 %collective-permute-start.1 = (bf16[64,128]{1,0:T(8,128)(2,1)S(1)}, bf16[64,128]{1,0:T(8,128)(2,1)S(1)}, u32[]{:S(2)}, u32[]{:S(2)}) collective-permute-start(bf16[64,128]{1,0:T(8,128)(2,1)S(1)} %bitcast.15), channel_id=1, source_target_pairs={{0,32},{32,64},{64,96},{96,0},{1,33},{33,65},{65,97},{97,1},{2,34}... | collective-permute-start | bytes 49160 | tf_op jit(solution)/shard_map/ppermute | solution.py:348
  28.5 5.7 %collective-permute-start = (bf16[64,128]{1,0:T(8,128)(2,1)S(1)}, bf16[64,128]{1,0:T(8,128)(2,1)S(1)}, u32[]{:S(2)}, u32[]{:S(2)}) collective-permute-start(bf16[64,128]{1,0:T(8,128)(2,1)S(1)} %bitcast.16), channel_id=1, source_target_pairs={{0,64},{32,96},{64,0},{96,32},{1,65},{33,97},{65,1},{97,33},{2,66}... | collective-permute-start | bytes 49160 | tf_op jit(solution)/shard_map/ppermute | solution.py:348
  36.7 28.7 %all-to-all-start.1 = ((bf16[4,2064,128]{2,1,0:T(8,128)(2,1)}), bf16[4,2064,128]{2,1,0:T(8,128)(2,1)}, u32[]{:S(2)}, u32[]{:S(2)}) async-start(bf16[4,2064,128]{2,1,0:T(8,128)(2,1)} %gather_pages.1), calls=%async_computation.1 | async-start | bytes 4227072 | tf_op jit(solution)/shard_map/all_to_all | solution.py:327
  41.2 36.9 %copy-start.2 = (bf16[8,2,2,1,128]{4,2,3,1,0:T(2,128)(2,1)S(1)}, bf16[8,2,2,1,128]{4,2,3,1,0:T(2,128)(2,1)}, u32[]{:S(2)}) copy-start(bf16[8,2,2,1,128]{4,2,3,1,0:T(2,128)(2,1)} %param.9) | copy-start | bytes 24580
  69.0 22.2 %all-to-all-start.2 = ((bf16[16,72,128]{2,1,0:T(8,128)(2,1)}), bf16[16,72,128]{2,1,0:T(8,128)(2,1)}, u32[]{:S(2)}, u32[]{:S(2)}) async-start(bf16[16,72,128]{2,1,0:T(8,128)(2,1)} %bitcast.7), calls=%async_computation.2 | async-start | bytes 589824 | tf_op jit(solution)/shard_map/all_to_all | solution.py:327
  78.1 1.5 %copy-start = (s32[8,24]{1,0:T(8,128)S(1)}, s32[8,24]{1,0:T(8,128)}, u32[]{:S(2)}) copy-start(s32[8,24]{1,0:T(8,128)} %own.1) | copy-start | bytes 2308
  78.1 1.5 %copy-start.1 = (s32[8]{0:T(128)S(1)}, s32[8]{0:T(128)}, u32[]{:S(2)}) copy-start(s32[8]{0:T(128)} %length.1) | copy-start | bytes 100

commit v6 on v5

--- a/solution.py
+++ b/solution.py
@@ -27,16 +27,19 @@
 NEG = -(2.0**100)
 SCALE = 1.0 / math.sqrt(HD)
 ZN, YN, XN, CN = 16, 4, 4, 2
-ZL = 4
+ZH, ZM, ZL = 4, 2, 2
 PARTS = 2
-AHEAD = 2
-Z = ("zh", "zl")
+POOL_AXES = ("zh", "zm", "zl", "y")
+NEAR = ("zl", "y")
+FAR = ("zh", "zm")
+SOURCES = ZL * YN
+MEMBERS = ZH * ZM
 POOL = ZN * YN
 TPN = XN * CN
 PREFIX_IDS = ROOTS * NPRE
 KEYS = SLOTS * PAGE
-PAGE_ROWS = ZN * KEYS
-CHUNK = 2 * PAGE_ROWS + ZN
+PAGE_ROWS = MEMBERS * KEYS
+CHUNK = 2 * PAGE_ROWS + 16
 RES = ROWS + 8
 
 VMEM = pl.BlockSpec(memory_space=pltpu.VMEM)
@@ -84,7 +87,8 @@
     place = jnp.where(row == 0, ids % P_DEV, 0)
     table = jnp.concatenate([tokens, place], 0).astype(F32).astype(BF16)
     holder = ids // P_DEV
-    holder = (holder % YN) * ZN + holder // YN
+    plane, row_y = holder // YN, holder % YN
+    holder = ((plane % ZL) * YN + row_y) * MEMBERS + plane // ZL
     member = jnp.broadcast_to(holder[0:1], (POOL, HD)) == iota((POOL, HD), 0)
     earlier = (iota((HD, HD), 0) < iota((HD, HD), 1)).astype(F32).astype(BF16)
     rank = dot(member.astype(F32).astype(BF16), earlier)
@@ -96,9 +100,9 @@
     req[...] = out.astype(I32)
 
 
-def order_kernel(place, own, far, left, right, out):
-    for k, ref in ((0, own), (2, far), (1, left), (3, right)):
-        out[(place[0] + ZL - k) % ZL] = ref[...]
+def order_kernel(place, own, other, out):
+    out[place[0]] = own[...]
+    out[1 - place[0]] = other[...]
 
 
 def prefetch_kernel(source, out, sems):
@@ -115,15 +119,17 @@
 
 def gather_kernel(places, req, store, out, stage, sems):
     copies = []
-    for y in range(YN):
-        for z in range(ZN):
+    for c in range(SOURCES):
+        for n in range(MEMBERS):
             for s in range(SLOTS):
-                at = places[y * ZN + z, 16 * s + 8]
-                start = z * KEYS + s * PAGE
-                stage[y, pl.ds(start, PAGE), :] = store[at, 0]
-                stage[y, pl.ds(PAGE_ROWS + start, PAGE), :] = store[at, 1]
-        stage[y, pl.ds(2 * PAGE_ROWS, ZN), :] = req[pl.ds(y * ZN, ZN), :].astype(F32).astype(BF16)
-        copy = pltpu.make_async_copy(stage.at[y], out.at[y], sems.at[y])
+                at = places[c * MEMBERS + n, 16 * s + 8]
+                start = n * KEYS + s * PAGE
+                stage[c, pl.ds(start, PAGE), :] = store[at, 0]
+                stage[c, pl.ds(PAGE_ROWS + start, PAGE), :] = store[at, 1]
+        rows = req[pl.ds(c * MEMBERS, MEMBERS), :].astype(F32)
+        rows = jnp.concatenate([rows, jnp.zeros((16 - MEMBERS, HD), F32)], 0)
+        stage[c, pl.ds(2 * PAGE_ROWS, 16), :] = rows.astype(BF16)
+        copy = pltpu.make_async_copy(stage.at[c], out.at[c], sems.at[c])
         copy.start()
         copies.append(copy)
     for copy in copies:
@@ -167,8 +173,8 @@
 
 def partial_kernel(source, queries, out, pages, meta, meta_sem, sems):
     size = PAGE_ROWS // PARTS
-    per = ZN // PARTS
-    meta_copy = pltpu.make_async_copy(source.at[:, pl.ds(2 * PAGE_ROWS, ZN), :], meta, meta_sem)
+    per = MEMBERS // PARTS
+    meta_copy = pltpu.make_async_copy(source.at[:, pl.ds(2 * PAGE_ROWS, 16), :], meta, meta_sem)
     meta_copy.start()
     copies = []
     for part in range(PARTS):
@@ -181,17 +187,17 @@
         copies.append(group)
     meta_copy.wait()
     pick = iota((16, HD), 1) % 16 == iota((16, HD), 0) // STEPS
-    blocks = []
-    for k in range(YN):
+    stacks = []
+    for k in range(SOURCES):
         tile = meta[k].astype(F32)
-        rows = [jnp.where(pick, jnp.broadcast_to(tile[z : z + 1], (16, HD)), 0.0).astype(BF16) for z in range(ZN)]
-        blocks.append(jnp.concatenate(rows, 0))
-    width = YN * KEYS
-    shape = (YN * HD, width)
-    origin, key = iota(shape, 0), iota(shape, 1)
-    expand = (origin // HD == key // KEYS) & ((origin % HD) // 16 == (key % KEYS) // PAGE)
-    tokens = dot(jnp.concatenate(blocks, 1), expand.astype(F32).astype(BF16))
-    number = (iota((ZN * 16, width), 1) % PAGE).astype(F32)
+        rows = [jnp.where(pick, jnp.broadcast_to(tile[n : n + 1], (16, HD)), 0.0).astype(BF16) for n in range(MEMBERS)]
+        stacks.append(jnp.concatenate(rows, 0))
+    pairs = [jnp.concatenate(stacks[k : k + 2], 1) for k in range(0, SOURCES, 2)]
+    shape = (2 * HD, 2 * KEYS)
+    expand = iota(shape, 0) // HD * KEYS + (iota(shape, 0) % HD) // 16 * PAGE == iota(shape, 1) // PAGE * PAGE
+    expand = expand & (iota(shape, 0) % HD < KEYS)
+    tokens = dot(jnp.concatenate(pairs, 0), expand.astype(F32).astype(BF16))
+    number = (iota((tokens.shape[0], 2 * KEYS), 1) % PAGE).astype(F32)
     mask = jnp.where(number < tokens, 0.0, NEG)
     column = iota((ROWS, HD), 1)
     row = iota((8, HD), 0)
@@ -201,12 +207,14 @@
             copy.wait()
         scores = []
         for z in members:
-            keys = jnp.concatenate([pages[k, pl.ds(z * KEYS, KEYS), :] for k in range(YN)], 0)
+            keys = jnp.concatenate([pages[k, pl.ds(z * KEYS, KEYS), :] for k in range(SOURCES)], 0)
             scores.append(dot(queries[z], keys, NT))
         stats = jnp.zeros((ROWS, HD), F32)
         weights = []
         for n, z in enumerate(members):
-            bias = jnp.concatenate([mask[z * 16 : (z + 1) * 16]] * GROUP, 0)
+            rows = range(z * 16, SOURCES // 2 * MEMBERS * 16, MEMBERS * 16)
+            bias = jnp.concatenate([mask[r : r + 16] for r in rows], 1)
+            bias = jnp.concatenate([bias] * GROUP, 0)
             score = jnp.where(bias < 0.0, NEG, scores[n] * SCALE)
             best = jnp.max(score, 1, keepdims=True).astype(BF16).astype(F32)
             weight = jnp.where(bias < 0.0, 0.0, jnp.exp(score - best)).astype(BF16)
@@ -220,35 +228,32 @@
         low = counts - high
         rows = []
         for n, z in enumerate(members):
-            values = jnp.concatenate([pages[k, pl.ds(PAGE_ROWS + z * KEYS, KEYS), :] for k in range(YN)], 0)
+            values = jnp.concatenate([pages[k, pl.ds(PAGE_ROWS + z * KEYS, KEYS), :] for k in range(SOURCES)], 0)
             tile = jnp.where(row == 1, high[n : n + 1], jnp.where(row == 2, low[n : n + 1], 0.0))
             rows += [dot(weights[n], values), jnp.where(row == 0, tops[n : n + 1], tile)]
         out[pl.ds(part * per * RES, per * RES), :] = jnp.concatenate(rows, 0).astype(BF16)
 
 
-def finish_kernel(parts, sums, top, total, early, weight_hbm, out, late, sems):
-    ahead = early.shape[0] // HD
+def finish_kernel(parts, sums, top, total, weight_hbm, out, weight, sems):
     copies = [
-        pltpu.make_async_copy(
-            weight_hbm.at[pl.ds((ahead + n) * HD, HD), :], late.at[pl.ds(n * HD, HD), :], sems.at[n]
-        )
-        for n in range(GROUP - ahead)
+        pltpu.make_async_copy(weight_hbm.at[pl.ds(g * HD, HD), :], weight.at[pl.ds(g * HD, HD), :], sems.at[g])
+        for g in range(GROUP)
     ]
     for copy in copies:
         copy.start()
-    row = iota((ZN, HD), 0)
-    tops = jnp.full((ZN, HD), NEG, F32)
-    counts = jnp.zeros((ZN, HD), F32)
+    row = iota((8, HD), 0)
+    tops = jnp.full((8, HD), NEG, F32)
+    counts = jnp.zeros((8, HD), F32)
     received = []
-    for z in range(0, ZN, 2):
+    for z in range(0, MEMBERS, 2):
         pair = parts[pl.ds(z * RES, 2 * RES), :].astype(F32)
         received += [pair[0:RES], pair[RES : 2 * RES]]
-    for z in range(ZN):
+    for z in range(MEMBERS):
         tile = received[z][ROWS:RES]
         tops = jnp.where(row == z, tile[0:1], tops)
         counts = jnp.where(row == z, tile[1:2] + tile[2:3], counts)
-    tops = jnp.concatenate([tops, jnp.full((HD - ZN, HD), NEG, F32)], 0)
-    counts = jnp.concatenate([counts, jnp.zeros((HD - ZN, HD), F32)], 0)
+    tops = jnp.concatenate([tops, jnp.full((HD - 8, HD), NEG, F32)], 0)
+    counts = jnp.concatenate([counts, jnp.zeros((HD - 8, HD), F32)], 0)
     tops = jnp.transpose(tops)[0:ROWS]
     counts = jnp.transpose(counts)[0:ROWS]
     own_top = top[...]
@@ -257,17 +262,13 @@
     own_factor = jnp.exp(own_top - best)
     denominator = jnp.sum(factor * counts, 1, keepdims=True) + own_factor * total[...]
     numerator = own_factor * sums[...]
-    for z in range(ZN):
+    for z in range(MEMBERS):
         numerator = numerator + factor[:, z : z + 1] * received[z][0:ROWS]
     attended = (numerator / denominator).astype(BF16)
-    result = jnp.zeros((16, late.shape[1]), F32)
+    result = jnp.zeros((16, weight.shape[1]), F32)
     for g in range(GROUP):
-        if g < ahead:
-            rows = early[pl.ds(g * HD, HD), :]
-        else:
-            copies[g - ahead].wait()
-            rows = late[pl.ds((g - ahead) * HD, HD), :]
-        result = result + dot(attended[16 * g : 16 * (g + 1)], rows)
+        copies[g].wait()
+        result = result + dot(attended[16 * g : 16 * (g + 1)], weight[pl.ds(g * HD, HD), :])
     result = result.astype(BF16).astype(F32)
     width = out.shape[2]
     for k in range(TPN):
@@ -304,10 +305,10 @@
     return pltpu.with_memory_space_constraint(x, pltpu.VMEM)
 
 
-def prefetch(x, name, rows=None):
+def prefetch(x, name):
     return call(
         prefetch_kernel,
-        pltpu.VMEM((rows or x.shape[0], *x.shape[1:]), x.dtype),
+        pltpu.VMEM(x.shape, x.dtype),
         [HBM],
         name,
         [pltpu.SemaphoreType.DMA((8,))],
@@ -316,8 +317,8 @@
 
 
 PARTIAL_SCRATCH = [
-    pltpu.VMEM((YN, CHUNK, HD), BF16),
-    pltpu.VMEM((YN, ZN, HD), BF16),
+    pltpu.VMEM((SOURCES, CHUNK, HD), BF16),
+    pltpu.VMEM((SOURCES, 16, HD), BF16),
     pltpu.SemaphoreType.DMA(()),
     pltpu.SemaphoreType.DMA((PARTS, 2)),
 ]
@@ -343,24 +344,24 @@
             pltpu.SemaphoreType.DMA((4,)),
         ],
     )(hbm(prefix_pages), hbm(own_pages), hbm(fork_of), hbm(lengths))
-    request = swap(request, ("y", *Z))
+    request = swap(request, NEAR + FAR)
     q = query.transpose(2, 0, 1, 3).reshape(ROWS, HD)
-    shifted = [lax.ppermute(q, "zl", [(z, (z + k) % ZL) for z in range(ZL)]) for k in (2, 1, 3)]
-    place = lax.axis_index("zl").astype(I32).reshape(1)
-    near = call(order_kernel, shape((ZL, ROWS, HD), BF16), [SMEM] + [VMEM] * ZL, "order")(place, q, *shifted)
+    other = lax.ppermute(q, "zm", [(0, 1), (1, 0)])
+    place = lax.axis_index("zm").astype(I32).reshape(1)
+    near = call(order_kernel, shape((ZM, ROWS, HD), BF16), [SMEM, VMEM, VMEM], "order")(place, q, other)
     request, near = lax.optimization_barrier((request, near))
     store = prefetch(store, "store_ahead")
     pages = call(
         gather_kernel,
-        pltpu.HBM((YN, CHUNK, HD), BF16),
+        pltpu.HBM((SOURCES, CHUNK, HD), BF16),
         [SMEM, VMEM, VMEM],
         "gather_pages",
-        [pltpu.VMEM((YN, CHUNK, HD), BF16), pltpu.SemaphoreType.DMA((YN,))],
+        [pltpu.VMEM((SOURCES, CHUNK, HD), BF16), pltpu.SemaphoreType.DMA((SOURCES,))],
         out_specs=HBM,
     )(request, request, vmem(store))
     near, pages = lax.optimization_barrier((near, pages))
-    pages = swap(pages, "y")
-    queries = lax.all_gather(near, "zh").reshape(ZN, ROWS, HD)
+    pages = swap(pages, NEAR)
+    queries = lax.all_gather(near, "zh").reshape(MEMBERS, ROWS, HD)
     fresh_k = new_kv[:, :, 0, 0].reshape(B * STEPS, HD)
     fresh_v = new_kv[:, :, 1, 0].reshape(B * STEPS, HD)
     local = call(
@@ -371,25 +372,25 @@
         [pltpu.VMEM(((B - MIG) * NOWN * PAGE, HD), BF16)] * 2,
         pl.CostEstimate(flops=10**8, bytes_accessed=3 * 2**20, transcendentals=10**5),
     )(own_pages, lengths, q, fresh_k, fresh_v, store)
-    parts = call(partial_kernel, shape((ZN * RES, HD), BF16), [HBM, VMEM], "partials", PARTIAL_SCRATCH)(pages, queries)
-    parts = swap(parts.reshape(ZN, RES, HD), Z).reshape(ZN * RES, HD)
+    parts = call(partial_kernel, shape((MEMBERS * RES, HD), BF16), [HBM, VMEM], "partials", PARTIAL_SCRATCH)(
+        pages, queries
+    )
+    parts = swap(parts.reshape(MEMBERS, RES, HD), FAR).reshape(MEMBERS * RES, HD)
     width = o_weight.shape[1] // TPN
-    early = prefetch(o_weight, "weight_ahead", AHEAD * HD)
-    rest = (GROUP - AHEAD) * HD
     shares = call(
         finish_kernel,
         shape((TPN, 16, width), BF16),
-        [VMEM] * 5 + [HBM],
+        [VMEM] * 4 + [HBM],
         "finish",
-        [pltpu.VMEM((rest, o_weight.shape[1]), BF16), pltpu.SemaphoreType.DMA((GROUP - AHEAD,))],
-    )(parts, *local, vmem(early), hbm(o_weight))
+        [pltpu.VMEM(o_weight.shape, BF16), pltpu.SemaphoreType.DMA((GROUP,))],
+    )(parts, *local, hbm(o_weight))
     shares = swap(shares, ("x", "c"))
     return call(total_kernel, shape((B, STEPS, width), BF16), [VMEM], "total")(shares)
 
 
 def solution(mesh):
-    fine = Mesh(mesh.devices.reshape(ZN // ZL, ZL, YN, XN, CN), ("zh", "zl", "y", "x", "c"))
-    pool, tp = ("zh", "zl", "y"), ("x", "c")
+    fine = Mesh(mesh.devices.reshape(ZH, ZM, ZL, YN, XN, CN), POOL_AXES + ("x", "c"))
+    pool, tp = POOL_AXES, ("x", "c")
     return jax.shard_map(
         shards,
         mesh=fine,

time: 112 us -> 115 us (1.027)
  blocking collectives: 36.4 us -> 46.1 us
  starting transfers between devices: 41.9 us -> 34.1 us
  waiting for transfers between devices: 16.6 us -> 19.9 us
  Pallas kernels: 15.5 us -> 13.4 us
    all_gather x1, blocking collectives: 19.4 us -> 30.8 us  [shards(): queries = lax.all_gather(near, 'zh').reshape(MEMBERS, ROWS, HD)]
    ppermute x3 -> x1, starting transfers between devices: 9.1 us -> 3.82 us  [shards(): other = lax.ppermute(q, 'zm', [(0, 1), (1, 0)])]
    all_to_all x3, waiting for transfers between devices: 15 us -> 19.6 us  [swap(): return lax.all_to_all(x, axes, split_axis=0, concat_axis=0, tiled=True)]
    all_to_all x3, starting transfers between devices: 32.8 us -> 30.3 us  [swap(): return lax.all_to_all(x, axes, split_axis=0, concat_axis=0, tiled=True)]
    pallas_call x6 -> x5, Pallas kernels: 11.6 us -> 9.52 us  [the longest x1 3.45 us: shards(): call(partial_kernel, shape((MEMBERS * RES, HD), BF16), [HBM, VMEM], 'part...]
    all_to_all x1, blocking collectives: 17 us -> 15.3 us  [swap(): return lax.all_to_all(x, axes, split_axis=0, concat_axis=0, tiled=True)]
    ppermute x3 -> x1, waiting for transfers between devices: 1.62 us -> 0.29 us  [shards(): other = lax.ppermute(q, 'zm', [(0, 1), (1, 0)])]
  transfers between devices with their start and end apart: 6 -> 4, of which waited for: 4 -> 3; matrix products, arithmetic and copies ran while one was open for 1% -> 1% of each run, Pallas kernels for 4% -> 3%
where the time goes in v6:
time: 115 us; the launch traced here: 114 us
  blocking collectives  46.1 us (40%)
  starting transfers between devices  34.1 us (30%)
  waiting for transfers between devices  19.9 us (17%)
  Pallas kernels  13.4 us (12%)
    all_gather x1, blocking collectives, shards(): queries = lax.all_gather(near, 'zh').reshape(MEMBERS, ROWS, HD)  30.8 us
    all_to_all x3, starting transfers between devices, swap(): return lax.all_to_all(x, axes, split_axis=0, concat_axis=0, tiled=True)  30.3 us
    all_to_all x3, waiting for transfers between devices, swap(): return lax.all_to_all(x, axes, split_axis=0, concat_axis=0, tiled=True)  19.6 us
    all_to_all x1, blocking collectives, swap(): return lax.all_to_all(x, axes, split_axis=0, concat_axis=0, tiled=True)  15.3 us
    ppermute x1, starting transfers between devices, shards(): other = lax.ppermute(q, 'zm', [(0, 1), (1, 0)])  3.82 us
    pallas_call x1, Pallas kernels, shards(): call(partial_kernel, shape((MEMBERS * RES, HD), BF16), [HBM, VMEM], 'part...  3.45 us
    pallas_call x1, Pallas kernels, shards(): call(gather_kernel, pltpu.HBM((SOURCES, CHUNK, HD), BF16), [SMEM, VMEM, V...  2.5 us
  transfers between devices with their start and end apart: 4, of which 3 were waited for; matrix products, arithmetic and copies ran while one was open for 1% of the time, Pallas kernels for 3%

profile of v6, /device:TPU:1, one launch (start us, length us, event | category | flops | bytes accessed | tf_op | source)
XLA Modules:
  0.0 114.5 jit_solution(10380523838667391826)
XLA Ops:
  0.0 1.8 %request.1 = s32[64,128]{1,0:T(8,128)} custom-call(s32[4,8]{1,0:T(4,128)} %prefix_hbm.1, s32[8,24]{1,0:T(8,128)} %own.1, s32[8]{0:T(128)} %fork_hbm.1, s32[8]{0:T(128)} %length.1), custom_call_target="tpu_custom_call" | custom-call | tf_op jit(solution)/shard_map/request/pallas_call | solution.py:334
  1.8 19.3 %all-to-all-start = ((s32[64,1,128]{2,1,0:T(1,128)}), s32[64,1,128]{2,1,0:T(1,128)S(1)}, u32[]{:S(2)}, u32[]{:S(2)}) async-start(s32[64,1,128]{2,1,0:T(1,128)} %bitcast.1), calls=%async_computation | async-start | bytes 65536 | tf_op jit(solution)/shard_map/all_to_all | solution.py:328
  21.1 0.7 copy.12
  21.8 3.8 %collective-permute-start = (bf16[64,128]{1,0:T(8,128)(2,1)S(1)}, bf16[64,128]{1,0:T(8,128)(2,1)S(1)}, u32[]{:S(2)}, u32[]{:S(2)}) collective-permute-start(bf16[64,128]{1,0:T(8,128)(2,1)S(1)} %bitcast.15), channel_id=1, source_target_pairs={{0,64},{64,0},{1,65},{65,1},{2,66},{66,2},{3,67},{67,3},{4,68},{68... | collective-permute-start | bytes 49160 | tf_op jit(solution)/shard_map/ppermute | solution.py:349
  25.7 1.6 %store_ahead.1.store = bf16[256,2,16,128]{3,2,1,0:T(8,128)(2,1)S(1)} custom-call(bf16[256,2,16,128]{3,2,1,0:T(8,128)(2,1)} %bitcast.20), custom_call_target="tpu_custom_call" | custom-call | tf_op jit(solution)/shard_map/store_ahead/pallas_call | solution.py:309
  27.2 0.3 collective-permute-done.other
  27.5 7.0 %all-to-all-done = s32[64,1,128]{2,1,0:T(1,128)S(1)} async-done(((s32[64,1,128]{2,1,0:T(1,128)}), s32[64,1,128]{2,1,0:T(1,128)S(1)}, u32[]{:S(2)}, u32[]{:S(2)}) %all-to-all-start) | async-done | bytes 32800 | tf_op jit(solution)/shard_map/all_to_all | solution.py:328
  34.5 2.5 %gather_pages.1 = bf16[8,1040,128]{2,1,0:T(8,128)(2,1)} custom-call(s32[64,128]{1,0:T(8,128)S(1)} %bitcast.13, s32[64,128]{1,0:T(8,128)S(1)} %bitcast.14, bf16[256,2,16,128]{3,2,1,0:T(8,128)(2,1)S(1)} %store_ahead.1.store), custom_call_target="tpu_custom_call" | custom-call | tf_op jit(solution)/shard_map/gather_pages/pallas_call | solution.py:354
  37.0 4.4 %all-to-all-start.1 = ((bf16[8,1040,128]{2,1,0:T(8,128)(2,1)}), bf16[8,1040,128]{2,1,0:T(8,128)(2,1)}, u32[]{:S(2)}, u32[]{:S(2)}) async-start(bf16[8,1040,128]{2,1,0:T(8,128)(2,1)} %gather_pages.1), calls=%async_computation.1 | async-start | bytes 4259840 | tf_op jit(solution)/shard_map/all_to_all | solution.py:328
  41.4 0.0 copy-start.2
  41.4 0.0 copy-start
  41.4 0.0 copy-start.1
  41.4 30.8 %all-gather.queries = bf16[8,64,128]{2,1,0:T(8,128)(2,1)S(1)} all-gather(bf16[2,64,128]{2,1,0:T(8,128)(2,1)S(1)} %order.1), channel_id=2, replica_groups=mesh['zh'=4,'zm'=2,'zl'=2,'y'=4,'x'=4,'c'=2] {'zh'}, dimensions={0}, use_global_device_ids=true | all-gather | bytes 163840 | tf_op jit(solution)/shard_map/all_gather | solution.py:364
  72.2 0.0 all-to-all-done.1.source
  72.2 3.4 %partials.1 = bf16[576,128]{1,0:T(8,128)(2,1)} custom-call(bf16[8,1040,128]{2,1,0:T(8,128)(2,1)} %all-to-all-done.1.source, bf16[8,64,128]{2,1,0:T(8,128)(2,1)S(1)} %all-gather.queries), custom_call_target="tpu_custom_call" | custom-call | tf_op jit(solution)/shard_map/partials/pallas_call | solution.py:375
  75.6 6.7 %all-to-all-start.2 = ((bf16[8,72,128]{2,1,0:T(8,128)(2,1)}), bf16[8,72,128]{2,1,0:T(8,128)(2,1)S(1)}, u32[]{:S(2)}, u32[]{:S(2)}) async-start(bf16[8,72,128]{2,1,0:T(8,128)(2,1)} %bitcast.7), calls=%async_computation.2 | async-start | bytes 294912 | tf_op jit(solution)/shard_map/all_to_all | solution.py:328
  82.3 0.0 copy-done.2
  82.4 0.0 copy-done
  82.4 0.0 copy-done.1
  82.4 1.5 %resident.1 = (f32[64,128]{1,0:T(8,128)S(1)}, f32[64,128]{1,0:T(8,128)S(1)}, f32[64,128]{1,0:T(8,128)S(1)}) custom-call(s32[8,24]{1,0:T(8,128)S(1)} %copy-done, s32[8]{0:T(128)S(1)} %copy-done.1, bf16[64,128]{1,0:T(8,128)(2,1)S(1)} %bitcast.17, bf16[16,128]{1,0:T(8,128)(2,1)S(1)} %bitcast.19, bf16[16,128]{1,0:T(8,128)(2,1)S(1)} %bitcast.18, ...), custom_call_target="tpu_custom_call" | custom-call | flops 100000000 | bytes 3145728 | tf_op jit(solution)/shard_map/resident/pallas_call | solution.py:367
  83.9 12.7 %all-to-all-done.2 = bf16[8,72,128]{2,1,0:T(8,128)(2,1)S(1)} async-done(((bf16[8,72,128]{2,1,0:T(8,128)(2,1)}), bf16[8,72,128]{2,1,0:T(8,128)(2,1)S(1)}, u32[]{:S(2)}, u32[]{:S(2)}) %all-to-all-start.2) | async-done | bytes 147488 | tf_op jit(solution)/shard_map/all_to_all | solution.py:328
  96.6 2.0 %finish.1 = bf16[8,16,320]{2,1,0:T(8,128)(2,1)S(1)} custom-call(bf16[576,128]{1,0:T(8,128)(2,1)S(1)} %bitcast.12, f32[64,128]{1,0:T(8,128)S(1)} %get-tuple-element.16.sums, f32[64,128]{1,0:T(8,128)S(1)} %get-tuple-element.17.top, f32[64,128]{1,0:T(8,128)S(1)} %get-tuple-element.18.total, bf16[512,2560]{1,0:T(8,128)(2,1)} %weight_hbm.1), custom_call_target="tpu_custom_call" | custom-call | tf_op jit(solution)/shard_map/finish/pallas_call | solution.py:380
  98.6 15.3 %all_to_all.27.shares = bf16[8,16,320]{2,1,0:T(8,128)(2,1)S(1)} all-to-all(bf16[8,16,320]{2,1,0:T(8,128)(2,1)S(1)} %finish.1), channel_id=1, replica_groups=mesh['zh'=4,'zm'=2,'zl'=2,'y'=4,'x'=4,'c'=2] {'x','c'}, dimensions={0} | all-to-all | bytes 163840 | tf_op jit(solution)/shard_map/all_to_all | solution.py:328
  113.9 0.6 total.1
  (4 shorter events, 0.0 us)
Async XLA Ops:
  1.8 32.7 %all-to-all-start = ((s32[64,1,128]{2,1,0:T(1,128)}), s32[64,1,128]{2,1,0:T(1,128)S(1)}, u32[]{:S(2)}, u32[]{:S(2)}) async-start(s32[64,1,128]{2,1,0:T(1,128)} %bitcast.1), calls=%async_computation | async-start | bytes 65536 | tf_op jit(solution)/shard_map/all_to_all | solution.py:328
  21.8 5.7 %collective-permute-start = (bf16[64,128]{1,0:T(8,128)(2,1)S(1)}, bf16[64,128]{1,0:T(8,128)(2,1)S(1)}, u32[]{:S(2)}, u32[]{:S(2)}) collective-permute-start(bf16[64,128]{1,0:T(8,128)(2,1)S(1)} %bitcast.15), channel_id=1, source_target_pairs={{0,64},{64,0},{1,65},{65,1},{2,66},{66,2},{3,67},{67,3},{4,68},{68... | collective-permute-start | bytes 49160 | tf_op jit(solution)/shard_map/ppermute | solution.py:349
  37.0 35.2 %all-to-all-start.1 = ((bf16[8,1040,128]{2,1,0:T(8,128)(2,1)}), bf16[8,1040,128]{2,1,0:T(8,128)(2,1)}, u32[]{:S(2)}, u32[]{:S(2)}) async-start(bf16[8,1040,128]{2,1,0:T(8,128)(2,1)} %gather_pages.1), calls=%async_computation.1 | async-start | bytes 4259840 | tf_op jit(solution)/shard_map/all_to_all | solution.py:328
  41.4 40.9 %copy-start.2 = (bf16[8,2,2,1,128]{4,2,3,1,0:T(2,128)(2,1)S(1)}, bf16[8,2,2,1,128]{4,2,3,1,0:T(2,128)(2,1)}, u32[]{:S(2)}) copy-start(bf16[8,2,2,1,128]{4,2,3,1,0:T(2,128)(2,1)} %param.9) | copy-start | bytes 24580
  41.4 41.0 %copy-start = (s32[8,24]{1,0:T(8,128)S(1)}, s32[8,24]{1,0:T(8,128)}, u32[]{:S(2)}) copy-start(s32[8,24]{1,0:T(8,128)} %own.1) | copy-start | bytes 2308
  41.4 41.0 %copy-start.1 = (s32[8]{0:T(128)S(1)}, s32[8]{0:T(128)}, u32[]{:S(2)}) copy-start(s32[8]{0:T(128)} %length.1) | copy-start | bytes 100
  75.6 20.9 %all-to-all-start.2 = ((bf16[8,72,128]{2,1,0:T(8,128)(2,1)}), bf16[8,72,128]{2,1,0:T(8,128)(2,1)S(1)}, u32[]{:S(2)}, u32[]{:S(2)}) async-start(bf16[8,72,128]{2,1,0:T(8,128)(2,1)} %bitcast.7), calls=%async_computation.2 | async-start | bytes 294912 | tf_op jit(solution)/shard_map/all_to_all | solution.py:328

commit v7 on v6

--- a/solution.py
+++ b/solution.py
@@ -100,9 +100,10 @@
     req[...] = out.astype(I32)
 
 
-def order_kernel(place, own, other, out):
-    out[place[0]] = own[...]
-    out[1 - place[0]] = other[...]
+def stack_kernel(own, other, out):
+    half = own.shape[0]
+    out[pl.ds(0, half)] = own[...]
+    out[pl.ds(half, half)] = other[...]
 
 
 def prefetch_kernel(source, out, sems):
@@ -171,7 +172,7 @@
     total[...] = jnp.broadcast_to(count, (ROWS, HD))
 
 
-def partial_kernel(source, queries, out, pages, meta, meta_sem, sems):
+def partial_kernel(me, source, near, far, out, pages, meta, queries, meta_sem, sems):
     size = PAGE_ROWS // PARTS
     per = MEMBERS // PARTS
     meta_copy = pltpu.make_async_copy(source.at[:, pl.ds(2 * PAGE_ROWS, 16), :], meta, meta_sem)
@@ -185,6 +186,9 @@
             copy.start()
             group.append(copy)
         copies.append(group)
+    for r in range(MEMBERS):
+        half = near if r < MEMBERS // 2 else far
+        queries[me[0] ^ r] = half[r % (MEMBERS // 2)]
     meta_copy.wait()
     pick = iota((16, HD), 1) % 16 == iota((16, HD), 0) // STEPS
     stacks = []
@@ -319,6 +323,7 @@
 PARTIAL_SCRATCH = [
     pltpu.VMEM((SOURCES, CHUNK, HD), BF16),
     pltpu.VMEM((SOURCES, 16, HD), BF16),
+    pltpu.VMEM((MEMBERS, ROWS, HD), BF16),
     pltpu.SemaphoreType.DMA(()),
     pltpu.SemaphoreType.DMA((PARTS, 2)),
 ]
@@ -346,9 +351,10 @@
     )(hbm(prefix_pages), hbm(own_pages), hbm(fork_of), hbm(lengths))
     request = swap(request, NEAR + FAR)
     q = query.transpose(2, 0, 1, 3).reshape(ROWS, HD)
-    other = lax.ppermute(q, "zm", [(0, 1), (1, 0)])
-    place = lax.axis_index("zm").astype(I32).reshape(1)
-    near = call(order_kernel, shape((ZM, ROWS, HD), BF16), [SMEM, VMEM, VMEM], "order")(place, q, other)
+    near = q[None]
+    for axis, pairs in (("zm", [(0, 1), (1, 0)]), ("zh", [(0, 1), (1, 0), (2, 3), (3, 2)])):
+        other = lax.ppermute(near, axis, pairs)
+        near = call(stack_kernel, shape((2 * near.shape[0], ROWS, HD), BF16), [VMEM, VMEM], "stack")(near, other)
     request, near = lax.optimization_barrier((request, near))
     store = prefetch(store, "store_ahead")
     pages = call(
@@ -361,7 +367,8 @@
     )(request, request, vmem(store))
     near, pages = lax.optimization_barrier((near, pages))
     pages = swap(pages, NEAR)
-    queries = lax.all_gather(near, "zh").reshape(MEMBERS, ROWS, HD)
+    far = lax.ppermute(near, "zh", [(0, 2), (1, 3), (2, 0), (3, 1)])
+    me = (lax.axis_index("zh") * ZM + lax.axis_index("zm")).astype(I32).reshape(1)
     fresh_k = new_kv[:, :, 0, 0].reshape(B * STEPS, HD)
     fresh_v = new_kv[:, :, 1, 0].reshape(B * STEPS, HD)
     local = call(
@@ -372,9 +379,9 @@
         [pltpu.VMEM(((B - MIG) * NOWN * PAGE, HD), BF16)] * 2,
         pl.CostEstimate(flops=10**8, bytes_accessed=3 * 2**20, transcendentals=10**5),
     )(own_pages, lengths, q, fresh_k, fresh_v, store)
-    parts = call(partial_kernel, shape((MEMBERS * RES, HD), BF16), [HBM, VMEM], "partials", PARTIAL_SCRATCH)(
-        pages, queries
-    )
+    parts = call(
+        partial_kernel, shape((MEMBERS * RES, HD), BF16), [SMEM, HBM, VMEM, VMEM], "partials", PARTIAL_SCRATCH
+    )(me, pages, near, far)
     parts = swap(parts.reshape(MEMBERS, RES, HD), FAR).reshape(MEMBERS * RES, HD)
     width = o_weight.shape[1] // TPN
     shares = call(

time: 115 us -> 117 us (1.017)
  blocking collectives: 46.1 us -> 17.1 us
  starting transfers between devices: 34.1 us -> 51.2 us
  waiting for transfers between devices: 19.9 us -> 33.5 us
    all_gather x1 -> x0, blocking collectives: 30.8 us -> none  [shards(): queries = lax.all_gather(near, 'zh').reshape(MEMBERS, ROWS, HD)]
    ppermute x1 -> x3, waiting for transfers between devices: 0.29 us -> 21.6 us  [the longest x1 19.7 us: shards(): far = lax.ppermute(near, 'zh', [(0, 2), (1, 3), (2, 0), (3, 1)])]
    ppermute x1 -> x3, starting transfers between devices: 3.82 us -> 22.3 us  [the longest x1 11.4 us: shards(): far = lax.ppermute(near, 'zh', [(0, 2), (1, 3), (2, 0), (3, 1)])]
    all_to_all x3, waiting for transfers between devices: 19.6 us -> 11.9 us  [swap(): return lax.all_to_all(x, axes, split_axis=0, concat_axis=0, tiled=True)]
    all_to_all x1, blocking collectives: 15.3 us -> 17.1 us  [swap(): return lax.all_to_all(x, axes, split_axis=0, concat_axis=0, tiled=True)]
    all_to_all x3, starting transfers between devices: 30.3 us -> 28.9 us  [swap(): return lax.all_to_all(x, axes, split_axis=0, concat_axis=0, tiled=True)]
    pallas_call x2 -> x3, Pallas kernels: 3.45 us -> 3.47 us  [the longest x1 3.47 us: shards(): call(partial_kernel, shape((MEMBERS * RES, HD), BF16), [SMEM, HBM, VMEM,...]
  transfers between devices with their start and end apart: 4 -> 6, of which waited for: 3 -> 3; matrix products, arithmetic and copies ran while one was open for 1% -> 1% of each run, Pallas kernels for 3% -> 3%
where the time goes in v7:
time: 117 us; the launch traced here: 116 us
  starting transfers between devices  51.2 us (44%)
  waiting for transfers between devices  33.5 us (29%)
  blocking collectives  17.1 us (15%)
  Pallas kernels  13.5 us (12%)
    all_to_all x3, starting transfers between devices, swap(): return lax.all_to_all(x, axes, split_axis=0, concat_axis=0, tiled=True)  28.9 us
    ppermute x1, waiting for transfers between devices, shards(): far = lax.ppermute(near, 'zh', [(0, 2), (1, 3), (2, 0), (3, 1)])  19.7 us
    all_to_all x1, blocking collectives, swap(): return lax.all_to_all(x, axes, split_axis=0, concat_axis=0, tiled=True)  17.1 us
    all_to_all x3, waiting for transfers between devices, swap(): return lax.all_to_all(x, axes, split_axis=0, concat_axis=0, tiled=True)  11.9 us
    ppermute x1, starting transfers between devices, shards(): far = lax.ppermute(near, 'zh', [(0, 2), (1, 3), (2, 0), (3, 1)])  11.4 us
    ppermute x2, starting transfers between devices, shards(): other = lax.ppermute(near, axis, pairs)  10.8 us
    pallas_call x1, Pallas kernels, shards(): call(partial_kernel, shape((MEMBERS * RES, HD), BF16), [SMEM, HBM, VMEM,...  3.47 us
    pallas_call x1, Pallas kernels, shards(): call(gather_kernel, pltpu.HBM((SOURCES, CHUNK, HD), BF16), [SMEM, VMEM, V...  2.51 us
  transfers between devices with their start and end apart: 6, of which 3 were waited for; matrix products, arithmetic and copies ran while one was open for 1% of the time, Pallas kernels for 3%

profile of v7, /device:TPU:1, one launch (start us, length us, event | category | flops | bytes accessed | tf_op | source)
XLA Modules:
  0.0 116.3 jit_solution(17126214447369827990)
XLA Ops:
  0.0 1.8 %request.1 = s32[64,128]{1,0:T(8,128)} custom-call(s32[4,8]{1,0:T(4,128)} %prefix_hbm.1, s32[8,24]{1,0:T(8,128)} %own.1, s32[8]{0:T(128)} %fork_hbm.1, s32[8]{0:T(128)} %length.1), custom_call_target="tpu_custom_call" | custom-call | tf_op jit(solution)/shard_map/request/pallas_call | solution.py:339
  1.8 19.3 %all-to-all-start = ((s32[64,1,128]{2,1,0:T(1,128)}), s32[64,1,128]{2,1,0:T(1,128)S(1)}, u32[]{:S(2)}, u32[]{:S(2)}) async-start(s32[64,1,128]{2,1,0:T(1,128)} %bitcast.2), calls=%async_computation | async-start | bytes 65536 | tf_op jit(solution)/shard_map/all_to_all | solution.py:333
  21.1 0.7 copy.14
  21.8 3.8 %collective-permute-start = (bf16[1,64,128]{2,1,0:T(8,128)(2,1)S(1)}, bf16[1,64,128]{2,1,0:T(8,128)(2,1)S(1)}, u32[]{:S(2)}, u32[]{:S(2)}) collective-permute-start(bf16[1,64,128]{2,1,0:T(8,128)(2,1)S(1)} %bitcast.16), channel_id=1, source_target_pairs={{0,64},{64,0},{1,65},{65,1},{2,66},{66,2},{3,67},{67,3},{4,68},{68... | collective-permute-start | bytes 49160 | tf_op jit(solution)/shard_map/ppermute | solution.py:356
  25.7 1.9 %collective-permute-done.other = bf16[1,64,128]{2,1,0:T(8,128)(2,1)S(1)} collective-permute-done((bf16[1,64,128]{2,1,0:T(8,128)(2,1)S(1)}, bf16[1,64,128]{2,1,0:T(8,128)(2,1)S(1)}, u32[]{:S(2)}, u32[]{:S(2)}) %collective-permute-start) | collective-permute-done | bytes 16416 | tf_op jit(solution)/shard_map/ppermute | solution.py:356
  27.5 7.0 %collective-permute-start.1 = (bf16[2,64,128]{2,1,0:T(8,128)(2,1)S(1)}, bf16[2,64,128]{2,1,0:T(8,128)(2,1)S(1)}, u32[]{:S(2)}, u32[]{:S(2)}) collective-permute-start(bf16[2,64,128]{2,1,0:T(8,128)(2,1)S(1)} %stack.2.own), channel_id=1, source_target_pairs={{0,128},{128,0},{256,384},{384,256},{1,129},{129,1},{257,385},{385... | collective-permute-start | bytes 98312 | tf_op jit(solution)/shard_map/ppermute | solution.py:356
  34.6 1.6 %store_ahead.1.store = bf16[256,2,16,128]{3,2,1,0:T(8,128)(2,1)S(1)} custom-call(bf16[256,2,16,128]{3,2,1,0:T(8,128)(2,1)} %bitcast.21), custom_call_target="tpu_custom_call" | custom-call | tf_op jit(solution)/shard_map/store_ahead/pallas_call | solution.py:313
  36.1 0.0 collective-permute-done.1.other
  36.2 0.0 all-to-all-done
  36.2 2.5 %gather_pages.1 = bf16[8,1040,128]{2,1,0:T(8,128)(2,1)} custom-call(s32[64,128]{1,0:T(8,128)S(1)} %bitcast.14, s32[64,128]{1,0:T(8,128)S(1)} %bitcast.15, bf16[256,2,16,128]{3,2,1,0:T(8,128)(2,1)S(1)} %store_ahead.1.store), custom_call_target="tpu_custom_call" | custom-call | tf_op jit(solution)/shard_map/gather_pages/pallas_call | solution.py:360
  38.7 5.0 %all-to-all-start.1 = ((bf16[8,1040,128]{2,1,0:T(8,128)(2,1)}), bf16[8,1040,128]{2,1,0:T(8,128)(2,1)}, u32[]{:S(2)}, u32[]{:S(2)}) async-start(bf16[8,1040,128]{2,1,0:T(8,128)(2,1)} %gather_pages.1), calls=%async_computation.1 | async-start | bytes 4259840 | tf_op jit(solution)/shard_map/all_to_all | solution.py:333
  43.7 0.0 copy-start
  43.7 0.0 copy-start.1
  43.7 11.4 %collective-permute-start.2 = (bf16[4,64,128]{2,1,0:T(8,128)(2,1)S(1)}, bf16[4,64,128]{2,1,0:T(8,128)(2,1)S(1)}, u32[]{:S(2)}, u32[]{:S(2)}) collective-permute-start(bf16[4,64,128]{2,1,0:T(8,128)(2,1)S(1)} %stack.3.near), channel_id=1, source_target_pairs={{0,256},{128,384},{256,0},{384,128},{1,257},{129,385},{257,1},{385... | collective-permute-start | bytes 196616 | tf_op jit(solution)/shard_map/ppermute | solution.py:370
  55.2 19.7 %collective-permute-done.2.far = bf16[4,64,128]{2,1,0:T(8,128)(2,1)S(1)} collective-permute-done((bf16[4,64,128]{2,1,0:T(8,128)(2,1)S(1)}, bf16[4,64,128]{2,1,0:T(8,128)(2,1)S(1)}, u32[]{:S(2)}, u32[]{:S(2)}) %collective-permute-start.2) | collective-permute-done | bytes 65568 | tf_op jit(solution)/shard_map/ppermute | solution.py:370
  74.8 0.0 all-to-all-done.1.source
  74.8 3.5 %partials.1 = bf16[576,128]{1,0:T(8,128)(2,1)} custom-call(s32[1]{0:T(128)} %bitcast.me, bf16[8,1040,128]{2,1,0:T(8,128)(2,1)} %all-to-all-done.1.source, bf16[4,64,128]{2,1,0:T(8,128)(2,1)S(1)} %stack.3.near, bf16[4,64,128]{2,1,0:T(8,128)(2,1)S(1)} %collective-permute-done.2.far), custom_call_target="tpu_custom_call" | custom-call | tf_op jit(solution)/shard_map/partials/pallas_call | solution.py:382
  78.3 4.7 %all-to-all-start.2 = ((bf16[8,72,128]{2,1,0:T(8,128)(2,1)}), bf16[8,72,128]{2,1,0:T(8,128)(2,1)S(1)}, u32[]{:S(2)}, u32[]{:S(2)}) async-start(bf16[8,72,128]{2,1,0:T(8,128)(2,1)} %bitcast.7), calls=%async_computation.2 | async-start | bytes 294912 | tf_op jit(solution)/shard_map/all_to_all | solution.py:333
  83.0 0.0 copy-done.2
  83.1 1.5 %resident.1 = (f32[64,128]{1,0:T(8,128)S(1)}, f32[64,128]{1,0:T(8,128)S(1)}, f32[64,128]{1,0:T(8,128)S(1)}) custom-call(s32[8,24]{1,0:T(8,128)S(1)} %copy-done, s32[8]{0:T(128)S(1)} %copy-done.1, bf16[64,128]{1,0:T(8,128)(2,1)S(1)} %bitcast.18, bf16[16,128]{1,0:T(8,128)(2,1)S(1)} %bitcast.20, bf16[16,128]{1,0:T(8,128)(2,1)S(1)} %bitcast.19, ...), custom_call_target="tpu_custom_call" | custom-call | flops 100000000 | bytes 3145728 | tf_op jit(solution)/shard_map/resident/pallas_call | solution.py:374
  84.6 11.9 %all-to-all-done.2 = bf16[8,72,128]{2,1,0:T(8,128)(2,1)S(1)} async-done(((bf16[8,72,128]{2,1,0:T(8,128)(2,1)}), bf16[8,72,128]{2,1,0:T(8,128)(2,1)S(1)}, u32[]{:S(2)}, u32[]{:S(2)}) %all-to-all-start.2) | async-done | bytes 147488 | tf_op jit(solution)/shard_map/all_to_all | solution.py:333
  96.5 2.0 %finish.1 = bf16[8,16,320]{2,1,0:T(8,128)(2,1)S(1)} custom-call(bf16[576,128]{1,0:T(8,128)(2,1)S(1)} %bitcast.13, f32[64,128]{1,0:T(8,128)S(1)} %get-tuple-element.16.sums, f32[64,128]{1,0:T(8,128)S(1)} %get-tuple-element.17.top, f32[64,128]{1,0:T(8,128)S(1)} %get-tuple-element.18.total, bf16[512,2560]{1,0:T(8,128)(2,1)} %weight_hbm.1), custom_call_target="tpu_custom_call" | custom-call | tf_op jit(solution)/shard_map/finish/pallas_call | solution.py:387
  98.5 17.1 %all_to_all.27.shares = bf16[8,16,320]{2,1,0:T(8,128)(2,1)S(1)} all-to-all(bf16[8,16,320]{2,1,0:T(8,128)(2,1)S(1)} %finish.1), channel_id=1, replica_groups=mesh['zh'=4,'zm'=2,'zl'=2,'y'=4,'x'=4,'c'=2] {'x','c'}, dimensions={0} | all-to-all | bytes 163840 | tf_op jit(solution)/shard_map/all_to_all | solution.py:333
  115.7 0.6 total.1
  (8 shorter events, 0.0 us)
Async XLA Ops:
  1.8 34.4 %all-to-all-start = ((s32[64,1,128]{2,1,0:T(1,128)}), s32[64,1,128]{2,1,0:T(1,128)S(1)}, u32[]{:S(2)}, u32[]{:S(2)}) async-start(s32[64,1,128]{2,1,0:T(1,128)} %bitcast.2), calls=%async_computation | async-start | bytes 65536 | tf_op jit(solution)/shard_map/all_to_all | solution.py:333
  21.8 5.7 %collective-permute-start = (bf16[1,64,128]{2,1,0:T(8,128)(2,1)S(1)}, bf16[1,64,128]{2,1,0:T(8,128)(2,1)S(1)}, u32[]{:S(2)}, u32[]{:S(2)}) collective-permute-start(bf16[1,64,128]{2,1,0:T(8,128)(2,1)S(1)} %bitcast.16), channel_id=1, source_target_pairs={{0,64},{64,0},{1,65},{65,1},{2,66},{66,2},{3,67},{67,3},{4,68},{68... | collective-permute-start | bytes 49160 | tf_op jit(solution)/shard_map/ppermute | solution.py:356
  27.5 8.6 %collective-permute-start.1 = (bf16[2,64,128]{2,1,0:T(8,128)(2,1)S(1)}, bf16[2,64,128]{2,1,0:T(8,128)(2,1)S(1)}, u32[]{:S(2)}, u32[]{:S(2)}) collective-permute-start(bf16[2,64,128]{2,1,0:T(8,128)(2,1)S(1)} %stack.2.own), channel_id=1, source_target_pairs={{0,128},{128,0},{256,384},{384,256},{1,129},{129,1},{257,385},{385... | collective-permute-start | bytes 98312 | tf_op jit(solution)/shard_map/ppermute | solution.py:356
  38.7 36.1 %all-to-all-start.1 = ((bf16[8,1040,128]{2,1,0:T(8,128)(2,1)}), bf16[8,1040,128]{2,1,0:T(8,128)(2,1)}, u32[]{:S(2)}, u32[]{:S(2)}) async-start(bf16[8,1040,128]{2,1,0:T(8,128)(2,1)} %gather_pages.1), calls=%async_computation.1 | async-start | bytes 4259840 | tf_op jit(solution)/shard_map/all_to_all | solution.py:333
  43.7 39.3 %copy-start.2 = (bf16[8,2,2,1,128]{4,2,3,1,0:T(2,128)(2,1)S(1)}, bf16[8,2,2,1,128]{4,2,3,1,0:T(2,128)(2,1)}, u32[]{:S(2)}) copy-start(bf16[8,2,2,1,128]{4,2,3,1,0:T(2,128)(2,1)} %param.9) | copy-start | bytes 24580
  43.7 39.4 %copy-start = (s32[8,24]{1,0:T(8,128)S(1)}, s32[8,24]{1,0:T(8,128)}, u32[]{:S(2)}) copy-start(s32[8,24]{1,0:T(8,128)} %own.1) | copy-start | bytes 2308
  43.7 39.4 %copy-start.1 = (s32[8]{0:T(128)S(1)}, s32[8]{0:T(128)}, u32[]{:S(2)}) copy-start(s32[8]{0:T(128)} %length.1) | copy-start | bytes 100
  43.7 31.1 %collective-permute-start.2 = (bf16[4,64,128]{2,1,0:T(8,128)(2,1)S(1)}, bf16[4,64,128]{2,1,0:T(8,128)(2,1)S(1)}, u32[]{:S(2)}, u32[]{:S(2)}) collective-permute-start(bf16[4,64,128]{2,1,0:T(8,128)(2,1)S(1)} %stack.3.near), channel_id=1, source_target_pairs={{0,256},{128,384},{256,0},{384,128},{1,257},{129,385},{257,1},{385... | collective-permute-start | bytes 196616 | tf_op jit(solution)/shard_map/ppermute | solution.py:370
  78.3 18.2 %all-to-all-start.2 = ((bf16[8,72,128]{2,1,0:T(8,128)(2,1)}), bf16[8,72,128]{2,1,0:T(8,128)(2,1)S(1)}, u32[]{:S(2)}, u32[]{:S(2)}) async-start(bf16[8,72,128]{2,1,0:T(8,128)(2,1)} %bitcast.7), calls=%async_computation.2 | async-start | bytes 294912 | tf_op jit(solution)/shard_map/all_to_all | solution.py:333

commit v8 on v6

--- a/solution.py
+++ b/solution.py
@@ -28,7 +28,7 @@
 SCALE = 1.0 / math.sqrt(HD)
 ZN, YN, XN, CN = 16, 4, 4, 2
 ZH, ZM, ZL = 4, 2, 2
-PARTS = 2
+PARTS = 1
 POOL_AXES = ("zh", "zm", "zl", "y")
 NEAR = ("zl", "y")
 FAR = ("zh", "zm")
@@ -39,7 +39,9 @@
 PREFIX_IDS = ROOTS * NPRE
 KEYS = SLOTS * PAGE
 PAGE_ROWS = MEMBERS * KEYS
-CHUNK = 2 * PAGE_ROWS + 16
+QROWS = STEPS * GROUP
+TAIL = MEMBERS * QROWS + 16
+CHUNK = 2 * PAGE_ROWS + TAIL
 RES = ROWS + 8
 
 VMEM = pl.BlockSpec(memory_space=pltpu.VMEM)
@@ -58,7 +60,7 @@
     return lax.dot_general(a, b, dims, preferred_element_type=F32)
 
 
-def request_kernel(prefix_hbm, own_hbm, fork_hbm, length_hbm, req, prefix, own, fork, length, sems):
+def request_kernel(prefix_hbm, own_hbm, fork_hbm, length_hbm, query, req, q, prefix, own, fork, length, sems):
     pairs = ((prefix_hbm, prefix), (own_hbm, own), (fork_hbm, fork), (length_hbm, length))
     copies = [pltpu.make_async_copy(a, b, sems.at[n]) for n, (a, b) in enumerate(pairs)]
     for copy in copies:
@@ -97,12 +99,14 @@
         chosen = jnp.where(member & (rank == float(s)), 1.0, 0.0).astype(BF16)
         parts = [table if k == s else jnp.zeros((16, HD), BF16) for k in range(HD // 16)]
         out = out + dot(chosen, jnp.concatenate(parts, 0), NT)
-    req[...] = out.astype(I32)
-
-
-def order_kernel(place, own, other, out):
-    out[place[0]] = own[...]
-    out[1 - place[0]] = other[...]
+    for b in range(B):
+        rows = jnp.concatenate([query[b, t].astype(F32) for t in range(STEPS)], 0)
+        for m in range(MEMBERS):
+            d = b * MEMBERS + m
+            req[d] = jnp.concatenate([rows, jnp.broadcast_to(out[d : d + 1], (8, HD))], 0).astype(BF16)
+    for b in range(0, B, 2):
+        rows = [query[n, t].astype(F32) for n in (b, b + 1) for t in range(STEPS)]
+        q[pl.ds(b * QROWS, 2 * QROWS), :] = jnp.concatenate(rows, 0).astype(BF16)
 
 
 def prefetch_kernel(source, out, sems):
@@ -117,7 +121,21 @@
         copy.wait()
 
 
-def gather_kernel(places, req, store, out, stage, sems):
+def gather_kernel(req, store, out, stage, wanted, places, place_sem, sems):
+    row = iota((MEMBERS, HD), 0)
+    tails = []
+    for c in range(SOURCES):
+        tiles = [req[c * MEMBERS + n].astype(F32) for n in range(MEMBERS)]
+        asked = tiles[0][8:16]
+        for n in range(1, MEMBERS):
+            asked = jnp.where(row == n, tiles[n][8:16], asked)
+        wanted[pl.ds(c * MEMBERS, MEMBERS), :] = asked.astype(I32)
+        tails.append([tile[0:8] for tile in tiles] + [asked, jnp.zeros((16 - MEMBERS, HD), F32)])
+    copy = pltpu.make_async_copy(wanted, places, place_sem)
+    copy.start()
+    for c in range(SOURCES):
+        stage[c, pl.ds(2 * PAGE_ROWS, TAIL), :] = jnp.concatenate(tails[c], 0).astype(BF16)
+    copy.wait()
     copies = []
     for c in range(SOURCES):
         for n in range(MEMBERS):
@@ -126,9 +144,6 @@
                 start = n * KEYS + s * PAGE
                 stage[c, pl.ds(start, PAGE), :] = store[at, 0]
                 stage[c, pl.ds(PAGE_ROWS + start, PAGE), :] = store[at, 1]
-        rows = req[pl.ds(c * MEMBERS, MEMBERS), :].astype(F32)
-        rows = jnp.concatenate([rows, jnp.zeros((16 - MEMBERS, HD), F32)], 0)
-        stage[c, pl.ds(2 * PAGE_ROWS, 16), :] = rows.astype(BF16)
         copy = pltpu.make_async_copy(stage.at[c], out.at[c], sems.at[c])
         copy.start()
         copies.append(copy)
@@ -146,8 +161,8 @@
             keys[pl.ds(start, PAGE), :] = store[at, 0]
             values[pl.ds(start, PAGE), :] = store[at, 1]
     rows = q[...]
-    branch_of = (iota((ROWS, 1), 0) % 16) // STEPS
-    step_of = iota((ROWS, 1), 0) % STEPS
+    branch_of = iota((ROWS, 1), 0) // QROWS
+    step_of = iota((ROWS, 1), 0) // GROUP % STEPS
     lane16 = iota((ROWS, 16), 1)
     score = dot(rows, fresh_k[...], NT) * SCALE
     ok = (lane16 // STEPS == branch_of) & (lane16 % STEPS <= step_of)
@@ -171,27 +186,17 @@
     total[...] = jnp.broadcast_to(count, (ROWS, HD))
 
 
-def partial_kernel(source, queries, out, pages, meta, meta_sem, sems):
-    size = PAGE_ROWS // PARTS
+def partial_kernel(pages, out):
     per = MEMBERS // PARTS
-    meta_copy = pltpu.make_async_copy(source.at[:, pl.ds(2 * PAGE_ROWS, 16), :], meta, meta_sem)
-    meta_copy.start()
-    copies = []
-    for part in range(PARTS):
-        group = []
-        for kv in range(2):
-            rows = pl.ds(kv * PAGE_ROWS + part * size, size)
-            copy = pltpu.make_async_copy(source.at[:, rows, :], pages.at[:, rows, :], sems.at[part, kv])
-            copy.start()
-            group.append(copy)
-        copies.append(group)
-    meta_copy.wait()
-    pick = iota((16, HD), 1) % 16 == iota((16, HD), 0) // STEPS
+    pick = iota((B, HD), 1) % 16 == iota((B, HD), 0)
     stacks = []
+    asking = []
     for k in range(SOURCES):
-        tile = meta[k].astype(F32)
-        rows = [jnp.where(pick, jnp.broadcast_to(tile[n : n + 1], (16, HD)), 0.0).astype(BF16) for n in range(MEMBERS)]
-        stacks.append(jnp.concatenate(rows, 0))
+        tail = pages[k, pl.ds(2 * PAGE_ROWS, TAIL), :].astype(F32)
+        asking.append(tail)
+        tile = tail[MEMBERS * QROWS : MEMBERS * QROWS + MEMBERS]
+        rows = [jnp.where(pick, jnp.broadcast_to(tile[n : n + 1], (B, HD)), 0.0) for n in range(MEMBERS)]
+        stacks.append(jnp.concatenate(rows, 0).astype(BF16))
     pairs = [jnp.concatenate(stacks[k : k + 2], 1) for k in range(0, SOURCES, 2)]
     shape = (2 * HD, 2 * KEYS)
     expand = iota(shape, 0) // HD * KEYS + (iota(shape, 0) % HD) // 16 * PAGE == iota(shape, 1) // PAGE * PAGE
@@ -203,18 +208,17 @@
     row = iota((8, HD), 0)
     for part in range(PARTS):
         members = range(part * per, (part + 1) * per)
-        for copy in copies[part]:
-            copy.wait()
         scores = []
         for z in members:
             keys = jnp.concatenate([pages[k, pl.ds(z * KEYS, KEYS), :] for k in range(SOURCES)], 0)
-            scores.append(dot(queries[z], keys, NT))
+            queries = jnp.concatenate([tail[z * QROWS : (z + 1) * QROWS] for tail in asking], 0).astype(BF16)
+            scores.append(dot(queries, keys, NT))
         stats = jnp.zeros((ROWS, HD), F32)
         weights = []
         for n, z in enumerate(members):
-            rows = range(z * 16, SOURCES // 2 * MEMBERS * 16, MEMBERS * 16)
-            bias = jnp.concatenate([mask[r : r + 16] for r in rows], 1)
-            bias = jnp.concatenate([bias] * GROUP, 0)
+            rows = range(z * B, SOURCES // 2 * MEMBERS * B, MEMBERS * B)
+            bias = jnp.concatenate([mask[r : r + B] for r in rows], 1)
+            bias = jnp.concatenate([jnp.broadcast_to(bias[b : b + 1], (QROWS, bias.shape[1])) for b in range(B)], 0)
             score = jnp.where(bias < 0.0, NEG, scores[n] * SCALE)
             best = jnp.max(score, 1, keepdims=True).astype(BF16).astype(F32)
             weight = jnp.where(bias < 0.0, 0.0, jnp.exp(score - best)).astype(BF16)
@@ -234,7 +238,7 @@
         out[pl.ds(part * per * RES, per * RES), :] = jnp.concatenate(rows, 0).astype(BF16)
 
 
-def finish_kernel(parts, sums, top, total, weight_hbm, out, weight, sems):
+def finish_kernel(parts, sums, top, total, weight_hbm, out, weight, rows, sems):
     copies = [
         pltpu.make_async_copy(weight_hbm.at[pl.ds(g * HD, HD), :], weight.at[pl.ds(g * HD, HD), :], sems.at[g])
         for g in range(GROUP)
@@ -264,11 +268,12 @@
     numerator = own_factor * sums[...]
     for z in range(MEMBERS):
         numerator = numerator + factor[:, z : z + 1] * received[z][0:ROWS]
-    attended = (numerator / denominator).astype(BF16)
+    rows[...] = numerator / denominator
     result = jnp.zeros((16, weight.shape[1]), F32)
     for g in range(GROUP):
         copies[g].wait()
-        result = result + dot(attended[16 * g : 16 * (g + 1)], weight[pl.ds(g * HD, HD), :])
+        attended = rows[pl.ds(g, 16, stride=GROUP), :].astype(BF16)
+        result = result + dot(attended, weight[pl.ds(g * HD, HD), :])
     result = result.astype(BF16).astype(F32)
     width = out.shape[2]
     for k in range(TPN):
@@ -316,14 +321,6 @@
     )(hbm(x))
 
 
-PARTIAL_SCRATCH = [
-    pltpu.VMEM((SOURCES, CHUNK, HD), BF16),
-    pltpu.VMEM((SOURCES, 16, HD), BF16),
-    pltpu.SemaphoreType.DMA(()),
-    pltpu.SemaphoreType.DMA((PARTS, 2)),
-]
-
-
 def swap(x, axes):
     return lax.all_to_all(x, axes, split_axis=0, concat_axis=0, tiled=True)
 
@@ -331,10 +328,10 @@
 def shards(query, new_kv, kv_store, prefix_pages, fork_of, own_pages, lengths, o_weight):
     shape = jax.ShapeDtypeStruct
     store = kv_store.reshape(P_DEV, 2, PAGE, HD)
-    request = call(
+    request, q = call(
         request_kernel,
-        shape((POOL, HD), I32),
-        [HBM] * 4,
+        [shape((POOL, 16, HD), BF16), shape((ROWS, HD), BF16)],
+        [HBM] * 4 + [VMEM],
         "request",
         [
             pltpu.SMEM(prefix_pages.shape, I32),
@@ -343,25 +340,24 @@
             pltpu.SMEM(lengths.shape, I32),
             pltpu.SemaphoreType.DMA((4,)),
         ],
-    )(hbm(prefix_pages), hbm(own_pages), hbm(fork_of), hbm(lengths))
+    )(hbm(prefix_pages), hbm(own_pages), hbm(fork_of), hbm(lengths), query)
     request = swap(request, NEAR + FAR)
-    q = query.transpose(2, 0, 1, 3).reshape(ROWS, HD)
-    other = lax.ppermute(q, "zm", [(0, 1), (1, 0)])
-    place = lax.axis_index("zm").astype(I32).reshape(1)
-    near = call(order_kernel, shape((ZM, ROWS, HD), BF16), [SMEM, VMEM, VMEM], "order")(place, q, other)
-    request, near = lax.optimization_barrier((request, near))
     store = prefetch(store, "store_ahead")
     pages = call(
         gather_kernel,
         pltpu.HBM((SOURCES, CHUNK, HD), BF16),
-        [SMEM, VMEM, VMEM],
+        [VMEM, VMEM],
         "gather_pages",
-        [pltpu.VMEM((SOURCES, CHUNK, HD), BF16), pltpu.SemaphoreType.DMA((SOURCES,))],
+        [
+            pltpu.VMEM((SOURCES, CHUNK, HD), BF16),
+            pltpu.VMEM((POOL, HD), I32),
+            pltpu.SMEM((POOL, HD), I32),
+            pltpu.SemaphoreType.DMA(()),
+            pltpu.SemaphoreType.DMA((SOURCES,)),
+        ],
         out_specs=HBM,
-    )(request, request, vmem(store))
-    near, pages = lax.optimization_barrier((near, pages))
+    )(request, vmem(store))
     pages = swap(pages, NEAR)
-    queries = lax.all_gather(near, "zh").reshape(MEMBERS, ROWS, HD)
     fresh_k = new_kv[:, :, 0, 0].reshape(B * STEPS, HD)
     fresh_v = new_kv[:, :, 1, 0].reshape(B * STEPS, HD)
     local = call(
@@ -372,9 +368,7 @@
         [pltpu.VMEM(((B - MIG) * NOWN * PAGE, HD), BF16)] * 2,
         pl.CostEstimate(flops=10**8, bytes_accessed=3 * 2**20, transcendentals=10**5),
     )(own_pages, lengths, q, fresh_k, fresh_v, store)
-    parts = call(partial_kernel, shape((MEMBERS * RES, HD), BF16), [HBM, VMEM], "partials", PARTIAL_SCRATCH)(
-        pages, queries
-    )
+    parts = call(partial_kernel, shape((MEMBERS * RES, HD), BF16), [VMEM], "partials")(vmem(pages))
     parts = swap(parts.reshape(MEMBERS, RES, HD), FAR).reshape(MEMBERS * RES, HD)
     width = o_weight.shape[1] // TPN
     shares = call(
@@ -382,7 +376,7 @@
         shape((TPN, 16, width), BF16),
         [VMEM] * 4 + [HBM],
         "finish",
-        [pltpu.VMEM(o_weight.shape, BF16), pltpu.SemaphoreType.DMA((GROUP,))],
+        [pltpu.VMEM(o_weight.shape, BF16), pltpu.VMEM((ROWS, HD), F32), pltpu.SemaphoreType.DMA((GROUP,))],
     )(parts, *local, hbm(o_weight))
     shares = swap(shares, ("x", "c"))
     return call(total_kernel, shape((B, STEPS, width), BF16), [VMEM], "total")(shares)

time: 115 us -> 111 us (0.965)
  waiting for transfers between devices: 19.9 us -> 30.3 us
  starting transfers between devices: 34.1 us -> 25.1 us
  blocking collectives: 46.1 us -> 42.6 us
  Pallas kernels: 13.4 us -> 11.9 us
    all_gather x1 -> x0, blocking collectives: 30.8 us -> none  [shards(): queries = lax.all_gather(near, 'zh').reshape(MEMBERS, ROWS, HD)]
    all_to_all x1 -> x2, blocking collectives: 15.3 us -> 42.6 us  [swap(): return lax.all_to_all(x, axes, split_axis=0, concat_axis=0, tiled=True)]
    all_to_all x3 -> x2, waiting for transfers between devices: 19.6 us -> 30.3 us  [swap(): return lax.all_to_all(x, axes, split_axis=0, concat_axis=0, tiled=True)]
    all_to_all x3 -> x2, starting transfers between devices: 30.3 us -> 25.1 us  [swap(): return lax.all_to_all(x, axes, split_axis=0, concat_axis=0, tiled=True)]
    ppermute x1 -> x0, starting transfers between devices: 3.82 us -> none  [shards(): other = lax.ppermute(q, 'zm', [(0, 1), (1, 0)])]
    pallas_call x4 -> x3, Pallas kernels: 7.73 us -> 6.2 us  [the longest x1 2.59 us: shards(): call(gather_kernel, pltpu.HBM((SOURCES, CHUNK, HD), BF16), [VMEM, VMEM],...]
  transfers between devices with their start and end apart: 4 -> 2, of which waited for: 3 -> 2; matrix products, arithmetic and copies ran while one was open for 1% -> 0% of each run, Pallas kernels for 3% -> 3%
where the time goes in v8:
time: 111 us
  blocking collectives  42.6 us (38%)
  waiting for transfers between devices  30.3 us (27%)
  starting transfers between devices  25.1 us (23%)
  Pallas kernels  11.9 us (11%)
    all_to_all x2, blocking collectives, swap(): return lax.all_to_all(x, axes, split_axis=0, concat_axis=0, tiled=True)  42.6 us
    all_to_all x2, waiting for transfers between devices, swap(): return lax.all_to_all(x, axes, split_axis=0, concat_axis=0, tiled=True)  30.3 us
    all_to_all x2, starting transfers between devices, swap(): return lax.all_to_all(x, axes, split_axis=0, concat_axis=0, tiled=True)  25.1 us
    pallas_call x1, Pallas kernels, shards(): call(gather_kernel, pltpu.HBM((SOURCES, CHUNK, HD), BF16), [VMEM, VMEM],...  2.59 us
  transfers between devices with their start and end apart: 2, of which 2 were waited for; matrix products, arithmetic and copies ran while one was open for 0% of the time, Pallas kernels for 3%

profile of v8, /device:TPU:1, one launch (start us, length us, event | category | flops | bytes accessed | tf_op | source)
XLA Modules:
  0.0 110.7 jit_solution(7188264006848339090)
XLA Ops:
  0.0 0.0 copy-start.1
  0.0 0.7 copy-done.1
  0.7 1.9 %request.1 = (bf16[64,16,128]{2,1,0:T(8,128)(2,1)}, bf16[64,128]{1,0:T(8,128)(2,1)S(1)}) custom-call(s32[4,8]{1,0:T(4,128)} %prefix_hbm.1, s32[8,24]{1,0:T(8,128)} %own.1, s32[8]{0:T(128)} %fork_hbm.1, s32[8]{0:T(128)} %length.1, bf16[8,2,4,128]{3,2,1,0:T(4,128)(2,1)S(1)} %copy-done.1), custom_call_target="tpu_custom_call" | custom-call | tf_op jit(solution)/shard_map/request/pallas_call | solution.py:331
  2.6 19.3 %all-to-all-start = ((bf16[64,16,128]{2,1,0:T(8,128)(2,1)}), bf16[64,16,128]{2,1,0:T(8,128)(2,1)S(1)}, u32[]{:S(2)}, u32[]{:S(2)}) async-start(bf16[64,16,128]{2,1,0:T(8,128)(2,1)} %get-tuple-element.10), calls=%async_computation | async-start | bytes 524288 | tf_op jit(solution)/shard_map/all_to_all | solution.py:325
  21.9 1.6 %store_ahead.1.store = bf16[256,2,16,128]{3,2,1,0:T(8,128)(2,1)S(1)} custom-call(bf16[256,2,16,128]{3,2,1,0:T(8,128)(2,1)} %bitcast.8), custom_call_target="tpu_custom_call" | custom-call | tf_op jit(solution)/shard_map/store_ahead/pallas_call | solution.py:314
  23.5 18.8 %all-to-all-done.req = bf16[64,16,128]{2,1,0:T(8,128)(2,1)S(1)} async-done(((bf16[64,16,128]{2,1,0:T(8,128)(2,1)}), bf16[64,16,128]{2,1,0:T(8,128)(2,1)S(1)}, u32[]{:S(2)}, u32[]{:S(2)}) %all-to-all-start) | async-done | bytes 262176 | tf_op jit(solution)/shard_map/all_to_all | solution.py:325
  42.3 2.6 %gather_pages.1 = bf16[8,1104,128]{2,1,0:T(8,128)(2,1)} custom-call(bf16[64,16,128]{2,1,0:T(8,128)(2,1)S(1)} %all-to-all-done.req, bf16[256,2,16,128]{3,2,1,0:T(8,128)(2,1)S(1)} %store_ahead.1.store), custom_call_target="tpu_custom_call" | custom-call | tf_op jit(solution)/shard_map/gather_pages/pallas_call | solution.py:346
  44.9 29.4 %all_to_all.20.pages = bf16[8,1104,128]{2,1,0:T(8,128)(2,1)S(1)} all-to-all(bf16[8,1104,128]{2,1,0:T(8,128)(2,1)} %gather_pages.1), channel_id=1, replica_groups=mesh['zh'=4,'zm'=2,'zl'=2,'y'=4,'x'=4,'c'=2] {'zl','y'}, dimensions={0} | all-to-all | bytes 4521984 | tf_op jit(solution)/shard_map/all_to_all | solution.py:325
  74.3 0.0 copy-start.3
  74.3 0.0 copy-start
  74.3 0.0 copy-start.2
  74.3 1.7 %partials.1 = bf16[576,128]{1,0:T(8,128)(2,1)} custom-call(bf16[8,1104,128]{2,1,0:T(8,128)(2,1)S(1)} %all_to_all.20.pages), custom_call_target="tpu_custom_call" | custom-call | tf_op jit(solution)/shard_map/partials/pallas_call | solution.py:371
  76.0 5.8 %all-to-all-start.2 = ((bf16[8,72,128]{2,1,0:T(8,128)(2,1)}), bf16[8,72,128]{2,1,0:T(8,128)(2,1)S(1)}, u32[]{:S(2)}, u32[]{:S(2)}) async-start(bf16[8,72,128]{2,1,0:T(8,128)(2,1)} %bitcast.1), calls=%async_computation.2 | async-start | bytes 294912 | tf_op jit(solution)/shard_map/all_to_all | solution.py:325
  81.8 0.0 copy-done.3
  81.9 0.0 copy-done
  81.9 0.0 copy-done.2
  81.9 1.5 %resident.1 = (f32[64,128]{1,0:T(8,128)S(1)}, f32[64,128]{1,0:T(8,128)S(1)}, f32[64,128]{1,0:T(8,128)S(1)}) custom-call(s32[8,24]{1,0:T(8,128)S(1)} %copy-done, s32[8]{0:T(128)S(1)} %copy-done.2, bf16[64,128]{1,0:T(8,128)(2,1)S(1)} %get-tuple-element.11.q, bf16[16,128]{1,0:T(8,128)(2,1)S(1)} %bitcast.6, bf16[16,128]{1,0:T(8,128)(2,1)S(1)} %bitcast.7, ...), custom_call_target="tpu_custom_call" | custom-call | flops 100000000 | bytes 3145728 | tf_op jit(solution)/shard_map/resident/pallas_call | solution.py:363
  83.3 11.6 %all-to-all-done.2 = bf16[8,72,128]{2,1,0:T(8,128)(2,1)S(1)} async-done(((bf16[8,72,128]{2,1,0:T(8,128)(2,1)}), bf16[8,72,128]{2,1,0:T(8,128)(2,1)S(1)}, u32[]{:S(2)}, u32[]{:S(2)}) %all-to-all-start.2) | async-done | bytes 147488 | tf_op jit(solution)/shard_map/all_to_all | solution.py:325
  94.9 2.0 %finish.1 = bf16[8,16,320]{2,1,0:T(8,128)(2,1)S(1)} custom-call(bf16[576,128]{1,0:T(8,128)(2,1)S(1)} %bitcast.5, f32[64,128]{1,0:T(8,128)S(1)} %get-tuple-element.12.sums, f32[64,128]{1,0:T(8,128)S(1)} %get-tuple-element.13.top, f32[64,128]{1,0:T(8,128)S(1)} %get-tuple-element.14.total, bf16[512,2560]{1,0:T(8,128)(2,1)} %weight_hbm.1), custom_call_target="tpu_custom_call" | custom-call | tf_op jit(solution)/shard_map/finish/pallas_call | solution.py:374
  96.9 13.2 %all_to_all.21.shares = bf16[8,16,320]{2,1,0:T(8,128)(2,1)S(1)} all-to-all(bf16[8,16,320]{2,1,0:T(8,128)(2,1)S(1)} %finish.1), channel_id=1, replica_groups=mesh['zh'=4,'zm'=2,'zl'=2,'y'=4,'x'=4,'c'=2] {'x','c'}, dimensions={0} | all-to-all | bytes 163840 | tf_op jit(solution)/shard_map/all_to_all | solution.py:325
  110.1 0.6 total.1
  (3 shorter events, 0.0 us)
Async XLA Ops:
  0.0 0.7 copy-start.1
  2.6 39.6 %all-to-all-start = ((bf16[64,16,128]{2,1,0:T(8,128)(2,1)}), bf16[64,16,128]{2,1,0:T(8,128)(2,1)S(1)}, u32[]{:S(2)}, u32[]{:S(2)}) async-start(bf16[64,16,128]{2,1,0:T(8,128)(2,1)} %get-tuple-element.10), calls=%async_computation | async-start | bytes 524288 | tf_op jit(solution)/shard_map/all_to_all | solution.py:325
  74.3 7.5 %copy-start.3 = (bf16[8,2,2,1,128]{4,2,3,1,0:T(2,128)(2,1)S(1)}, bf16[8,2,2,1,128]{4,2,3,1,0:T(2,128)(2,1)}, u32[]{:S(2)}) copy-start(bf16[8,2,2,1,128]{4,2,3,1,0:T(2,128)(2,1)} %param.9) | copy-start | bytes 24580
  74.3 7.5 %copy-start = (s32[8,24]{1,0:T(8,128)S(1)}, s32[8,24]{1,0:T(8,128)}, u32[]{:S(2)}) copy-start(s32[8,24]{1,0:T(8,128)} %own.1) | copy-start | bytes 2308
  74.3 7.5 %copy-start.2 = (s32[8]{0:T(128)S(1)}, s32[8]{0:T(128)}, u32[]{:S(2)}) copy-start(s32[8]{0:T(128)} %length.1) | copy-start | bytes 100
  76.0 18.9 %all-to-all-start.2 = ((bf16[8,72,128]{2,1,0:T(8,128)(2,1)}), bf16[8,72,128]{2,1,0:T(8,128)(2,1)S(1)}, u32[]{:S(2)}, u32[]{:S(2)}) async-start(bf16[8,72,128]{2,1,0:T(8,128)(2,1)} %bitcast.1), calls=%async_computation.2 | async-start | bytes 294912 | tf_op jit(solution)/shard_map/all_to_all | solution.py:325

commit v9 on v8

--- a/solution.py
+++ b/solution.py
@@ -60,8 +60,10 @@
     return lax.dot_general(a, b, dims, preferred_element_type=F32)
 
 
-def request_kernel(prefix_hbm, own_hbm, fork_hbm, length_hbm, query, req, q, prefix, own, fork, length, sems):
-    pairs = ((prefix_hbm, prefix), (own_hbm, own), (fork_hbm, fork), (length_hbm, length))
+def request_kernel(
+    prefix_hbm, own_hbm, fork_hbm, length_hbm, query_hbm, req, prefix, own, fork, length, query, sems
+):
+    pairs = ((prefix_hbm, prefix), (own_hbm, own), (fork_hbm, fork), (length_hbm, length), (query_hbm, query))
     copies = [pltpu.make_async_copy(a, b, sems.at[n]) for n, (a, b) in enumerate(pairs)]
     for copy in copies:
         copy.start()
@@ -100,13 +102,12 @@
         parts = [table if k == s else jnp.zeros((16, HD), BF16) for k in range(HD // 16)]
         out = out + dot(chosen, jnp.concatenate(parts, 0), NT)
     for b in range(B):
-        rows = jnp.concatenate([query[b, t].astype(F32) for t in range(STEPS)], 0)
-        for m in range(MEMBERS):
-            d = b * MEMBERS + m
-            req[d] = jnp.concatenate([rows, jnp.broadcast_to(out[d : d + 1], (8, HD))], 0).astype(BF16)
-    for b in range(0, B, 2):
-        rows = [query[n, t].astype(F32) for n in (b, b + 1) for t in range(STEPS)]
-        q[pl.ds(b * QROWS, 2 * QROWS), :] = jnp.concatenate(rows, 0).astype(BF16)
+        for n in range(QROWS // 2):
+            rows = query[b, n]
+            for m in range(MEMBERS):
+                req[b * MEMBERS + m, n] = rows
+    for d in range(POOL):
+        req[d, QROWS // 2] = jnp.broadcast_to(out[d : d + 1], (2, HD)).astype(BF16)
 
 
 def prefetch_kernel(source, out, sems):
@@ -125,12 +126,14 @@
     row = iota((MEMBERS, HD), 0)
     tails = []
     for c in range(SOURCES):
-        tiles = [req[c * MEMBERS + n].astype(F32) for n in range(MEMBERS)]
-        asked = tiles[0][8:16]
-        for n in range(1, MEMBERS):
-            asked = jnp.where(row == n, tiles[n][8:16], asked)
+        asked = jnp.zeros((MEMBERS, HD), F32)
+        rows = []
+        for n in range(MEMBERS):
+            block = req[c * MEMBERS + n].astype(F32)
+            rows += [block[k] for k in range(QROWS // 2)]
+            asked = jnp.where(row == n, block[QROWS // 2, 0:1], asked)
         wanted[pl.ds(c * MEMBERS, MEMBERS), :] = asked.astype(I32)
-        tails.append([tile[0:8] for tile in tiles] + [asked, jnp.zeros((16 - MEMBERS, HD), F32)])
+        tails.append(rows + [asked, jnp.zeros((16 - MEMBERS, HD), F32)])
     copy = pltpu.make_async_copy(wanted, places, place_sem)
     copy.start()
     for c in range(SOURCES):
@@ -328,19 +331,21 @@
 def shards(query, new_kv, kv_store, prefix_pages, fork_of, own_pages, lengths, o_weight):
     shape = jax.ShapeDtypeStruct
     store = kv_store.reshape(P_DEV, 2, PAGE, HD)
-    request, q = call(
+    pairs = query.reshape(B, QROWS // 2, 2, HD)
+    request = call(
         request_kernel,
-        [shape((POOL, 16, HD), BF16), shape((ROWS, HD), BF16)],
-        [HBM] * 4 + [VMEM],
+        shape((POOL, QROWS // 2 + 1, 2, HD), BF16),
+        [HBM] * 5,
         "request",
         [
             pltpu.SMEM(prefix_pages.shape, I32),
             pltpu.SMEM(own_pages.shape, I32),
             pltpu.SMEM(fork_of.shape, I32),
             pltpu.SMEM(lengths.shape, I32),
-            pltpu.SemaphoreType.DMA((4,)),
+            pltpu.VMEM(pairs.shape, BF16),
+            pltpu.SemaphoreType.DMA((5,)),
         ],
-    )(hbm(prefix_pages), hbm(own_pages), hbm(fork_of), hbm(lengths), query)
+    )(hbm(prefix_pages), hbm(own_pages), hbm(fork_of), hbm(lengths), hbm(pairs))
     request = swap(request, NEAR + FAR)
     store = prefetch(store, "store_ahead")
     pages = call(
@@ -358,6 +363,7 @@
         out_specs=HBM,
     )(request, vmem(store))
     pages = swap(pages, NEAR)
+    q = query.reshape(ROWS, HD)
     fresh_k = new_kv[:, :, 0, 0].reshape(B * STEPS, HD)
     fresh_v = new_kv[:, :, 1, 0].reshape(B * STEPS, HD)
     local = call(

time: 111 us -> 106 us (0.955)
  waiting for transfers between devices: 30.3 us -> 27.3 us
    all_to_all x2, waiting for transfers between devices: 30.3 us -> 27.3 us  [swap(): return lax.all_to_all(x, axes, split_axis=0, concat_axis=0, tiled=True)]
where the time goes in v9:
time: 106 us
  blocking collectives  41.6 us (39%)
  waiting for transfers between devices  27.3 us (26%)
  starting transfers between devices  25.2 us (24%)
  Pallas kernels  11.8 us (11%)
    all_to_all x2, blocking collectives, swap(): return lax.all_to_all(x, axes, split_axis=0, concat_axis=0, tiled=True)  41.6 us
    all_to_all x2, waiting for transfers between devices, swap(): return lax.all_to_all(x, axes, split_axis=0, concat_axis=0, tiled=True)  27.3 us
    all_to_all x2, starting transfers between devices, swap(): return lax.all_to_all(x, axes, split_axis=0, concat_axis=0, tiled=True)  25.2 us
    pallas_call x1, Pallas kernels, shards(): call(gather_kernel, pltpu.HBM((SOURCES, CHUNK, HD), BF16), [VMEM, VMEM],...  2.6 us
  transfers between devices with their start and end apart: 2, of which 2 were waited for; matrix products, arithmetic and copies ran while one was open for 0% of the time, Pallas kernels for 3%

profile of v9, /device:TPU:1, one launch (start us, length us, event | category | flops | bytes accessed | tf_op | source)
XLA Modules:
  0.0 106.0 jit_solution(1238329970283531799)
XLA Ops:
  0.0 1.9 %request.1 = bf16[64,5,2,128]{3,2,1,0:T(2,128)(2,1)} custom-call(s32[4,8]{1,0:T(4,128)} %prefix_hbm.1, s32[8,24]{1,0:T(8,128)} %own.1, s32[8]{0:T(128)} %fork_hbm.1, s32[8]{0:T(128)} %length.1, bf16[8,4,2,128]{3,2,1,0:T(2,128)(2,1)} %bitcast.8), custom_call_target="tpu_custom_call" | custom-call | tf_op jit(solution)/shard_map/request/pallas_call | solution.py:335
  1.9 19.3 %all-to-all-start = ((bf16[64,5,2,128]{3,2,1,0:T(2,128)(2,1)}), bf16[64,5,2,128]{3,2,1,0:T(2,128)(2,1)S(1)}, u32[]{:S(2)}, u32[]{:S(2)}) async-start(bf16[64,5,2,128]{3,2,1,0:T(2,128)(2,1)} %request.1), calls=%async_computation | async-start | bytes 327680 | tf_op jit(solution)/shard_map/all_to_all | solution.py:328
  21.2 1.6 %store_ahead.1.store = bf16[256,2,16,128]{3,2,1,0:T(8,128)(2,1)S(1)} custom-call(bf16[256,2,16,128]{3,2,1,0:T(8,128)(2,1)} %bitcast.12), custom_call_target="tpu_custom_call" | custom-call | tf_op jit(solution)/shard_map/store_ahead/pallas_call | solution.py:317
  22.8 15.4 %all-to-all-done.req = bf16[64,5,2,128]{3,2,1,0:T(2,128)(2,1)S(1)} async-done(((bf16[64,5,2,128]{3,2,1,0:T(2,128)(2,1)}), bf16[64,5,2,128]{3,2,1,0:T(2,128)(2,1)S(1)}, u32[]{:S(2)}, u32[]{:S(2)}) %all-to-all-start) | async-done | bytes 163872 | tf_op jit(solution)/shard_map/all_to_all | solution.py:328
  38.2 2.6 %gather_pages.1 = bf16[8,1104,128]{2,1,0:T(8,128)(2,1)} custom-call(bf16[64,5,2,128]{3,2,1,0:T(2,128)(2,1)S(1)} %all-to-all-done.req, bf16[256,2,16,128]{3,2,1,0:T(8,128)(2,1)S(1)} %store_ahead.1.store), custom_call_target="tpu_custom_call" | custom-call | tf_op jit(solution)/shard_map/gather_pages/pallas_call | solution.py:351
  40.8 28.7 %all_to_all.20.pages = bf16[8,1104,128]{2,1,0:T(8,128)(2,1)S(1)} all-to-all(bf16[8,1104,128]{2,1,0:T(8,128)(2,1)} %gather_pages.1), channel_id=1, replica_groups=mesh['zh'=4,'zm'=2,'zl'=2,'y'=4,'x'=4,'c'=2] {'zl','y'}, dimensions={0} | all-to-all | bytes 4521984 | tf_op jit(solution)/shard_map/all_to_all | solution.py:328
  69.5 0.0 copy-start.3
  69.5 0.0 copy-start
  69.5 0.0 copy-start.1
  69.5 0.0 copy-start.2
  69.5 1.7 %partials.1 = bf16[576,128]{1,0:T(8,128)(2,1)} custom-call(bf16[8,1104,128]{2,1,0:T(8,128)(2,1)S(1)} %all_to_all.20.pages), custom_call_target="tpu_custom_call" | custom-call | tf_op jit(solution)/shard_map/partials/pallas_call | solution.py:377
  71.2 5.9 %all-to-all-start.2 = ((bf16[8,72,128]{2,1,0:T(8,128)(2,1)}), bf16[8,72,128]{2,1,0:T(8,128)(2,1)S(1)}, u32[]{:S(2)}, u32[]{:S(2)}) async-start(bf16[8,72,128]{2,1,0:T(8,128)(2,1)} %bitcast.2), calls=%async_computation.2 | async-start | bytes 294912 | tf_op jit(solution)/shard_map/all_to_all | solution.py:328
  77.1 0.0 copy-done.3
  77.2 0.0 copy-done
  77.2 0.0 copy-done.1
  77.2 0.0 copy-done.2
  77.2 1.5 %resident.1 = (f32[64,128]{1,0:T(8,128)S(1)}, f32[64,128]{1,0:T(8,128)S(1)}, f32[64,128]{1,0:T(8,128)S(1)}) custom-call(s32[8,24]{1,0:T(8,128)S(1)} %copy-done.1, s32[8]{0:T(128)S(1)} %copy-done.2, bf16[64,128]{1,0:T(8,128)(2,1)S(1)} %bitcast.9, bf16[16,128]{1,0:T(8,128)(2,1)S(1)} %bitcast.11, bf16[16,128]{1,0:T(8,128)(2,1)S(1)} %bitcast.10, ...), custom_call_target="tpu_custom_call" | custom-call | flops 100000000 | bytes 3145728 | tf_op jit(solution)/shard_map/resident/pallas_call | solution.py:369
  78.7 11.9 %all-to-all-done.2 = bf16[8,72,128]{2,1,0:T(8,128)(2,1)S(1)} async-done(((bf16[8,72,128]{2,1,0:T(8,128)(2,1)}), bf16[8,72,128]{2,1,0:T(8,128)(2,1)S(1)}, u32[]{:S(2)}, u32[]{:S(2)}) %all-to-all-start.2) | async-done | bytes 147488 | tf_op jit(solution)/shard_map/all_to_all | solution.py:328
  90.5 2.0 %finish.1 = bf16[8,16,320]{2,1,0:T(8,128)(2,1)S(1)} custom-call(bf16[576,128]{1,0:T(8,128)(2,1)S(1)} %bitcast.7, f32[64,128]{1,0:T(8,128)S(1)} %get-tuple-element.8.sums, f32[64,128]{1,0:T(8,128)S(1)} %get-tuple-element.9.top, f32[64,128]{1,0:T(8,128)S(1)} %get-tuple-element.10.total, bf16[512,2560]{1,0:T(8,128)(2,1)} %weight_hbm.1), custom_call_target="tpu_custom_call" | custom-call | tf_op jit(solution)/shard_map/finish/pallas_call | solution.py:380
  92.5 12.9 %all_to_all.21.shares = bf16[8,16,320]{2,1,0:T(8,128)(2,1)S(1)} all-to-all(bf16[8,16,320]{2,1,0:T(8,128)(2,1)S(1)} %finish.1), channel_id=1, replica_groups=mesh['zh'=4,'zm'=2,'zl'=2,'y'=4,'x'=4,'c'=2] {'x','c'}, dimensions={0} | all-to-all | bytes 163840 | tf_op jit(solution)/shard_map/all_to_all | solution.py:328
  105.4 0.6 total.1
  (3 shorter events, 0.0 us)
Async XLA Ops:
  1.9 36.3 %all-to-all-start = ((bf16[64,5,2,128]{3,2,1,0:T(2,128)(2,1)}), bf16[64,5,2,128]{3,2,1,0:T(2,128)(2,1)S(1)}, u32[]{:S(2)}, u32[]{:S(2)}) async-start(bf16[64,5,2,128]{3,2,1,0:T(2,128)(2,1)} %request.1), calls=%async_computation | async-start | bytes 327680 | tf_op jit(solution)/shard_map/all_to_all | solution.py:328
  69.5 7.6 %copy-start.3 = (bf16[8,2,2,1,128]{4,2,3,1,0:T(2,128)(2,1)S(1)}, bf16[8,2,2,1,128]{4,2,3,1,0:T(2,128)(2,1)}, u32[]{:S(2)}) copy-start(bf16[8,2,2,1,128]{4,2,3,1,0:T(2,128)(2,1)} %param.9) | copy-start | bytes 24580
  69.5 7.6 %copy-start = (bf16[8,2,4,128]{3,2,1,0:T(4,128)(2,1)S(1)}, bf16[8,2,4,128]{3,2,1,0:T(4,128)(2,1)}, u32[]{:S(2)}) copy-start(bf16[8,2,4,128]{3,2,1,0:T(4,128)(2,1)} %param.8) | copy-start | bytes 49156
  69.5 7.6 %copy-start.1 = (s32[8,24]{1,0:T(8,128)S(1)}, s32[8,24]{1,0:T(8,128)}, u32[]{:S(2)}) copy-start(s32[8,24]{1,0:T(8,128)} %own.1) | copy-start | bytes 2308
  69.5 7.7 %copy-start.2 = (s32[8]{0:T(128)S(1)}, s32[8]{0:T(128)}, u32[]{:S(2)}) copy-start(s32[8]{0:T(128)} %length.1) | copy-start | bytes 100
  71.2 19.3 %all-to-all-start.2 = ((bf16[8,72,128]{2,1,0:T(8,128)(2,1)}), bf16[8,72,128]{2,1,0:T(8,128)(2,1)S(1)}, u32[]{:S(2)}, u32[]{:S(2)}) async-start(bf16[8,72,128]{2,1,0:T(8,128)(2,1)} %bitcast.2), calls=%async_computation.2 | async-start | bytes 294912 | tf_op jit(solution)/shard_map/all_to_all | solution.py:328

commit v10 on v9

--- a/solution.py
+++ b/solution.py
@@ -69,6 +69,11 @@
         copy.start()
     for copy in copies:
         copy.wait()
+    for b in range(B):
+        for n in range(QROWS // 2):
+            rows = query[b, n]
+            for m in range(MEMBERS):
+                req[b * MEMBERS + m, n] = rows
     lane = iota((8, HD), 1)
     row = iota((8, HD), 0)
     ids = jnp.zeros((8, HD), I32)
@@ -101,11 +106,6 @@
         chosen = jnp.where(member & (rank == float(s)), 1.0, 0.0).astype(BF16)
         parts = [table if k == s else jnp.zeros((16, HD), BF16) for k in range(HD // 16)]
         out = out + dot(chosen, jnp.concatenate(parts, 0), NT)
-    for b in range(B):
-        for n in range(QROWS // 2):
-            rows = query[b, n]
-            for m in range(MEMBERS):
-                req[b * MEMBERS + m, n] = rows
     for d in range(POOL):
         req[d, QROWS // 2] = jnp.broadcast_to(out[d : d + 1], (2, HD)).astype(BF16)
 
@@ -122,7 +122,7 @@
         copy.wait()
 
 
-def gather_kernel(req, store, out, stage, wanted, places, place_sem, sems):
+def gather_kernel(req, store, out, wanted, places, place_sem):
     row = iota((MEMBERS, HD), 0)
     tails = []
     for c in range(SOURCES):
@@ -137,21 +137,15 @@
     copy = pltpu.make_async_copy(wanted, places, place_sem)
     copy.start()
     for c in range(SOURCES):
-        stage[c, pl.ds(2 * PAGE_ROWS, TAIL), :] = jnp.concatenate(tails[c], 0).astype(BF16)
+        out[c, pl.ds(2 * PAGE_ROWS, TAIL), :] = jnp.concatenate(tails[c], 0).astype(BF16)
     copy.wait()
-    copies = []
     for c in range(SOURCES):
         for n in range(MEMBERS):
             for s in range(SLOTS):
                 at = places[c * MEMBERS + n, 16 * s + 8]
                 start = n * KEYS + s * PAGE
-                stage[c, pl.ds(start, PAGE), :] = store[at, 0]
-                stage[c, pl.ds(PAGE_ROWS + start, PAGE), :] = store[at, 1]
-        copy = pltpu.make_async_copy(stage.at[c], out.at[c], sems.at[c])
-        copy.start()
-        copies.append(copy)
-    for copy in copies:
-        copy.wait()
+                out[c, pl.ds(start, PAGE), :] = store[at, 0]
+                out[c, pl.ds(PAGE_ROWS + start, PAGE), :] = store[at, 1]
 
 
 def local_kernel(own, length, q, fresh_k, fresh_v, store, sums, top, total, keys, values):
@@ -350,17 +344,11 @@
     store = prefetch(store, "store_ahead")
     pages = call(
         gather_kernel,
-        pltpu.HBM((SOURCES, CHUNK, HD), BF16),
+        pltpu.VMEM((SOURCES, CHUNK, HD), BF16),
         [VMEM, VMEM],
         "gather_pages",
-        [
-            pltpu.VMEM((SOURCES, CHUNK, HD), BF16),
-            pltpu.VMEM((POOL, HD), I32),
-            pltpu.SMEM((POOL, HD), I32),
-            pltpu.SemaphoreType.DMA(()),
-            pltpu.SemaphoreType.DMA((SOURCES,)),
-        ],
-        out_specs=HBM,
+        [pltpu.VMEM((POOL, HD), I32), pltpu.SMEM((POOL, HD), I32), pltpu.SemaphoreType.DMA(())],
+        out_specs=VMEM,
     )(request, vmem(store))
     pages = swap(pages, NEAR)
     q = query.reshape(ROWS, HD)

time: 106 us -> 105 us (level)
  starting transfers between devices: 25.2 us -> 22.9 us
  blocking collectives: 41.6 us -> 43.1 us
  Pallas kernels: 11.8 us -> 10.6 us
    all_to_all x2, starting transfers between devices: 25.2 us -> 22.9 us  [swap(): return lax.all_to_all(x, axes, split_axis=0, concat_axis=0, tiled=True)]
    all_to_all x2, blocking collectives: 41.6 us -> 43.1 us  [swap(): return lax.all_to_all(x, axes, split_axis=0, concat_axis=0, tiled=True)]
    pallas_call x1, Pallas kernels: 2.6 us -> 1.34 us  [shards(): call(gather_kernel, pltpu.VMEM((SOURCES, CHUNK, HD), BF16), [VMEM, VMEM],...]
where the time goes in v10:
time: 105 us; the launch traced here: 104 us
  blocking collectives  43.1 us (41%)
  waiting for transfers between devices  27.5 us (26%)
  starting transfers between devices  22.9 us (22%)
  Pallas kernels  10.6 us (10%)
    all_to_all x2, blocking collectives, swap(): return lax.all_to_all(x, axes, split_axis=0, concat_axis=0, tiled=True)  43.1 us
    all_to_all x2, waiting for transfers between devices, swap(): return lax.all_to_all(x, axes, split_axis=0, concat_axis=0, tiled=True)  27.5 us
    all_to_all x2, starting transfers between devices, swap(): return lax.all_to_all(x, axes, split_axis=0, concat_axis=0, tiled=True)  22.9 us
  transfers between devices with their start and end apart: 2, of which 2 were waited for; matrix products, arithmetic and copies ran while one was open for 0% of the time, Pallas kernels for 3%

profile of v10, /device:TPU:1, one launch (start us, length us, event | category | flops | bytes accessed | tf_op | source)
XLA Modules:
  0.0 104.2 jit_solution(6529327928886289740)
XLA Ops:
  0.0 1.9 %request.1 = bf16[64,5,2,128]{3,2,1,0:T(2,128)(2,1)} custom-call(s32[4,8]{1,0:T(4,128)} %prefix_hbm.1, s32[8,24]{1,0:T(8,128)} %own.1, s32[8]{0:T(128)} %fork_hbm.1, s32[8]{0:T(128)} %length.1, bf16[8,4,2,128]{3,2,1,0:T(2,128)(2,1)} %bitcast.8), custom_call_target="tpu_custom_call" | custom-call | tf_op jit(solution)/shard_map/request/pallas_call | solution.py:329
  1.9 19.3 %all-to-all-start = ((bf16[64,5,2,128]{3,2,1,0:T(2,128)(2,1)}), bf16[64,5,2,128]{3,2,1,0:T(2,128)(2,1)S(1)}, u32[]{:S(2)}, u32[]{:S(2)}) async-start(bf16[64,5,2,128]{3,2,1,0:T(2,128)(2,1)} %request.1), calls=%async_computation | async-start | bytes 327680 | tf_op jit(solution)/shard_map/all_to_all | solution.py:322
  21.2 1.6 %store_ahead.1.store = bf16[256,2,16,128]{3,2,1,0:T(8,128)(2,1)S(1)} custom-call(bf16[256,2,16,128]{3,2,1,0:T(8,128)(2,1)} %bitcast.12), custom_call_target="tpu_custom_call" | custom-call | tf_op jit(solution)/shard_map/store_ahead/pallas_call | solution.py:311
  22.8 15.4 %all-to-all-done.req = bf16[64,5,2,128]{3,2,1,0:T(2,128)(2,1)S(1)} async-done(((bf16[64,5,2,128]{3,2,1,0:T(2,128)(2,1)}), bf16[64,5,2,128]{3,2,1,0:T(2,128)(2,1)S(1)}, u32[]{:S(2)}, u32[]{:S(2)}) %all-to-all-start) | async-done | bytes 163872 | tf_op jit(solution)/shard_map/all_to_all | solution.py:322
  38.2 1.3 %gather_pages.1 = bf16[8,1104,128]{2,1,0:T(8,128)(2,1)S(1)} custom-call(bf16[64,5,2,128]{3,2,1,0:T(2,128)(2,1)S(1)} %all-to-all-done.req, bf16[256,2,16,128]{3,2,1,0:T(8,128)(2,1)S(1)} %store_ahead.1.store), custom_call_target="tpu_custom_call" | custom-call | tf_op jit(solution)/shard_map/gather_pages/pallas_call | solution.py:345
  39.6 29.6 %all_to_all.20.pages = bf16[8,1104,128]{2,1,0:T(8,128)(2,1)S(1)} all-to-all(bf16[8,1104,128]{2,1,0:T(8,128)(2,1)S(1)} %gather_pages.1), channel_id=1, replica_groups=mesh['zh'=4,'zm'=2,'zl'=2,'y'=4,'x'=4,'c'=2] {'zl','y'}, dimensions={0} | all-to-all | bytes 4521984 | tf_op jit(solution)/shard_map/all_to_all | solution.py:322
  69.2 0.0 copy-start.3
  69.2 0.0 copy-start
  69.2 0.0 copy-start.1
  69.2 0.0 copy-start.2
  69.2 1.7 %partials.1 = bf16[576,128]{1,0:T(8,128)(2,1)} custom-call(bf16[8,1104,128]{2,1,0:T(8,128)(2,1)S(1)} %all_to_all.20.pages), custom_call_target="tpu_custom_call" | custom-call | tf_op jit(solution)/shard_map/partials/pallas_call | solution.py:365
  70.9 3.6 %all-to-all-start.2 = ((bf16[8,72,128]{2,1,0:T(8,128)(2,1)}), bf16[8,72,128]{2,1,0:T(8,128)(2,1)S(1)}, u32[]{:S(2)}, u32[]{:S(2)}) async-start(bf16[8,72,128]{2,1,0:T(8,128)(2,1)} %bitcast.2), calls=%async_computation.2 | async-start | bytes 294912 | tf_op jit(solution)/shard_map/all_to_all | solution.py:322
  74.5 0.0 copy-done.3
  74.6 0.0 copy-done
  74.6 0.0 copy-done.1
  74.6 0.0 copy-done.2
  74.6 1.5 %resident.1 = (f32[64,128]{1,0:T(8,128)S(1)}, f32[64,128]{1,0:T(8,128)S(1)}, f32[64,128]{1,0:T(8,128)S(1)}) custom-call(s32[8,24]{1,0:T(8,128)S(1)} %copy-done.1, s32[8]{0:T(128)S(1)} %copy-done.2, bf16[64,128]{1,0:T(8,128)(2,1)S(1)} %bitcast.9, bf16[16,128]{1,0:T(8,128)(2,1)S(1)} %bitcast.11, bf16[16,128]{1,0:T(8,128)(2,1)S(1)} %bitcast.10, ...), custom_call_target="tpu_custom_call" | custom-call | flops 100000000 | bytes 3145728 | tf_op jit(solution)/shard_map/resident/pallas_call | solution.py:357
  76.1 12.1 %all-to-all-done.2 = bf16[8,72,128]{2,1,0:T(8,128)(2,1)S(1)} async-done(((bf16[8,72,128]{2,1,0:T(8,128)(2,1)}), bf16[8,72,128]{2,1,0:T(8,128)(2,1)S(1)}, u32[]{:S(2)}, u32[]{:S(2)}) %all-to-all-start.2) | async-done | bytes 147488 | tf_op jit(solution)/shard_map/all_to_all | solution.py:322
  88.2 2.0 %finish.1 = bf16[8,16,320]{2,1,0:T(8,128)(2,1)S(1)} custom-call(bf16[576,128]{1,0:T(8,128)(2,1)S(1)} %bitcast.7, f32[64,128]{1,0:T(8,128)S(1)} %get-tuple-element.8.sums, f32[64,128]{1,0:T(8,128)S(1)} %get-tuple-element.9.top, f32[64,128]{1,0:T(8,128)S(1)} %get-tuple-element.10.total, bf16[512,2560]{1,0:T(8,128)(2,1)} %weight_hbm.1), custom_call_target="tpu_custom_call" | custom-call | tf_op jit(solution)/shard_map/finish/pallas_call | solution.py:368
  90.2 13.4 %all_to_all.21.shares = bf16[8,16,320]{2,1,0:T(8,128)(2,1)S(1)} all-to-all(bf16[8,16,320]{2,1,0:T(8,128)(2,1)S(1)} %finish.1), channel_id=1, replica_groups=mesh['zh'=4,'zm'=2,'zl'=2,'y'=4,'x'=4,'c'=2] {'x','c'}, dimensions={0} | all-to-all | bytes 163840 | tf_op jit(solution)/shard_map/all_to_all | solution.py:322
  103.6 0.6 total.1
  (3 shorter events, 0.0 us)
Async XLA Ops:
  1.9 36.3 %all-to-all-start = ((bf16[64,5,2,128]{3,2,1,0:T(2,128)(2,1)}), bf16[64,5,2,128]{3,2,1,0:T(2,128)(2,1)S(1)}, u32[]{:S(2)}, u32[]{:S(2)}) async-start(bf16[64,5,2,128]{3,2,1,0:T(2,128)(2,1)} %request.1), calls=%async_computation | async-start | bytes 327680 | tf_op jit(solution)/shard_map/all_to_all | solution.py:322
  69.2 5.3 %copy-start.3 = (bf16[8,2,2,1,128]{4,2,3,1,0:T(2,128)(2,1)S(1)}, bf16[8,2,2,1,128]{4,2,3,1,0:T(2,128)(2,1)}, u32[]{:S(2)}) copy-start(bf16[8,2,2,1,128]{4,2,3,1,0:T(2,128)(2,1)} %param.9) | copy-start | bytes 24580
  69.2 5.4 %copy-start = (bf16[8,2,4,128]{3,2,1,0:T(4,128)(2,1)S(1)}, bf16[8,2,4,128]{3,2,1,0:T(4,128)(2,1)}, u32[]{:S(2)}) copy-start(bf16[8,2,4,128]{3,2,1,0:T(4,128)(2,1)} %param.8) | copy-start | bytes 49156
  69.2 5.4 %copy-start.1 = (s32[8,24]{1,0:T(8,128)S(1)}, s32[8,24]{1,0:T(8,128)}, u32[]{:S(2)}) copy-start(s32[8,24]{1,0:T(8,128)} %own.1) | copy-start | bytes 2308
  69.2 5.4 %copy-start.2 = (s32[8]{0:T(128)S(1)}, s32[8]{0:T(128)}, u32[]{:S(2)}) copy-start(s32[8]{0:T(128)} %length.1) | copy-start | bytes 100
  70.9 17.3 %all-to-all-start.2 = ((bf16[8,72,128]{2,1,0:T(8,128)(2,1)}), bf16[8,72,128]{2,1,0:T(8,128)(2,1)S(1)}, u32[]{:S(2)}, u32[]{:S(2)}) async-start(bf16[8,72,128]{2,1,0:T(8,128)(2,1)} %bitcast.2), calls=%async_computation.2 | async-start | bytes 294912 | tf_op jit(solution)/shard_map/all_to_all | solution.py:322

commit v11 on v10

--- a/solution.py
+++ b/solution.py
@@ -31,7 +31,7 @@
 PARTS = 1
 POOL_AXES = ("zh", "zm", "zl", "y")
 NEAR = ("zl", "y")
-FAR = ("zh", "zm")
+FAR = ("zm", "zh")
 SOURCES = ZL * YN
 MEMBERS = ZH * ZM
 POOL = ZN * YN
@@ -97,7 +97,8 @@
     table = jnp.concatenate([tokens, place], 0).astype(F32).astype(BF16)
     holder = ids // P_DEV
     plane, row_y = holder // YN, holder % YN
-    holder = ((plane % ZL) * YN + row_y) * MEMBERS + plane // ZL
+    member = plane // ZL % ZM * ZH + plane // (ZL * ZM)
+    holder = ((plane % ZL) * YN + row_y) * MEMBERS + member
     member = jnp.broadcast_to(holder[0:1], (POOL, HD)) == iota((POOL, HD), 0)
     earlier = (iota((HD, HD), 0) < iota((HD, HD), 1)).astype(F32).astype(BF16)
     rank = dot(member.astype(F32).astype(BF16), earlier)

time: 105 us -> 103 us (0.981)
  waiting for transfers between devices: 27.5 us -> 22.9 us
  blocking collectives: 43.1 us -> 45 us
  starting transfers between devices: 22.9 us -> 24.4 us
    all_to_all x2, waiting for transfers between devices: 27.5 us -> 22.9 us  [swap(): return lax.all_to_all(x, axes, split_axis=0, concat_axis=0, tiled=True)]
    all_to_all x2, blocking collectives: 43.1 us -> 45 us  [swap(): return lax.all_to_all(x, axes, split_axis=0, concat_axis=0, tiled=True)]
    all_to_all x2, starting transfers between devices: 22.9 us -> 24.4 us  [swap(): return lax.all_to_all(x, axes, split_axis=0, concat_axis=0, tiled=True)]
where the time goes in v11:
time: 103 us
  blocking collectives  45 us (44%)
  starting transfers between devices  24.4 us (24%)
  waiting for transfers between devices  22.9 us (22%)
  Pallas kernels  10.6 us (10%)
    all_to_all x2, blocking collectives, swap(): return lax.all_to_all(x, axes, split_axis=0, concat_axis=0, tiled=True)  45 us
    all_to_all x2, starting transfers between devices, swap(): return lax.all_to_all(x, axes, split_axis=0, concat_axis=0, tiled=True)  24.4 us
    all_to_all x2, waiting for transfers between devices, swap(): return lax.all_to_all(x, axes, split_axis=0, concat_axis=0, tiled=True)  22.9 us
  transfers between devices with their start and end apart: 2, of which 2 were waited for; matrix products, arithmetic and copies ran while one was open for 0% of the time, Pallas kernels for 3%

profile of v11, /device:TPU:1, one launch (start us, length us, event | category | flops | bytes accessed | tf_op | source)
XLA Modules:
  0.0 103.1 jit_solution(13478900405884675620)
XLA Ops:
  0.0 1.9 %request.1 = bf16[64,5,2,128]{3,2,1,0:T(2,128)(2,1)} custom-call(s32[4,8]{1,0:T(4,128)} %prefix_hbm.1, s32[8,24]{1,0:T(8,128)} %own.1, s32[8]{0:T(128)} %fork_hbm.1, s32[8]{0:T(128)} %length.1, bf16[8,4,2,128]{3,2,1,0:T(2,128)(2,1)} %bitcast.8), custom_call_target="tpu_custom_call" | custom-call | tf_op jit(solution)/shard_map/request/pallas_call | solution.py:330
  1.9 19.3 %all-to-all-start = ((bf16[64,5,2,128]{3,2,1,0:T(2,128)(2,1)}), bf16[64,5,2,128]{3,2,1,0:T(2,128)(2,1)S(1)}, u32[]{:S(2)}, u32[]{:S(2)}) async-start(bf16[64,5,2,128]{3,2,1,0:T(2,128)(2,1)} %request.1), calls=%async_computation | async-start | bytes 327680 | tf_op jit(solution)/shard_map/all_to_all | solution.py:323
  21.2 1.6 %store_ahead.1.store = bf16[256,2,16,128]{3,2,1,0:T(8,128)(2,1)S(1)} custom-call(bf16[256,2,16,128]{3,2,1,0:T(8,128)(2,1)} %bitcast.12), custom_call_target="tpu_custom_call" | custom-call | tf_op jit(solution)/shard_map/store_ahead/pallas_call | solution.py:312
  22.8 12.9 %all-to-all-done.req = bf16[64,5,2,128]{3,2,1,0:T(2,128)(2,1)S(1)} async-done(((bf16[64,5,2,128]{3,2,1,0:T(2,128)(2,1)}), bf16[64,5,2,128]{3,2,1,0:T(2,128)(2,1)S(1)}, u32[]{:S(2)}, u32[]{:S(2)}) %all-to-all-start) | async-done | bytes 163872 | tf_op jit(solution)/shard_map/all_to_all | solution.py:323
  35.7 1.3 %gather_pages.1 = bf16[8,1104,128]{2,1,0:T(8,128)(2,1)S(1)} custom-call(bf16[64,5,2,128]{3,2,1,0:T(2,128)(2,1)S(1)} %all-to-all-done.req, bf16[256,2,16,128]{3,2,1,0:T(8,128)(2,1)S(1)} %store_ahead.1.store), custom_call_target="tpu_custom_call" | custom-call | tf_op jit(solution)/shard_map/gather_pages/pallas_call | solution.py:346
  37.0 30.7 %all_to_all.20.pages = bf16[8,1104,128]{2,1,0:T(8,128)(2,1)S(1)} all-to-all(bf16[8,1104,128]{2,1,0:T(8,128)(2,1)S(1)} %gather_pages.1), channel_id=1, replica_groups=mesh['zh'=4,'zm'=2,'zl'=2,'y'=4,'x'=4,'c'=2] {'zl','y'}, dimensions={0} | all-to-all | bytes 4521984 | tf_op jit(solution)/shard_map/all_to_all | solution.py:323
  67.7 0.0 copy-start.3
  67.7 0.0 copy-start
  67.7 0.0 copy-start.1
  67.7 0.0 copy-start.2
  67.7 1.7 %partials.1 = bf16[576,128]{1,0:T(8,128)(2,1)} custom-call(bf16[8,1104,128]{2,1,0:T(8,128)(2,1)S(1)} %all_to_all.20.pages), custom_call_target="tpu_custom_call" | custom-call | tf_op jit(solution)/shard_map/partials/pallas_call | solution.py:366
  69.4 5.1 %all-to-all-start.2 = ((bf16[8,72,128]{2,1,0:T(8,128)(2,1)}), bf16[8,72,128]{2,1,0:T(8,128)(2,1)S(1)}, u32[]{:S(2)}, u32[]{:S(2)}) async-start(bf16[8,72,128]{2,1,0:T(8,128)(2,1)} %bitcast.2), calls=%async_computation.2 | async-start | bytes 294912 | tf_op jit(solution)/shard_map/all_to_all | solution.py:323
  74.5 0.0 copy-done.3
  74.6 0.0 copy-done
  74.6 0.0 copy-done.1
  74.6 0.0 copy-done.2
  74.6 1.5 %resident.1 = (f32[64,128]{1,0:T(8,128)S(1)}, f32[64,128]{1,0:T(8,128)S(1)}, f32[64,128]{1,0:T(8,128)S(1)}) custom-call(s32[8,24]{1,0:T(8,128)S(1)} %copy-done.1, s32[8]{0:T(128)S(1)} %copy-done.2, bf16[64,128]{1,0:T(8,128)(2,1)S(1)} %bitcast.9, bf16[16,128]{1,0:T(8,128)(2,1)S(1)} %bitcast.11, bf16[16,128]{1,0:T(8,128)(2,1)S(1)} %bitcast.10, ...), custom_call_target="tpu_custom_call" | custom-call | flops 100000000 | bytes 3145728 | tf_op jit(solution)/shard_map/resident/pallas_call | solution.py:358
  76.1 10.0 %all-to-all-done.2 = bf16[8,72,128]{2,1,0:T(8,128)(2,1)S(1)} async-done(((bf16[8,72,128]{2,1,0:T(8,128)(2,1)}), bf16[8,72,128]{2,1,0:T(8,128)(2,1)S(1)}, u32[]{:S(2)}, u32[]{:S(2)}) %all-to-all-start.2) | async-done | bytes 147488 | tf_op jit(solution)/shard_map/all_to_all | solution.py:323
  86.1 2.0 %finish.1 = bf16[8,16,320]{2,1,0:T(8,128)(2,1)S(1)} custom-call(bf16[576,128]{1,0:T(8,128)(2,1)S(1)} %bitcast.7, f32[64,128]{1,0:T(8,128)S(1)} %get-tuple-element.8.sums, f32[64,128]{1,0:T(8,128)S(1)} %get-tuple-element.9.top, f32[64,128]{1,0:T(8,128)S(1)} %get-tuple-element.10.total, bf16[512,2560]{1,0:T(8,128)(2,1)} %weight_hbm.1), custom_call_target="tpu_custom_call" | custom-call | tf_op jit(solution)/shard_map/finish/pallas_call | solution.py:369
  88.1 14.4 %all_to_all.21.shares = bf16[8,16,320]{2,1,0:T(8,128)(2,1)S(1)} all-to-all(bf16[8,16,320]{2,1,0:T(8,128)(2,1)S(1)} %finish.1), channel_id=1, replica_groups=mesh['zh'=4,'zm'=2,'zl'=2,'y'=4,'x'=4,'c'=2] {'x','c'}, dimensions={0} | all-to-all | bytes 163840 | tf_op jit(solution)/shard_map/all_to_all | solution.py:323
  102.4 0.6 total.1
  (3 shorter events, 0.0 us)
Async XLA Ops:
  1.9 33.8 %all-to-all-start = ((bf16[64,5,2,128]{3,2,1,0:T(2,128)(2,1)}), bf16[64,5,2,128]{3,2,1,0:T(2,128)(2,1)S(1)}, u32[]{:S(2)}, u32[]{:S(2)}) async-start(bf16[64,5,2,128]{3,2,1,0:T(2,128)(2,1)} %request.1), calls=%async_computation | async-start | bytes 327680 | tf_op jit(solution)/shard_map/all_to_all | solution.py:323
  67.7 6.8 %copy-start.3 = (bf16[8,2,2,1,128]{4,2,3,1,0:T(2,128)(2,1)S(1)}, bf16[8,2,2,1,128]{4,2,3,1,0:T(2,128)(2,1)}, u32[]{:S(2)}) copy-start(bf16[8,2,2,1,128]{4,2,3,1,0:T(2,128)(2,1)} %param.9) | copy-start | bytes 24580
  67.7 6.9 %copy-start = (bf16[8,2,4,128]{3,2,1,0:T(4,128)(2,1)S(1)}, bf16[8,2,4,128]{3,2,1,0:T(4,128)(2,1)}, u32[]{:S(2)}) copy-start(bf16[8,2,4,128]{3,2,1,0:T(4,128)(2,1)} %param.8) | copy-start | bytes 49156
  67.7 6.9 %copy-start.1 = (s32[8,24]{1,0:T(8,128)S(1)}, s32[8,24]{1,0:T(8,128)}, u32[]{:S(2)}) copy-start(s32[8,24]{1,0:T(8,128)} %own.1) | copy-start | bytes 2308
  67.7 6.9 %copy-start.2 = (s32[8]{0:T(128)S(1)}, s32[8]{0:T(128)}, u32[]{:S(2)}) copy-start(s32[8]{0:T(128)} %length.1) | copy-start | bytes 100
  69.4 16.7 %all-to-all-start.2 = ((bf16[8,72,128]{2,1,0:T(8,128)(2,1)}), bf16[8,72,128]{2,1,0:T(8,128)(2,1)S(1)}, u32[]{:S(2)}, u32[]{:S(2)}) async-start(bf16[8,72,128]{2,1,0:T(8,128)(2,1)} %bitcast.2), calls=%async_computation.2 | async-start | bytes 294912 | tf_op jit(solution)/shard_map/all_to_all | solution.py:323

commit v12 on v11

--- a/solution.py
+++ b/solution.py
@@ -343,15 +343,6 @@
     )(hbm(prefix_pages), hbm(own_pages), hbm(fork_of), hbm(lengths), hbm(pairs))
     request = swap(request, NEAR + FAR)
     store = prefetch(store, "store_ahead")
-    pages = call(
-        gather_kernel,
-        pltpu.VMEM((SOURCES, CHUNK, HD), BF16),
-        [VMEM, VMEM],
-        "gather_pages",
-        [pltpu.VMEM((POOL, HD), I32), pltpu.SMEM((POOL, HD), I32), pltpu.SemaphoreType.DMA(())],
-        out_specs=VMEM,
-    )(request, vmem(store))
-    pages = swap(pages, NEAR)
     q = query.reshape(ROWS, HD)
     fresh_k = new_kv[:, :, 0, 0].reshape(B * STEPS, HD)
     fresh_v = new_kv[:, :, 1, 0].reshape(B * STEPS, HD)
@@ -363,6 +354,16 @@
         [pltpu.VMEM(((B - MIG) * NOWN * PAGE, HD), BF16)] * 2,
         pl.CostEstimate(flops=10**8, bytes_accessed=3 * 2**20, transcendentals=10**5),
     )(own_pages, lengths, q, fresh_k, fresh_v, store)
+    request, *local = lax.optimization_barrier((request, *local))
+    pages = call(
+        gather_kernel,
+        pltpu.VMEM((SOURCES, CHUNK, HD), BF16),
+        [VMEM, VMEM],
+        "gather_pages",
+        [pltpu.VMEM((POOL, HD), I32), pltpu.SMEM((POOL, HD), I32), pltpu.SemaphoreType.DMA(())],
+        out_specs=VMEM,
+    )(request, vmem(store))
+    pages = swap(pages, NEAR)
     parts = call(partial_kernel, shape((MEMBERS * RES, HD), BF16), [VMEM], "partials")(vmem(pages))
     parts = swap(parts.reshape(MEMBERS, RES, HD), FAR).reshape(MEMBERS * RES, HD)
     width = o_weight.shape[1] // TPN

time: 103 us -> 103 us (level)
  blocking collectives: 45 us -> 61.5 us
  waiting for transfers between devices: 22.9 us -> 10.6 us
  starting transfers between devices: 24.4 us -> 19.4 us
    all_to_all x2 -> x3, blocking collectives: 45 us -> 61.5 us  [swap(): return lax.all_to_all(x, axes, split_axis=0, concat_axis=0, tiled=True)]
    all_to_all x2 -> x1, waiting for transfers between devices: 22.9 us -> 10.6 us  [swap(): return lax.all_to_all(x, axes, split_axis=0, concat_axis=0, tiled=True)]
    all_to_all x2 -> x1, starting transfers between devices: 24.4 us -> 19.4 us  [swap(): return lax.all_to_all(x, axes, split_axis=0, concat_axis=0, tiled=True)]
  transfers between devices with their start and end apart: 2 -> 1, of which waited for: 2 -> 1; matrix products, arithmetic and copies ran while one was open for 0% -> 1% of each run, Pallas kernels for 3% -> 3%
where the time goes in v12:
time: 103 us; the launch traced here: 102 us
  blocking collectives  61.5 us (60%)
  starting transfers between devices  19.4 us (19%)
  waiting for transfers between devices  10.6 us (10%)
  Pallas kernels  9.91 us (10%)
    all_to_all x3, blocking collectives, swap(): return lax.all_to_all(x, axes, split_axis=0, concat_axis=0, tiled=True)  61.5 us
    all_to_all x1, starting transfers between devices, swap(): return lax.all_to_all(x, axes, split_axis=0, concat_axis=0, tiled=True)  19.4 us
    all_to_all x1, waiting for transfers between devices, swap(): return lax.all_to_all(x, axes, split_axis=0, concat_axis=0, tiled=True)  10.6 us
  transfers between devices with their start and end apart: 1, of which 1 were waited for; matrix products, arithmetic and copies ran while one was open for 1% of the time, Pallas kernels for 3%

profile of v12, /device:TPU:1, one launch (start us, length us, event | category | flops | bytes accessed | tf_op | source)
XLA Modules:
  0.0 102.4 jit_solution(7819044223211286609)
XLA Ops:
  0.0 1.9 %request.1 = bf16[64,5,2,128]{3,2,1,0:T(2,128)(2,1)} custom-call(s32[4,8]{1,0:T(4,128)} %prefix_hbm.1, s32[8,24]{1,0:T(8,128)} %own.1, s32[8]{0:T(128)} %fork_hbm.1, s32[8]{0:T(128)} %length.1, bf16[8,4,2,128]{3,2,1,0:T(2,128)(2,1)} %bitcast.9), custom_call_target="tpu_custom_call" | custom-call | tf_op jit(solution)/shard_map/request/pallas_call | solution.py:330
  1.9 0.0 copy-start
  1.9 0.0 copy-start.1
  1.9 0.0 copy-start.2
  1.9 19.4 %all-to-all-start = ((bf16[64,5,2,128]{3,2,1,0:T(2,128)(2,1)}), bf16[64,5,2,128]{3,2,1,0:T(2,128)(2,1)S(1)}, u32[]{:S(2)}, u32[]{:S(2)}) async-start(bf16[64,5,2,128]{3,2,1,0:T(2,128)(2,1)} %request.1), calls=%async_computation | async-start | bytes 327680 | tf_op jit(solution)/shard_map/all_to_all | solution.py:323
  21.4 0.8 fusion
  22.2 1.6 %store_ahead.1.store = bf16[256,2,16,128]{3,2,1,0:T(8,128)(2,1)S(1)} custom-call(bf16[256,2,16,128]{3,2,1,0:T(8,128)(2,1)} %bitcast.13), custom_call_target="tpu_custom_call" | custom-call | tf_op jit(solution)/shard_map/store_ahead/pallas_call | solution.py:312
  23.8 0.0 copy-done
  23.8 0.0 copy-done.1
  23.8 0.0 copy-done.2
  23.8 1.5 %resident.1 = (f32[64,128]{1,0:T(8,128)S(1)}, f32[64,128]{1,0:T(8,128)S(1)}, f32[64,128]{1,0:T(8,128)S(1)}) custom-call(s32[8,24]{1,0:T(8,128)S(1)} %copy-done.1, s32[8]{0:T(128)S(1)} %copy-done.2, bf16[64,128]{1,0:T(8,128)(2,1)S(1)} %bitcast.10, bf16[16,128]{1,0:T(8,128)(2,1)S(1)} %bitcast.12, bf16[16,128]{1,0:T(8,128)(2,1)S(1)} %bitcast.11, ...), custom_call_target="tpu_custom_call" | custom-call | flops 100000000 | bytes 3145728 | tf_op jit(solution)/shard_map/resident/pallas_call | solution.py:349
  25.3 10.6 %all-to-all-done.req = bf16[64,5,2,128]{3,2,1,0:T(2,128)(2,1)S(1)} async-done(((bf16[64,5,2,128]{3,2,1,0:T(2,128)(2,1)}), bf16[64,5,2,128]{3,2,1,0:T(2,128)(2,1)S(1)}, u32[]{:S(2)}, u32[]{:S(2)}) %all-to-all-start) | async-done | bytes 163872 | tf_op jit(solution)/shard_map/all_to_all | solution.py:323
  35.9 1.3 %gather_pages.1 = bf16[8,1104,128]{2,1,0:T(8,128)(2,1)S(1)} custom-call(bf16[64,5,2,128]{3,2,1,0:T(2,128)(2,1)S(1)} %all-to-all-done.req, bf16[256,2,16,128]{3,2,1,0:T(8,128)(2,1)S(1)} %store_ahead.1.store), custom_call_target="tpu_custom_call" | custom-call | tf_op jit(solution)/shard_map/gather_pages/pallas_call | solution.py:358
  37.2 30.7 %all_to_all.20.pages = bf16[8,1104,128]{2,1,0:T(8,128)(2,1)S(1)} all-to-all(bf16[8,1104,128]{2,1,0:T(8,128)(2,1)S(1)} %gather_pages.1), channel_id=1, replica_groups=mesh['zh'=4,'zm'=2,'zl'=2,'y'=4,'x'=4,'c'=2] {'zl','y'}, dimensions={0} | all-to-all | bytes 4521984 | tf_op jit(solution)/shard_map/all_to_all | solution.py:323
  67.9 1.0 %partials.1 = bf16[576,128]{1,0:T(8,128)(2,1)S(1)} custom-call(bf16[8,1104,128]{2,1,0:T(8,128)(2,1)S(1)} %all_to_all.20.pages), custom_call_target="tpu_custom_call" | custom-call | tf_op jit(solution)/shard_map/partials/pallas_call | solution.py:367
  68.9 16.5 %all_to_all.21 = bf16[8,72,128]{2,1,0:T(8,128)(2,1)S(1)} all-to-all(bf16[8,72,128]{2,1,0:T(8,128)(2,1)S(1)} %bitcast.8), channel_id=1, replica_groups=mesh['zh'=4,'zm'=2,'zl'=2,'y'=4,'x'=4,'c'=2] {'zm','zh'}, dimensions={0} | all-to-all | bytes 294912 | tf_op jit(solution)/shard_map/all_to_all | solution.py:323
  85.4 2.0 %finish.1 = bf16[8,16,320]{2,1,0:T(8,128)(2,1)S(1)} custom-call(bf16[576,128]{1,0:T(8,128)(2,1)S(1)} %bitcast.7, f32[64,128]{1,0:T(8,128)S(1)} %get-tuple-element.16.sums, f32[64,128]{1,0:T(8,128)S(1)} %get-tuple-element.17.top, f32[64,128]{1,0:T(8,128)S(1)} %get-tuple-element.18.total, bf16[512,2560]{1,0:T(8,128)(2,1)} %weight_hbm.1), custom_call_target="tpu_custom_call" | custom-call | tf_op jit(solution)/shard_map/finish/pallas_call | solution.py:370
  87.4 14.4 %all_to_all.22.shares = bf16[8,16,320]{2,1,0:T(8,128)(2,1)S(1)} all-to-all(bf16[8,16,320]{2,1,0:T(8,128)(2,1)S(1)} %finish.1), channel_id=1, replica_groups=mesh['zh'=4,'zm'=2,'zl'=2,'y'=4,'x'=4,'c'=2] {'x','c'}, dimensions={0} | all-to-all | bytes 163840 | tf_op jit(solution)/shard_map/all_to_all | solution.py:323
  101.8 0.6 total.1
  (2 shorter events, 0.0 us)
Async XLA Ops:
  1.9 21.9 %copy-start = (bf16[8,2,4,128]{3,2,1,0:T(4,128)(2,1)S(1)}, bf16[8,2,4,128]{3,2,1,0:T(4,128)(2,1)}, u32[]{:S(2)}) copy-start(bf16[8,2,4,128]{3,2,1,0:T(4,128)(2,1)} %param.8) | copy-start | bytes 49156
  1.9 21.9 %copy-start.1 = (s32[8,24]{1,0:T(8,128)S(1)}, s32[8,24]{1,0:T(8,128)}, u32[]{:S(2)}) copy-start(s32[8,24]{1,0:T(8,128)} %own.1) | copy-start | bytes 2308
  1.9 21.9 %copy-start.2 = (s32[8]{0:T(128)S(1)}, s32[8]{0:T(128)}, u32[]{:S(2)}) copy-start(s32[8]{0:T(128)} %length.1) | copy-start | bytes 100
  1.9 33.9 %all-to-all-start = ((bf16[64,5,2,128]{3,2,1,0:T(2,128)(2,1)}), bf16[64,5,2,128]{3,2,1,0:T(2,128)(2,1)S(1)}, u32[]{:S(2)}, u32[]{:S(2)}) async-start(bf16[64,5,2,128]{3,2,1,0:T(2,128)(2,1)} %request.1), calls=%async_computation | async-start | bytes 327680 | tf_op jit(solution)/shard_map/all_to_all | solution.py:323

commit v13 on v12

--- a/solution.py
+++ b/solution.py
@@ -73,7 +73,7 @@
         for n in range(QROWS // 2):
             rows = query[b, n]
             for m in range(MEMBERS):
-                req[b * MEMBERS + m, n] = rows
+                req[m * SOURCES + b, n] = rows
     lane = iota((8, HD), 1)
     row = iota((8, HD), 0)
     ids = jnp.zeros((8, HD), I32)
@@ -98,7 +98,7 @@
     holder = ids // P_DEV
     plane, row_y = holder // YN, holder % YN
     member = plane // ZL % ZM * ZH + plane // (ZL * ZM)
-    holder = ((plane % ZL) * YN + row_y) * MEMBERS + member
+    holder = member * SOURCES + (plane % ZL) * YN + row_y
     member = jnp.broadcast_to(holder[0:1], (POOL, HD)) == iota((POOL, HD), 0)
     earlier = (iota((HD, HD), 0) < iota((HD, HD), 1)).astype(F32).astype(BF16)
     rank = dot(member.astype(F32).astype(BF16), earlier)
@@ -130,7 +130,7 @@
         asked = jnp.zeros((MEMBERS, HD), F32)
         rows = []
         for n in range(MEMBERS):
-            block = req[c * MEMBERS + n].astype(F32)
+            block = req[n * SOURCES + c].astype(F32)
             rows += [block[k] for k in range(QROWS // 2)]
             asked = jnp.where(row == n, block[QROWS // 2, 0:1], asked)
         wanted[pl.ds(c * MEMBERS, MEMBERS), :] = asked.astype(I32)
@@ -341,7 +341,7 @@
             pltpu.SemaphoreType.DMA((5,)),
         ],
     )(hbm(prefix_pages), hbm(own_pages), hbm(fork_of), hbm(lengths), hbm(pairs))
-    request = swap(request, NEAR + FAR)
+    request = swap(request, FAR + NEAR)
     store = prefetch(store, "store_ahead")
     q = query.reshape(ROWS, HD)
     fresh_k = new_kv[:, :, 0, 0].reshape(B * STEPS, HD)

time: 103 us -> 103 us (level)
  waiting for transfers between devices: 10.6 us -> 9.18 us
  blocking collectives: 61.5 us -> 62.7 us
    all_to_all x1, waiting for transfers between devices: 10.6 us -> 9.18 us  [swap(): return lax.all_to_all(x, axes, split_axis=0, concat_axis=0, tiled=True)]
    all_to_all x3, blocking collectives: 61.5 us -> 62.7 us  [swap(): return lax.all_to_all(x, axes, split_axis=0, concat_axis=0, tiled=True)]
where the time goes in v13:
time: 103 us; the launch traced here: 102 us
  blocking collectives  62.7 us (61%)
  starting transfers between devices  19.4 us (19%)
  Pallas kernels  9.91 us (10%)
  waiting for transfers between devices  9.18 us (9%)
    all_to_all x3, blocking collectives, swap(): return lax.all_to_all(x, axes, split_axis=0, concat_axis=0, tiled=True)  62.7 us
    all_to_all x1, starting transfers between devices, swap(): return lax.all_to_all(x, axes, split_axis=0, concat_axis=0, tiled=True)  19.4 us
    all_to_all x1, waiting for transfers between devices, swap(): return lax.all_to_all(x, axes, split_axis=0, concat_axis=0, tiled=True)  9.18 us
  transfers between devices with their start and end apart: 1, of which 1 were waited for; matrix products, arithmetic and copies ran while one was open for 1% of the time, Pallas kernels for 3%

profile of v13, /device:TPU:1, one launch (start us, length us, event | category | flops | bytes accessed | tf_op | source)
XLA Modules:
  0.0 102.2 jit_solution(7728681225443514545)
XLA Ops:
  0.0 1.9 %request.1 = bf16[64,5,2,128]{3,2,1,0:T(2,128)(2,1)} custom-call(s32[4,8]{1,0:T(4,128)} %prefix_hbm.1, s32[8,24]{1,0:T(8,128)} %own.1, s32[8]{0:T(128)} %fork_hbm.1, s32[8]{0:T(128)} %length.1, bf16[8,4,2,128]{3,2,1,0:T(2,128)(2,1)} %bitcast.9), custom_call_target="tpu_custom_call" | custom-call | tf_op jit(solution)/shard_map/request/pallas_call | solution.py:330
  1.9 0.0 copy-start
  1.9 0.0 copy-start.1
  1.9 0.0 copy-start.2
  1.9 19.4 %all-to-all-start = ((bf16[64,5,2,128]{3,2,1,0:T(2,128)(2,1)}), bf16[64,5,2,128]{3,2,1,0:T(2,128)(2,1)S(1)}, u32[]{:S(2)}, u32[]{:S(2)}) async-start(bf16[64,5,2,128]{3,2,1,0:T(2,128)(2,1)} %request.1), calls=%async_computation | async-start | bytes 327680 | tf_op jit(solution)/shard_map/all_to_all | solution.py:323
  21.4 0.8 fusion
  22.2 1.6 %store_ahead.1.store = bf16[256,2,16,128]{3,2,1,0:T(8,128)(2,1)S(1)} custom-call(bf16[256,2,16,128]{3,2,1,0:T(8,128)(2,1)} %bitcast.13), custom_call_target="tpu_custom_call" | custom-call | tf_op jit(solution)/shard_map/store_ahead/pallas_call | solution.py:312
  23.8 0.0 copy-done
  23.8 0.0 copy-done.1
  23.8 0.0 copy-done.2
  23.8 1.5 %resident.1 = (f32[64,128]{1,0:T(8,128)S(1)}, f32[64,128]{1,0:T(8,128)S(1)}, f32[64,128]{1,0:T(8,128)S(1)}) custom-call(s32[8,24]{1,0:T(8,128)S(1)} %copy-done.1, s32[8]{0:T(128)S(1)} %copy-done.2, bf16[64,128]{1,0:T(8,128)(2,1)S(1)} %bitcast.10, bf16[16,128]{1,0:T(8,128)(2,1)S(1)} %bitcast.12, bf16[16,128]{1,0:T(8,128)(2,1)S(1)} %bitcast.11, ...), custom_call_target="tpu_custom_call" | custom-call | flops 100000000 | bytes 3145728 | tf_op jit(solution)/shard_map/resident/pallas_call | solution.py:349
  25.3 9.2 %all-to-all-done.req = bf16[64,5,2,128]{3,2,1,0:T(2,128)(2,1)S(1)} async-done(((bf16[64,5,2,128]{3,2,1,0:T(2,128)(2,1)}), bf16[64,5,2,128]{3,2,1,0:T(2,128)(2,1)S(1)}, u32[]{:S(2)}, u32[]{:S(2)}) %all-to-all-start) | async-done | bytes 163872 | tf_op jit(solution)/shard_map/all_to_all | solution.py:323
  34.5 1.3 %gather_pages.1 = bf16[8,1104,128]{2,1,0:T(8,128)(2,1)S(1)} custom-call(bf16[64,5,2,128]{3,2,1,0:T(2,128)(2,1)S(1)} %all-to-all-done.req, bf16[256,2,16,128]{3,2,1,0:T(8,128)(2,1)S(1)} %store_ahead.1.store), custom_call_target="tpu_custom_call" | custom-call | tf_op jit(solution)/shard_map/gather_pages/pallas_call | solution.py:358
  35.8 30.6 %all_to_all.20.pages = bf16[8,1104,128]{2,1,0:T(8,128)(2,1)S(1)} all-to-all(bf16[8,1104,128]{2,1,0:T(8,128)(2,1)S(1)} %gather_pages.1), channel_id=1, replica_groups=mesh['zh'=4,'zm'=2,'zl'=2,'y'=4,'x'=4,'c'=2] {'zl','y'}, dimensions={0} | all-to-all | bytes 4521984 | tf_op jit(solution)/shard_map/all_to_all | solution.py:323
  66.4 1.0 %partials.1 = bf16[576,128]{1,0:T(8,128)(2,1)S(1)} custom-call(bf16[8,1104,128]{2,1,0:T(8,128)(2,1)S(1)} %all_to_all.20.pages), custom_call_target="tpu_custom_call" | custom-call | tf_op jit(solution)/shard_map/partials/pallas_call | solution.py:367
  67.4 18.1 %all_to_all.21 = bf16[8,72,128]{2,1,0:T(8,128)(2,1)S(1)} all-to-all(bf16[8,72,128]{2,1,0:T(8,128)(2,1)S(1)} %bitcast.8), channel_id=1, replica_groups=mesh['zh'=4,'zm'=2,'zl'=2,'y'=4,'x'=4,'c'=2] {'zm','zh'}, dimensions={0} | all-to-all | bytes 294912 | tf_op jit(solution)/shard_map/all_to_all | solution.py:323
  85.6 2.0 %finish.1 = bf16[8,16,320]{2,1,0:T(8,128)(2,1)S(1)} custom-call(bf16[576,128]{1,0:T(8,128)(2,1)S(1)} %bitcast.7, f32[64,128]{1,0:T(8,128)S(1)} %get-tuple-element.16.sums, f32[64,128]{1,0:T(8,128)S(1)} %get-tuple-element.17.top, f32[64,128]{1,0:T(8,128)S(1)} %get-tuple-element.18.total, bf16[512,2560]{1,0:T(8,128)(2,1)} %weight_hbm.1), custom_call_target="tpu_custom_call" | custom-call | tf_op jit(solution)/shard_map/finish/pallas_call | solution.py:370
  87.6 14.0 %all_to_all.22.shares = bf16[8,16,320]{2,1,0:T(8,128)(2,1)S(1)} all-to-all(bf16[8,16,320]{2,1,0:T(8,128)(2,1)S(1)} %finish.1), channel_id=1, replica_groups=mesh['zh'=4,'zm'=2,'zl'=2,'y'=4,'x'=4,'c'=2] {'x','c'}, dimensions={0} | all-to-all | bytes 163840 | tf_op jit(solution)/shard_map/all_to_all | solution.py:323
  101.5 0.6 total.1
  (2 shorter events, 0.0 us)
Async XLA Ops:
  1.9 21.9 %copy-start = (bf16[8,2,4,128]{3,2,1,0:T(4,128)(2,1)S(1)}, bf16[8,2,4,128]{3,2,1,0:T(4,128)(2,1)}, u32[]{:S(2)}) copy-start(bf16[8,2,4,128]{3,2,1,0:T(4,128)(2,1)} %param.8) | copy-start | bytes 49156
  1.9 21.9 %copy-start.1 = (s32[8,24]{1,0:T(8,128)S(1)}, s32[8,24]{1,0:T(8,128)}, u32[]{:S(2)}) copy-start(s32[8,24]{1,0:T(8,128)} %own.1) | copy-start | bytes 2308
  1.9 21.9 %copy-start.2 = (s32[8]{0:T(128)S(1)}, s32[8]{0:T(128)}, u32[]{:S(2)}) copy-start(s32[8]{0:T(128)} %length.1) | copy-start | bytes 100
  1.9 32.5 %all-to-all-start = ((bf16[64,5,2,128]{3,2,1,0:T(2,128)(2,1)}), bf16[64,5,2,128]{3,2,1,0:T(2,128)(2,1)S(1)}, u32[]{:S(2)}, u32[]{:S(2)}) async-start(bf16[64,5,2,128]{3,2,1,0:T(2,128)(2,1)} %request.1), calls=%async_computation | async-start | bytes 327680 | tf_op jit(solution)/shard_map/all_to_all | solution.py:323
